TPU v7x, 32 devices: a whole 2x2x4 slice. The times are simulated.
32 devices in a mesh: head: 4 (over x, core), blk: 8 (over z, y).
Axes of the slice: x: 2, y: 2, z: 4, core: 2. Of those that a mesh axis runs over, the one named last changes fastest.
Arguments:
- tokens: bfloat16 [2048, 4, 768], P('blk', 'head'), may hold values from -6 to 6
- attn_gain: bfloat16 [768], P(('head', 'blk')), may hold values from 0.5 to 1.5
- w_query: bfloat16 [768, 768], P(('head', 'blk')), may hold values from -0.109375 to 0.109375
- w_key: bfloat16 [768, 768], P(('head', 'blk')), may hold values from -0.109375 to 0.109375
- w_value: bfloat16 [768, 768], P(('head', 'blk')), may hold values from -0.21875 to 0.21875
- w_out: bfloat16 [768, 768], P(None, ('head', 'blk')), may hold values from -0.875 to 0.875
- bias_table: bfloat16 [384], P(('head', 'blk')), may hold values from -3 to 3
- moe_gain: bfloat16 [768], P(('head', 'blk')), may hold values from 0.5 to 1.5
- w_router: bfloat16 [768, 8], P(('head', 'blk')), may hold values from -0.15625 to 0.15625
- expert_in: bfloat16 [8, 768, 3072], P('blk', None, 'head'), may hold values from -0.21875 to 0.21875
- expert_out: bfloat16 [8, 3072, 768], P('blk', 'head'), may hold values from -0.875 to 0.875
- seq_lengths: int32 [4], replicated, may hold values from 1024 to 2048, as said below
- rel_buckets: int32 [2048], replicated, may hold values from 0 to 31, as said below
- routes: int32 [4, 2048, 1, 1], P('head', 'blk'), may hold values from 0 to 7; in each aligned block of 256 rows (0 to 255, 256 to 511, ..., all dimensions but the last counted through in order) at most 48 rows name the same one
- cotangent: bfloat16 [2048, 4, 768], P('blk', 'head'), may hold values from -6 to 6
Outputs:
- result: bfloat16 [2048, 4, 768], P('blk', 'head')
- grad_tokens: float32 [2048, 4, 768], P('blk', 'head')
- grad_attn_gain: float32 [768], P(('head', 'blk'))
- grad_query: float32 [768, 768], P(('head', 'blk'))
- grad_key: float32 [768, 768], P(('head', 'blk'))
- grad_value: float32 [768, 768], P(('head', 'blk'))
- grad_out: float32 [768, 768], P(None, ('head', 'blk'))
- grad_table: float32 [384], P(('head', 'blk'))
- grad_moe_gain: float32 [768], P(('head', 'blk'))
- grad_router: float32 [768, 8], P(('head', 'blk'))
- grad_expert_in: float32 [8, 768, 3072], P('blk', None, 'head')
- grad_expert_out: float32 [8, 3072, 768], P('blk', 'head')
Inputs may be any that keep to these rules, and one draw needn't show every extreme that they name: `seq_lengths`: one sequence, which one drawn from the seed, has exactly 2048 tokens. `rel_buckets`: entry j is the bucket of distance j: j itself for j below half of 32, never falling, and 31 at the last entry. `routes`: in each aligned block of 256 rows (the rows of one device, in the array's order) no expert is named more than 48 times; in some blocks one expert is named exactly 48 times.
All inputs are finite; a program needn't handle non-finite values.
Results may differ from a plain program's by a relative error of at most 0.02.
Values may be sent and summed in bfloat16 or wider, within the bound.
No kernel may reach another device: no remote copies, remote signals or barrier semaphores. Data moves between devices by JAX's collectives and lax.ppermute only.
A program may use at most 256 MiB of HBM per device.

v0:
```python
import functools
import math

import jax
import jax.numpy as jnp
from jax import lax
from jax.experimental import pallas as pl
from jax.experimental.pallas import tpu as pltpu
from jax.sharding import PartitionSpec as P

HEADS = 12
HEAD_DIM = 64
NUM_BUCKETS = 32
HEAD, BLK = "head", "blk"


norm_eps = 1e-06
masked_score = -1e30


def inverse_rms(values):
    return lax.rsqrt(jnp.mean(values * values, axis=-1, keepdims=True) + norm_eps)


def norm_backward(grad_normed, source, inv_scale, gain):
    weighted = grad_normed * gain
    inner_mean = jnp.mean(weighted * source, axis=-1, keepdims=True)
    grad_source = inv_scale * weighted - source * (inv_scale * inv_scale * inv_scale) * inner_mean
    grad_gain = jnp.sum(grad_normed * source * inv_scale, axis=0)
    return (grad_source, grad_gain)


def same_state(running):
    return running


def bucket_bounds(rel_buckets):
    bucket_count = NUM_BUCKETS
    labels = jnp.arange(bucket_count, dtype=jnp.int32)
    starts = jnp.sum((rel_buckets[:, None] < labels[None, :]).astype(jnp.int32), axis=0)
    ends = jnp.concatenate([starts[1:], jnp.full((1,), rel_buckets.shape[0] + 1, jnp.int32)])
    return (starts, ends)


def bias_terms(query_positions, key_positions, bounds, table32):
    starts, ends = bounds
    distance = jnp.maximum(query_positions[:, None] - key_positions[None, :], 0)[:, :, None]
    inside = (distance >= starts[None, None, :]) & (distance < ends[None, None, :])
    onehot = inside.astype(jnp.bfloat16)
    bias = jnp.einsum(
        "qkb,bh->hqk", onehot, table32.astype(jnp.bfloat16), preferred_element_type=jnp.float32
    )
    return (onehot, bias)


def block_scores(queries, keys, query_positions, key_positions, seq_lengths, bounds, table32):
    onehot, bias = bias_terms(query_positions, key_positions, bounds, table32)
    raw = jnp.einsum("qshd,kshd->hsqk", queries, keys, preferred_element_type=jnp.float32)
    causal = key_positions[None, :] <= query_positions[:, None]
    present = key_positions[None, :] < seq_lengths[:, None]
    valid = causal[None, :, :] & present[:, None, :]
    return (raw + bias[:, None, :, :], valid[None], onehot)


def attend_step(
    running, queries, keys, values, query_positions, key_positions, seq_lengths, bounds, table32
):
    row_top, row_total, weighted = running
    scores, valid, unused = block_scores(
        queries, keys, query_positions, key_positions, seq_lengths, bounds, table32
    )
    scores = jnp.where(valid, scores, masked_score)
    new_top = jnp.maximum(row_top, jnp.max(scores, axis=-1))
    weights = jnp.where(valid, jnp.exp(scores - new_top[..., None]), 0.0)
    decay = jnp.exp(row_top - new_top)
    row_total = row_total * decay + jnp.sum(weights, axis=-1)
    mixed = jnp.einsum(
        "hsqk,kshd->qshd", weights.astype(jnp.bfloat16), values, preferred_element_type=jnp.float32
    )
    weighted = weighted * jnp.transpose(decay, (2, 1, 0))[..., None] + mixed
    return (new_top, row_total, weighted)


def grad_step(
    queries,
    grad_heads,
    log_total,
    delta,
    query_positions,
    keys,
    values,
    key_positions,
    seq_lengths,
    bounds,
    table32,
):
    scores, valid, onehot = block_scores(
        queries, keys, query_positions, key_positions, seq_lengths, bounds, table32
    )
    probs = jnp.where(valid, jnp.exp(scores - jnp.transpose(log_total, (2, 1, 0))[..., None]), 0.0)
    grad_probs = jnp.einsum(
        "qshd,kshd->hsqk", grad_heads, values, preferred_element_type=jnp.float32
    )
    grad_scores = probs * (grad_probs - jnp.transpose(delta, (2, 1, 0))[..., None])
    grad_table = jnp.einsum(
        "hqk,qkb->bh",
        jnp.sum(grad_scores, axis=1),
        onehot.astype(jnp.float32),
        precision=lax.Precision.HIGHEST,
    )
    low_scores = grad_scores.astype(jnp.bfloat16)
    grad_queries = jnp.einsum(
        "hsqk,kshd->qshd", low_scores, keys, preferred_element_type=jnp.float32
    )
    grad_keys = jnp.einsum(
        "hsqk,qshd->kshd", low_scores, queries, preferred_element_type=jnp.float32
    )
    grad_values = jnp.einsum(
        "hsqk,qshd->kshd",
        probs.astype(jnp.bfloat16),
        grad_heads,
        preferred_element_type=jnp.float32,
    )
    return (grad_queries, grad_keys, grad_values, grad_table)


def on_device(
    tokens,
    attn_gain,
    w_query,
    w_key,
    w_value,
    w_out,
    bias_table,
    moe_gain,
    w_router,
    expert_in,
    expert_out,
    seq_lengths,
    rel_buckets,
    routes,
    cotangent,
):
    head_count = lax.axis_size(HEAD)
    blk_count = lax.axis_size(BLK)
    head_index = lax.axis_index(HEAD)
    blk_index = lax.axis_index(BLK)
    block_rows, group_seqs, width = tokens.shape
    seq_count = group_seqs * head_count
    tok_rows = block_rows * group_seqs
    local_heads = HEADS // head_count
    head_width = local_heads * HEAD_DIM
    group_rows = block_rows * max(1, blk_count // 8)
    longest = jnp.max(seq_lengths)
    query_first = blk_index * block_rows
    query_last = query_first + block_rows - 1
    query_positions = query_first + jnp.arange(block_rows, dtype=jnp.int32)
    bounds = bucket_bounds(rel_buckets)
    fetched = (
        lax.all_gather(w_query, (HEAD, BLK), axis=0, tiled=True),
        lax.all_gather(w_key, (HEAD, BLK), axis=0, tiled=True),
        lax.all_gather(w_value, (HEAD, BLK), axis=0, tiled=True),
        lax.all_gather(w_out, (HEAD, BLK), axis=1, tiled=True),
        lax.all_gather(attn_gain, (HEAD, BLK), axis=0, tiled=True),
        lax.all_gather(bias_table, (HEAD, BLK), axis=0, tiled=True),
        lax.all_gather(moe_gain, (HEAD, BLK), axis=0, tiled=True),
        lax.all_gather(w_router, (HEAD, BLK), axis=0, tiled=True),
    )
    full_query, full_key, full_value, full_out, gain_attn, table_flat, gain_moe, full_router = (
        fetched
    )
    inner_width = full_query.shape[1]
    table_all = table_flat.astype(jnp.float32).reshape(NUM_BUCKETS, HEADS)
    table32 = lax.dynamic_slice_in_dim(table_all, head_index * local_heads, local_heads, 1)
    gain_attn32 = gain_attn.astype(jnp.float32)
    gain_moe32 = gain_moe.astype(jnp.float32)

    def to_heads(values):
        parts = values.shape[1]
        shaped = values.reshape(block_rows, group_seqs, parts, head_count, head_width)
        moved = lax.all_to_all(shaped, HEAD, split_axis=3, concat_axis=1, tiled=True)
        return moved.reshape(block_rows, seq_count, parts, local_heads, HEAD_DIM)

    def to_tokens(values):
        parts = values.shape[2]
        shaped = values.reshape(block_rows, seq_count, parts, 1, head_width)
        moved = lax.all_to_all(shaped, HEAD, split_axis=1, concat_axis=3, tiled=True)
        return moved.reshape(tok_rows, parts, inner_width)

    source = tokens.astype(jnp.float32).reshape(tok_rows, width)
    inv_attn = inverse_rms(source)
    attn_in = (source * inv_attn * gain_attn32).astype(jnp.bfloat16)
    stacked_weights = jnp.stack((full_query, full_key, full_value))
    projected = jnp.einsum(
        "td,cde->tce", attn_in, stacked_weights, preferred_element_type=jnp.float32
    ).astype(jnp.bfloat16)
    heads_in = to_heads(projected)
    queries = heads_in[:, :, 0]
    keys = heads_in[:, :, 1]
    values = heads_in[:, :, 2]
    start_state = (
        jnp.full((local_heads, seq_count, block_rows), masked_score, jnp.float32),
        jnp.zeros((local_heads, seq_count, block_rows), jnp.float32),
        jnp.zeros((block_rows, seq_count, local_heads, HEAD_DIM), jnp.float32),
    )
    key_piece = lax.all_gather(keys, BLK, axis=0, tiled=True)
    value_piece = lax.all_gather(values, BLK, axis=0, tiled=True)
    piece_rows = key_piece.shape[0]
    part_rows = math.gcd(piece_rows, group_rows)

    def forward_one_part(step_index, inner_state):
        offset = step_index * part_rows
        key_part = lax.dynamic_slice_in_dim(key_piece, offset, part_rows, 0)
        value_part = lax.dynamic_slice_in_dim(value_piece, offset, part_rows, 0)
        key_positions = offset + jnp.arange(part_rows, dtype=jnp.int32)

        def attend_now(current):
            return attend_step(
                current,
                queries,
                key_part,
                value_part,
                query_positions,
                key_positions,
                seq_lengths,
                bounds,
                table32,
            )

        skipped = (offset > query_last) | (offset >= longest)
        return lax.cond(skipped, same_state, attend_now, inner_state)

    row_top, row_total, weighted = lax.fori_loop(
        0, piece_rows // part_rows, forward_one_part, start_state
    )
    attn_heads = (weighted / jnp.transpose(row_total, (2, 1, 0))[..., None]).astype(jnp.bfloat16)
    log_total = jnp.transpose(row_top + jnp.log(row_total), (2, 1, 0))
    attn_tok = to_tokens(attn_heads[:, :, None])[:, 0]
    branch = jnp.dot(attn_tok, full_out, preferred_element_type=jnp.float32)
    hidden = source + branch
    expert_count = full_router.shape[1]
    local_experts = expert_in.shape[0]
    capacity = max(2, 3 * tok_rows // (2 * expert_count))
    inv_moe = inverse_rms(hidden)
    moe_in = (hidden * inv_moe * gain_moe32).astype(jnp.bfloat16)
    logits = jnp.dot(moe_in, full_router, preferred_element_type=jnp.float32)
    router_probs = jax.nn.softmax(logits, axis=-1)
    route_flat = routes.reshape(tok_rows)
    chosen = route_flat[:, None] == jnp.arange(expert_count, dtype=jnp.int32)[None, :]
    gate = jnp.sum(jnp.where(chosen, router_probs, 0.0), axis=-1)
    filled = jnp.cumsum(chosen.astype(jnp.int32), axis=0)
    slot = jnp.sum(jnp.where(chosen, filled - 1, 0), axis=-1)
    target = route_flat * capacity + slot
    dispatch = (
        target[:, None] == jnp.arange(expert_count * capacity, dtype=jnp.int32)[None, :]
    ).astype(jnp.bfloat16)

    def to_buffer(token_rows):
        packed = jnp.einsum(
            "tj,td->jd", dispatch, token_rows, preferred_element_type=jnp.float32
        ).astype(jnp.bfloat16)
        return packed.reshape(blk_count, local_experts, capacity, width)

    def from_buffer(buffer):
        return jnp.dot(
            dispatch,
            buffer.reshape(expert_count * capacity, width),
            preferred_element_type=jnp.float32,
        )

    def to_experts(buffer):
        return lax.all_to_all(buffer, BLK, split_axis=0, concat_axis=0, tiled=True)

    def all_rows(buffer):
        return lax.all_gather(buffer, HEAD, axis=0, tiled=True)

    def summed_rows(partial_terms):
        return lax.psum_scatter(
            partial_terms.astype(jnp.bfloat16), HEAD, scatter_dimension=0, tiled=True
        ).astype(jnp.float32)

    def to_owners(buffer):
        return lax.all_to_all(buffer, BLK, split_axis=0, concat_axis=0, tiled=True)

    expert_rows_in = all_rows(to_experts(to_buffer(moe_in)))
    expert_pre = jnp.einsum(
        "necd,edf->necf", expert_rows_in, expert_in, preferred_element_type=jnp.float32
    )
    expert_act, gelu_pull = jax.vjp(jax.nn.gelu, expert_pre)
    expert_low = expert_act.astype(jnp.bfloat16)
    expert_terms = jnp.einsum(
        "necf,efd->necd", expert_low, expert_out, preferred_element_type=jnp.float32
    )
    expert_tok = from_buffer(to_owners(summed_rows(expert_terms).astype(jnp.bfloat16)))
    result = hidden + gate[:, None] * expert_tok
    grad_result = cotangent.astype(jnp.float32).reshape(tok_rows, width)
    grad_expert_tok = (gate[:, None] * grad_result).astype(jnp.bfloat16)
    grad_gate = jnp.sum(grad_result * expert_tok, axis=-1)
    grad_logits = (
        router_probs * (jnp.where(chosen, grad_gate[:, None], 0.0) - (gate * grad_gate)[:, None])
    ).astype(jnp.bfloat16)
    grad_router = jnp.einsum("td,te->de", moe_in, grad_logits, preferred_element_type=jnp.float32)
    grad_rows = all_rows(to_experts(to_buffer(grad_expert_tok)))
    grad_act = jnp.einsum(
        "necd,efd->necf", grad_rows, expert_out, preferred_element_type=jnp.float32
    )
    grad_pre = gelu_pull(grad_act)[0].astype(jnp.bfloat16)
    grad_expert_out = jnp.einsum(
        "necf,necd->efd", expert_low, grad_rows, preferred_element_type=jnp.float32
    )
    grad_expert_in = jnp.einsum(
        "necd,necf->edf", expert_rows_in, grad_pre, preferred_element_type=jnp.float32
    )
    grad_back = jnp.einsum(
        "necf,edf->necd", grad_pre, expert_in, preferred_element_type=jnp.float32
    )
    grad_moe_in = from_buffer(to_owners(summed_rows(grad_back).astype(jnp.bfloat16)))
    grad_moe_in = grad_moe_in + jnp.einsum(
        "te,de->td", grad_logits, full_router, preferred_element_type=jnp.float32
    )
    grad_norm_moe, grad_gain_moe = norm_backward(grad_moe_in, hidden, inv_moe, gain_moe32)
    grad_hidden = grad_result + grad_norm_moe
    grad_branch = grad_hidden.astype(jnp.bfloat16)
    grad_out_w = jnp.einsum("te,td->ed", attn_tok, grad_branch, preferred_element_type=jnp.float32)
    grad_attn_tok = jnp.einsum(
        "td,ed->te", grad_branch, full_out, preferred_element_type=jnp.float32
    ).astype(jnp.bfloat16)
    grad_heads = to_heads(grad_attn_tok[:, None])[:, :, 0]
    delta = jnp.sum(grad_heads.astype(jnp.float32) * attn_heads.astype(jnp.float32), axis=-1)
    all_keys = lax.all_gather(keys, BLK, axis=0, tiled=True)
    all_values = lax.all_gather(values, BLK, axis=0, tiled=True)
    total_rows = all_keys.shape[0]
    step_rows = math.gcd(total_rows, group_rows)
    zero_heads = jnp.zeros((block_rows, seq_count, local_heads, HEAD_DIM), jnp.float32)
    zero_table = jnp.zeros(table32.shape, jnp.float32)

    def query_side(step_index, running):
        offset = step_index * step_rows
        key_block = lax.dynamic_slice_in_dim(all_keys, offset, step_rows, 0)
        value_block = lax.dynamic_slice_in_dim(all_values, offset, step_rows, 0)
        key_positions = offset + jnp.arange(step_rows, dtype=jnp.int32)

        def query_compute(current):
            grads = grad_step(
                queries,
                grad_heads,
                log_total,
                delta,
                query_positions,
                key_block,
                value_block,
                key_positions,
                seq_lengths,
                bounds,
                table32,
            )
            return (current[0] + grads[0], current[1] + grads[3])

        skipped = (offset > query_last) | (offset >= longest)
        return lax.cond(skipped, same_state, query_compute, running)

    grad_queries, grad_table = lax.fori_loop(
        0, total_rows // step_rows, query_side, (zero_heads, zero_table)
    )
    all_totals, all_deltas = (
        lax.all_gather(log_total, BLK, axis=0, tiled=True),
        lax.all_gather(delta, BLK, axis=0, tiled=True),
    )
    query_piece = lax.all_gather(queries, BLK, axis=0, tiled=True)
    grad_piece = lax.all_gather(grad_heads, BLK, axis=0, tiled=True)
    piece_rows = query_piece.shape[0]
    key_part_rows = math.gcd(piece_rows, group_rows)

    def key_one_part(step_index, inner_state):
        offset = step_index * key_part_rows
        query_part = lax.dynamic_slice_in_dim(query_piece, offset, key_part_rows, 0)
        grad_part = lax.dynamic_slice_in_dim(grad_piece, offset, key_part_rows, 0)
        total_part = lax.dynamic_slice_in_dim(all_totals, offset, key_part_rows, 0)
        delta_part = lax.dynamic_slice_in_dim(all_deltas, offset, key_part_rows, 0)
        part_positions = offset + jnp.arange(key_part_rows, dtype=jnp.int32)

        def key_compute(current):
            grads = grad_step(
                query_part,
                grad_part,
                total_part,
                delta_part,
                part_positions,
                keys,
                values,
                query_positions,
                seq_lengths,
                bounds,
                table32,
            )
            return (current[0] + grads[1], current[1] + grads[2])

        skipped = (offset + key_part_rows - 1 < query_first) | (query_first >= longest)
        return lax.cond(skipped, same_state, key_compute, inner_state)

    grad_keys, grad_values = lax.fori_loop(
        0, piece_rows // key_part_rows, key_one_part, (zero_heads, zero_heads)
    )
    grad_stack = jnp.stack((grad_queries, grad_keys, grad_values), axis=2).astype(jnp.bfloat16)
    grad_projected = to_tokens(grad_stack)
    grad_weights = jnp.einsum(
        "td,tce->cde", attn_in, grad_projected, preferred_element_type=jnp.float32
    )
    grad_attn_in = jnp.einsum(
        "tce,cde->td", grad_projected, stacked_weights, preferred_element_type=jnp.float32
    )
    grad_norm_attn, grad_gain_attn = norm_backward(grad_attn_in, source, inv_attn, gain_attn32)
    grad_tokens = grad_hidden + grad_norm_attn
    table_terms = lax.dynamic_update_slice_in_dim(
        jnp.zeros((NUM_BUCKETS, HEADS), jnp.float32), grad_table, head_index * local_heads, 1
    ).reshape(NUM_BUCKETS * HEADS)
    reduced = (
        lax.psum_scatter(grad_weights[0], (HEAD, BLK), scatter_dimension=0, tiled=True),
        lax.psum_scatter(grad_weights[1], (HEAD, BLK), scatter_dimension=0, tiled=True),
        lax.psum_scatter(grad_weights[2], (HEAD, BLK), scatter_dimension=0, tiled=True),
        lax.psum_scatter(grad_out_w, (HEAD, BLK), scatter_dimension=1, tiled=True),
        lax.psum_scatter(grad_gain_attn, (HEAD, BLK), scatter_dimension=0, tiled=True),
        lax.psum_scatter(table_terms, (HEAD, BLK), scatter_dimension=0, tiled=True),
        lax.psum_scatter(grad_gain_moe, (HEAD, BLK), scatter_dimension=0, tiled=True),
        lax.psum_scatter(grad_router, (HEAD, BLK), scatter_dimension=0, tiled=True),
    )
    return (
        result.astype(jnp.bfloat16).reshape(tokens.shape),
        grad_tokens.reshape(tokens.shape),
        reduced[4],
        reduced[0],
        reduced[1],
        reduced[2],
        reduced[3],
        reduced[5],
        reduced[6],
        reduced[7],
        grad_expert_in,
        grad_expert_out,
    )


BF = jnp.bfloat16
F4 = jnp.float32
NEG = -1e30
QB = 256
TILE = 512
LANES = 128


def dot(left, right, left_dim=1, right_dim=0):
    dims = (((left_dim,), (right_dim,)), ((), ()))
    return lax.dot_general(left, right, dims, preferred_element_type=F4)


def iota(shape, dim):
    return lax.broadcasted_iota(jnp.int32, shape, dim)


class Place:
    def __init__(self, lengths):
        self.lengths = lengths

    def __getitem__(self, item):
        if item == 0:
            return lax.axis_index(BLK)
        if item == 1:
            return lax.axis_index(HEAD)
        return self.lengths[lax.axis_index(HEAD)]


class Made(tuple):
    @property
    def token(self):
        return self[-1]


def vmem_call(body, lengths, args, outs, scratch=(), ties=(), loose=(), away=()):
    count, tied, made = len(args), len(ties), len(outs)

    def kernel(length_ref, *refs):
        inputs, rest = refs[:count], refs[count + tied :]
        body(Place(length_ref), *inputs, *rest[:made], *rest[made + 1 :])
        rest[made][...] = jnp.zeros((8, LANES), F4)

    vmem = pl.BlockSpec(memory_space=pltpu.VMEM)
    place = pl.BlockSpec(memory_space=pl.ANY)
    return Made(
        pl.pallas_call(
            kernel,
            out_shape=tuple(outs) + (shaped((8, LANES), F4),),
            in_specs=[pl.BlockSpec(memory_space=pltpu.SMEM)]
            + [place if i in loose else vmem for i in range(count)]
            + [vmem] * tied,
            out_specs=tuple(place if i in away else vmem for i in range(made)) + (vmem,),
            scratch_shapes=list(scratch),
            compiler_params=pltpu.CompilerParams(vmem_limit_bytes=60 * 1024 * 1024),
            cost_estimate=pl.CostEstimate(flops=1, bytes_accessed=1, transcendentals=0),
        )(lengths, *args, *ties)
    )


def shaped(shape, dtype):
    return jax.ShapeDtypeStruct(shape, dtype)


def ring_block(step, own_blk, ring_len):
    half = ring_len // 2
    place = jnp.where((own_blk & 1) == 0, own_blk >> 1, ring_len - 1 - (own_blk >> 1))
    place = (place + step) & (ring_len - 1)
    return jnp.where(place < half, 2 * place, 2 * ring_len - 1 - 2 * place)


def ring_steps(ring_len):
    steps = [0]
    for hop in range(1, ring_len // 2):
        steps += [-hop, hop]
    return steps + [ring_len // 2]


def norm_scale(values):
    return lax.rsqrt(jnp.mean(values * values, axis=-1, keepdims=True) + norm_eps)


def head_tile(block, head, place):
    tile = block[:, LANES * (head // 2) : LANES * (head // 2) + LANES].astype(F4)
    return tile if head % 2 == place else pltpu.roll(tile, HEAD_DIM, 1)


def column(row, size):
    square = jnp.where(iota((size, size), 0) == iota((size, size), 1), row.astype(F4), 0.0)
    return jnp.sum(square, axis=1, keepdims=True)


def pack_units(n, sc, wq, wk, wv, gain_a, gain_m, router, table, out):
    rows = wq.shape[0]
    lane = iota((rows, LANES), 1)
    row = iota((rows, LANES), 0)

    def widen(values, at):
        blank = jnp.zeros((values.shape[0], LANES - values.shape[1]), F4)
        return pltpu.roll(jnp.concatenate([values.astype(F4), blank], axis=1), at, 1)

    misc = widen(jnp.transpose(router[...].astype(F4)), 2)
    misc = jnp.where(lane == 0, column(gain_a[...], rows), misc)
    misc = jnp.where(lane == 1, column(gain_m[...], rows), misc)
    listed = jnp.broadcast_to(widen(table[...], 16), (rows, LANES))
    misc = (misc + jnp.where(row == 0, listed, 0.0)).astype(BF)
    for j in range(n):
        pair, turn = j // 2, j % 2
        for c, weight in enumerate((wq, wk, wv)):
            own = head_tile(weight, 3 * pair + turn, 0)
            both = head_tile(weight, 3 * pair + 2, 1)
            out[j, :, LANES * c : LANES * c + LANES] = jnp.where(
                lane < HEAD_DIM, own, both
            ).astype(BF)
        out[j, :, 3 * LANES : 4 * LANES] = misc


def place_rows(sc, n, rows, parts, dest):
    for kk, part in enumerate(parts):
        for j in range(n):
            first = pl.multiple_of(((sc[1] ^ kk) * n + j) * rows, 8)
            dest[pl.ds(first, rows), :] = part[j].astype(F4)


def unpack_units(n, rows, sc, p0, p1, p2, p3, unit_w, misc, misc_t, table, buf):
    place_rows(sc, n, rows, (p0, p1, p2, p3), buf)
    unit_w[...] = buf[:, 0 : 3 * LANES].astype(BF)
    for b in range(NUM_BUCKETS):
        table[b : b + 1, :] = buf[rows * b : rows * b + 1, 3 * LANES : 4 * LANES]
    tail = buf[:, 3 * LANES : 4 * LANES]
    misc[...] = tail.astype(BF)
    misc_t[...] = jnp.transpose(tail)


def bias_strips(n, sc, table, buckets, out, line):
    row = iota((8, TILE), 0)
    pair, turn = sc[0] >> 1, sc[0] & 1
    listed = table[...]
    lane = iota(listed.shape, 1)
    reach = buckets.shape[1]
    inside = iota((NUM_BUCKETS, reach), 0) == buckets[...]
    for unit, head in enumerate((3 * pair + turn, 3 * pair + 2)):
        entry = jnp.sum(jnp.where(lane == 16 + head, listed, 0.0), axis=1, keepdims=True)
        line[:, 0:QB] = jnp.zeros((1, QB), F4)
        line[:, QB:] = jnp.sum(jnp.where(inside, entry, 0.0), axis=0, keepdims=True)
        out[unit, 0] = jnp.full((QB, QB), NEG, F4)
        for far in range(n):
            flat = jnp.broadcast_to(line[:, far * QB : far * QB + TILE], (8, TILE))
            turned = flat
            for c in range(1, 8):
                turned = jnp.where(row == c, pltpu.roll(flat, c, 1), turned)
            for group in range(QB // 8):
                moved = turned if group == 0 else pltpu.roll(turned, 8 * group, 1)
                strip = moved[:, QB:]
                if far == 0:
                    after = iota((8, QB), 1) >= iota((8, QB), 0) + 8 * group
                    strip = jnp.where(after, strip, NEG)
                out[unit, far + 1, 8 * group : 8 * group + 8, :] = strip


def ones_row(cols):
    return jnp.where(iota((HEAD_DIM, cols), 0) == 0, 1.0, 0.0).astype(BF)


def unit_operands(n, sc, blocks, misc_t, unit_w, normed, outs):
    key_own, key_both, query_t, key_t, value_t, value_r = outs
    lane = iota((QB, LANES), 1)
    row = iota((QB, LANES), 0)
    gain = misc_t[0:1, :]
    for i, step in enumerate(ring_steps(n)):
        place = ring_block(step, sc[0], n)
        first = pl.multiple_of(place * QB, QB)
        block = jnp.concatenate([part[...].astype(F4) for part in blocks[i]], axis=0)
        rows = (block * norm_scale(block) * gain).astype(BF)
        normed[place] = rows
        made = dot(rows, unit_w[...])
        low = made.astype(BF)
        turned = jnp.transpose(made).astype(BF)
        keys = made[:, LANES : 2 * LANES]
        hidden_key = jnp.where(first + row < sc[2], 0.0, NEG)
        own = jnp.where(lane < HEAD_DIM, keys, jnp.where(lane == HEAD_DIM, hidden_key, 0.0))
        both = jnp.where(lane >= HEAD_DIM, keys, jnp.where(lane == 0, hidden_key, 0.0))
        key_own[pl.ds(first, QB), :] = own.astype(BF)
        key_both[pl.ds(first, QB), :] = both.astype(BF)
        query_t[:, pl.ds(first, QB)] = turned[0:LANES]
        key_t[:, pl.ds(first, QB)] = turned[LANES : 2 * LANES]
        value_t[:, pl.ds(first, QB)] = turned[2 * LANES :]
        value_r[pl.ds(first, QB), :] = low[:, 2 * LANES :]


class Unit:
    def __init__(self, shared, sc):
        self.shared = shared
        self.lo = HEAD_DIM if shared else 0
        self.part = LANES if shared else QB
        self.shift = pl.multiple_of((sc[0] & 1) * LANES, LANES) if shared else 0

    def lanes(self, block):
        start = block * QB if isinstance(block, int) else pl.multiple_of(block * QB, QB)
        return pl.ds(start + self.shift, self.part)

    def columns(self, ref, pair):
        rows = pl.ds(self.lo, HEAD_DIM)
        return jnp.concatenate([ref[rows, self.lanes(2 * pair + q)] for q in range(2)], axis=1)

    def padded(self, half, other):
        return jnp.concatenate([other, half] if self.shared else [half, other], axis=0)

    def strip(self, bias, far):
        def piece(key_half, query_half):
            at = max(far + query_half - key_half, -1) + 1 if isinstance(far, int) else (
                jnp.maximum(far + query_half - key_half, -1) + 1
            )
            return bias[at, :, pl.ds(self.shift, self.part)]

        return jnp.concatenate(
            [jnp.concatenate([piece(k, 0), piece(k, 1)], axis=1) for k in range(2)], axis=0
        )


def attend_tiles(n, unit, key_ref, query_t, value_t, bias, heads, log_ref):
    cols = 2 * unit.part
    for pair in range(n // 2):
        queries = unit.padded(unit.columns(query_t, pair), ones_row(cols))
        top = jnp.zeros((1, cols), F4) + NEG
        total = jnp.zeros((1, cols), F4)
        mixed = jnp.zeros((HEAD_DIM, cols), F4)
        for part in range(pair + 1):
            tile = dot(key_ref[part * TILE : (part + 1) * TILE, :], queries)
            tile = tile + unit.strip(bias, 2 * (pair - part))
            new_top = jnp.maximum(top, jnp.max(tile, axis=0, keepdims=True))
            weights = jnp.exp(tile - new_top)
            decay = jnp.exp(top - new_top)
            top = new_top
            total = total * decay + jnp.sum(weights, axis=0, keepdims=True)
            values = value_t[unit.lo : unit.lo + HEAD_DIM, part * TILE : (part + 1) * TILE]
            mixed = mixed * decay + dot(values, weights.astype(BF))
        made = (mixed / total).astype(BF)
        log_total = top + jnp.log(total)
        at = slice(QB, QB + LANES) if unit.shared else slice(0, QB)
        for q in range(2):
            cut = slice(q * unit.part, (q + 1) * unit.part)
            heads[2 * pair + q, :, at] = made[:, cut]
            log_ref[2 * pair + q] = log_total[:, cut]


def copies_of(pairs, sems):
    return [
        pltpu.make_async_copy(source, dest, sems.at[i]) for i, (source, dest) in enumerate(pairs)
    ]


def attend_units(n, sc, *refs):
    blocks = [(ref,) for ref in refs[: n - 1]] + [refs[n - 1 : n + 1]]
    misc_t, unit_w, table, buckets, heads, logs_own, logs_both = refs[n + 1 : n + 8]
    outs = refs[n + 8 : n + 15]
    kept, (value_t, line, sems) = refs[n + 15 : n + 22], refs[n + 22 :]
    normed, key_own, key_both, query_t, key_t, value_r, bias = kept
    copies = copies_of(list(zip(kept, outs)), sems)
    placed = (key_own, key_both, query_t, key_t, value_t, value_r)
    unit_operands(n, sc, blocks, misc_t, unit_w, normed, placed)
    for copy in copies[:-1]:
        copy.start()
    bias_strips(n, sc, table, buckets, bias, line)
    copies[-1].start()
    for shared, key_ref, log_ref in ((False, key_own, logs_own), (True, key_both, logs_both)):
        strips = bias.at[int(shared)]
        attend_tiles(n, Unit(shared, sc), key_ref, query_t, value_t, strips, heads, log_ref)
    for copy in copies:
        copy.wait()


def split_units(ref):
    return (ref.at[:, 0 : 3 * HEAD_DIM, :], ref.at[:, 3 * HEAD_DIM :, :])


def unit_grads(n, sc, *refs):
    key_own, key_both, query_t, key_t, value_r, strips_in, heads, grads_in = refs[:8]
    logs_own, logs_both, stacked, table = refs[8:12]
    grads_own, grads_both, delta_own, delta_both, grad_k, grad_v, strips, bias, sems = refs[12:]
    copies = copies_of([(strips_in.at[i], bias.at[i]) for i in (1, 0)], sems)
    for copy in copies:
        copy.start()
    own, both = split_units(stacked)
    common = (query_t, key_t, value_r, heads, grads_in)
    shared_only = (logs_both, both, table.at[n : 2 * n], grads_both, delta_both)
    own_only = (logs_own, own, table.at[0:n], grads_own, delta_own)
    sums = (grad_k, grad_v, strips)
    grads_of_unit(n, True, sc, copies[0], bias.at[1], key_both, *common, *shared_only, *sums)
    grads_of_unit(n, False, sc, copies[1], bias.at[0], key_own, *common, *own_only, *sums)


def grads_of_unit(
    n,
    shared,
    sc,
    copy,
    bias,
    key_ref,
    query_t,
    key_t,
    value_r,
    heads,
    grads_in,
    logs,
    stacked,
    table,
    grad_t,
    delta,
    grad_k,
    grad_v,
    strips,
):
    unit = Unit(shared, sc)
    cols = 2 * unit.part
    at = slice(QB, QB + LANES) if shared else slice(0, QB)
    rows = slice(unit.lo, unit.lo + HEAD_DIM)
    for j in range(n):
        grads = grads_in[j, :, at]
        grad_t[:, j * unit.part : (j + 1) * unit.part] = grads
        product = grads.astype(F4) * heads[j, :, at].astype(F4)
        delta[j] = jnp.sum(product, axis=0, keepdims=True)
    grad_k[...] = jnp.zeros(grad_k.shape, F4)
    grad_v[...] = jnp.zeros(grad_v.shape, F4)
    strips[...] = jnp.zeros(strips.shape, F4)
    copy.wait()

    def one_tile(pair, carry):
        nothing = jnp.zeros((HEAD_DIM, cols), BF)
        raw_queries = unit.columns(query_t, pair)
        queries = unit.padded(raw_queries, ones_row(cols))
        plain = unit.padded(raw_queries, nothing)
        start = pair * cols
        grads = unit.padded(grad_t[:, pl.ds(start, cols)], nothing)
        log_total = jnp.concatenate([logs[2 * pair + q] for q in range(2)], axis=1)
        inner = jnp.concatenate([delta[2 * pair + q] for q in range(2)], axis=1)

        def step(part, made):
            key_at = part * TILE
            far = 2 * (pair - part)
            scores = dot(key_ref[pl.ds(key_at, TILE), :], queries)
            scores = scores + unit.strip(bias, far)
            probs = jnp.exp(scores - log_total)
            grad_probs = dot(value_r[pl.ds(key_at, TILE), :], grads)
            grad_scores = probs * (grad_probs - inner)
            for key_half in range(2):
                for q in range(2):
                    place = max(far + q - key_half, -1) + 1
                    strips[place, :, pl.ds(unit.shift, unit.part)] += grad_scores[
                        key_half * QB : (key_half + 1) * QB, q * unit.part : (q + 1) * unit.part
                    ]
            low = grad_scores.astype(BF)
            grad_v[pl.ds(key_at, TILE), :] += dot(probs.astype(BF), grads, 1, 1)
            grad_k[pl.ds(key_at, TILE), :] += dot(low, plain, 1, 1)
            return made + dot(key_t[pl.ds(unit.lo, HEAD_DIM), pl.ds(key_at, TILE)], low)

        made = jnp.zeros((HEAD_DIM, cols), F4)
        for part in range(pair + 1):
            made = step(part, made)
        for q in range(2):
            cut = made[:, q * unit.part : (q + 1) * unit.part]
            if shared:
                half = HEAD_DIM // 2
                cut = jnp.concatenate([cut[0:half], cut[half:]], axis=1)
            stacked[2 * pair + q, 2 * HEAD_DIM :, :] = cut.astype(BF)
        return carry

    for pair in range(n // 2):
        one_tile(pair, 0)
    for j in range(n):
        block = slice(QB * j, QB * (j + 1))
        stacked[j, 0:HEAD_DIM, :] = jnp.transpose(grad_k[block, :])[rows].astype(BF)
        stacked[j, HEAD_DIM : 2 * HEAD_DIM, :] = jnp.transpose(grad_v[block, :])[rows].astype(BF)
    row = iota((8, TILE), 0)
    empty = jnp.zeros((8, QB), F4)
    for far in range(n):
        total = jnp.zeros((8, TILE), F4)
        for group in range(QB // 8):
            rows8 = strips[far + 1, 8 * group : 8 * group + 8, :]
            wide = jnp.concatenate([empty, rows8], axis=1)
            total = total + (wide if group == 0 else pltpu.roll(wide, TILE - 8 * group, 1))
        lined = jnp.where(row == 0, total, 0.0)
        for c in range(1, 8):
            lined = lined + jnp.where(row == c, pltpu.roll(total, TILE - c, 1), 0.0)
        table[far] = jnp.sum(lined, axis=0, keepdims=True)


def dispatch_rows(n, cap, sc, route_ref, cot, wo_t, wq, wk, wv, out, target, w_out):
    tok = cot.shape[0]
    route = route_ref[...]
    chosen = iota((n, tok), 0) == route
    upto = jnp.where(iota((tok, tok), 0) <= iota((tok, tok), 1), 1.0, 0.0).astype(BF)
    filled = dot(jnp.where(chosen, 1.0, 0.0).astype(BF), upto)
    slot = jnp.sum(jnp.where(chosen, filled - 1.0, 0.0), axis=0, keepdims=True)
    slot = slot.astype(jnp.int32)
    place = route * cap + slot
    target[...] = jnp.broadcast_to(place, target.shape)
    spread = jnp.where(iota((n * cap, tok), 0) == place, 1.0, 0.0).astype(BF)
    packed = dot(spread, cot[...]).astype(BF)
    weights = jnp.concatenate([w[...].astype(F4) for w in (wq, wk, wv)], axis=0).astype(BF)
    for j in range(n):
        out[j, 0:cap, :] = packed[j * cap : (j + 1) * cap]
        out[j, cap:, :] = wo_t[...]
        w_out[j] = weights


def spread_matrix(target, rows):
    place = target[0:1, :]
    return jnp.where(iota((rows, place.shape[1]), 0) == place, 1.0, 0.0)


def hidden_rows(
    n, cap, sc, heads, p0, p1, p2, p3, tokens, misc_t, target, attn, hidden_out, out, wo_t, buf, wide
):
    place_rows(sc, n, p0.shape[1], (p0, p1, p2, p3), wide)
    wo_t[...] = wide[...].astype(BF)
    for pair in range(n // 2):
        at = 3 * pair * HEAD_DIM
        for turn in range(2):
            made = heads[2 * pair + turn].astype(F4)
            buf[at + turn * HEAD_DIM : at + (turn + 1) * HEAD_DIM, :] = made[:, 0:QB]
            both = slice(turn * LANES, (turn + 1) * LANES)
            buf[at + 2 * HEAD_DIM : at + 3 * HEAD_DIM, both] = made[:, QB:]
    rows = jnp.transpose(buf[...]).astype(BF)
    attn[...] = rows
    hidden = tokens[...].astype(F4) + dot(rows, wo_t[...], 1, 1)
    hidden_out[...] = hidden
    moe_in = (hidden * norm_scale(hidden) * misc_t[1:2, :]).astype(BF)
    packed = dot(spread_matrix(target, n * cap).astype(BF), moe_in).astype(BF)
    for j in range(n):
        out[j] = packed[j * cap : (j + 1) * cap]


def gelu_pair(values):
    scale = math.sqrt(2.0 / math.pi)
    square = values * values
    bend = jnp.tanh(scale * (values + 0.044715 * values * square))
    act = 0.5 * values * (1.0 + bend)
    slope = 0.5 * (1.0 + bend) + 0.5 * values * (1.0 - bend * bend) * scale * (
        1.0 + 3.0 * 0.044715 * square
    )
    return (act, slope)


def route_probs(experts, sc, rows, misc):
    logits = dot(rows, misc[...])
    lane = iota(logits.shape, 1)
    real = (lane >= 2) & (lane < 2 + experts)
    logits = jnp.where(real, logits, NEG)
    powers = jnp.where(real, jnp.exp(logits - jnp.max(logits, axis=-1, keepdims=True)), 0.0)
    probs = powers / jnp.sum(powers, axis=-1, keepdims=True)
    chosen = lane == sc[0] + 2
    gate = jnp.sum(jnp.where(chosen, probs, 0.0), axis=-1, keepdims=True)
    return (probs, chosen, gate)


def flat_rows(ref, cap=None):
    return jnp.concatenate([ref[j][0:cap] for j in range(ref.shape[0])], axis=0)


def expert_back(
    experts, sc, rows_ref, cot_ref, in_a, out_a, in_b, out_b, misc, back, made, log_out
):
    rows, cots = flat_rows(rows_ref), flat_rows(cot_ref, rows_ref.shape[1])
    probs, chosen, gate = route_probs(experts, sc, rows, misc)
    inner = jnp.zeros(gate.shape, F4)
    total = jnp.zeros(rows.shape, F4)
    result = jnp.zeros(rows.shape, F4)
    for w_in, w_out in ((in_a, out_a), (in_b, out_b)):
        act, slope = gelu_pair(dot(rows, w_in[...]))
        low = act.astype(BF)
        result = result + dot(low, w_out[...])
        grad_act = dot(cots, w_out[...], 1, 1)
        inner = inner + jnp.sum(low.astype(F4) * grad_act, axis=-1, keepdims=True)
        total = total + dot((gate * grad_act * slope).astype(BF), w_in[...], 1, 1)
    grad_logits = (inner * probs * (jnp.where(chosen, 1.0, 0.0) - gate)).astype(BF)
    log_out[...] = grad_logits
    made[...] = (gate * result).astype(made.dtype)
    back[...] = (total + dot(grad_logits, misc[...], 1, 1)).astype(back.dtype)


def expert_weights(experts, count, more, sc, *refs):
    rows_refs, cot_refs = refs[:count], refs[count : 2 * count]
    w_in, w_out, misc = refs[2 * count : 2 * count + 3]
    begun = refs[2 * count + 3 : 2 * count + 5] if more else None
    grad_in, grad_out, token, all_rows, all_grads, turned = refs[2 * count + (5 if more else 3) :]
    token[...] = jnp.zeros(token.shape, F4)
    size = rows_refs[0].shape[0] * rows_refs[0].shape[1]

    @pl.when(pl.program_id(0) == 0)
    def _():
        for i in range(count):
            at = slice(i * size, (i + 1) * size)
            rows, cots = flat_rows(rows_refs[i]), flat_rows(cot_refs[i], rows_refs[i].shape[1])
            gate = route_probs(experts, sc, rows, misc)[2]
            all_rows[at, :] = rows
            turned[:, at] = jnp.transpose(rows.astype(F4)).astype(BF)
            all_grads[at, :] = (gate * cots.astype(F4)).astype(BF)

    rows, grads = all_rows[...], all_grads[...]
    act, slope = gelu_pair(dot(rows, w_in[...]))
    grad_pre = (dot(grads, w_out[...], 1, 1) * slope).astype(BF)
    in_part = dot(turned[...], grad_pre)
    out_part = dot(act.astype(BF), grads, 0, 0)
    grad_in[...] = begun[0][...] + in_part if more else in_part
    grad_out[...] = begun[1][...] + out_part if more else out_part


def chunked_specs(w_in):
    depth, hidden = w_in.shape
    chunk = 2 * LANES
    columns = pl.BlockSpec((depth, chunk), lambda i: (0, i))
    lines = pl.BlockSpec((chunk, depth), lambda i: (i, 0))
    return hidden // chunk, columns, lines


def expert_weights_call(experts, lengths, rows_in, cots_in, w_in, w_out, misc, ties, begun=()):
    count, (depth, hidden) = len(rows_in), w_in.shape
    size = rows_in[0].shape[0] * rows_in[0].shape[1]
    body = functools.partial(expert_weights, experts, count, bool(begun))
    args = tuple(rows_in) + tuple(cots_in) + (w_in, w_out, misc) + tuple(begun)

    def kernel(length_ref, *refs):
        body(Place(length_ref), *refs[: len(args)], *refs[len(args) + len(ties) :])

    whole = pl.BlockSpec(memory_space=pltpu.VMEM)
    steps, columns, lines = chunked_specs(w_in)
    return pl.pallas_call(
        kernel,
        grid=(steps,),
        out_shape=(
            shaped((depth, hidden), F4),
            shaped((hidden, depth), F4),
            shaped((8, LANES), F4),
        ),
        in_specs=[pl.BlockSpec(memory_space=pltpu.SMEM)]
        + [whole] * (2 * count)
        + [columns, lines, whole]
        + ([columns, lines] if begun else [])
        + [whole] * len(ties),
        out_specs=(columns, lines, whole),
        scratch_shapes=[
            pltpu.VMEM((count * size, depth), BF),
            pltpu.VMEM((count * size, depth), BF),
            pltpu.VMEM((depth, count * size), BF),
        ],
        compiler_params=pltpu.CompilerParams(vmem_limit_bytes=60 * 1024 * 1024),
        cost_estimate=pl.CostEstimate(flops=1, bytes_accessed=1, transcendentals=0),
    )(lengths, *args, *ties)


def result_rows(n, cap, sc, made, target, hidden, out):
    rows = flat_rows(made)
    spread = jnp.transpose(spread_matrix(target, n * cap)).astype(BF)
    out[...] = (hidden[...] + dot(spread, rows)).astype(BF)


def norm_back(grads, source, gain):
    scale = norm_scale(source)
    weighted = grads * gain
    inner = jnp.mean(weighted * source, axis=-1, keepdims=True)
    return (scale * weighted - source * (scale * scale * scale) * inner, scale)


def hidden_grads(
    n, cap, sc, back, target, hidden_ref, misc_t, cot, wo_t, grad_out, low_out, gain_out, out, buf
):
    spread = jnp.transpose(spread_matrix(target, n * cap)).astype(BF)
    grads = dot(spread, flat_rows(back))
    hidden = hidden_ref[...]
    normed, scale = norm_back(grads, hidden, misc_t[1:2, :])
    gain_out[...] = jnp.broadcast_to(
        jnp.sum(grads * hidden * scale, axis=0, keepdims=True), gain_out.shape
    )
    total = cot[...].astype(F4) + normed
    grad_out[...] = total
    low = total.astype(BF)
    low_out[...] = low
    buf[...] = jnp.transpose(dot(low, wo_t[...])).astype(BF)
    for pair in range(n // 2):
        at = 3 * pair * HEAD_DIM
        for turn in range(2):
            out[2 * pair + turn, :, 0:QB] = buf[at + turn * HEAD_DIM : at + (turn + 1) * HEAD_DIM, :]
            both = slice(turn * LANES, (turn + 1) * LANES)
            out[2 * pair + turn, :, QB:] = buf[at + 2 * HEAD_DIM : at + 3 * HEAD_DIM, both]


def unfolded(piece):
    return jnp.concatenate([piece[:, 0:LANES], piece[:, LANES:]], axis=0)


def unpack_full(n, rows, sc, p0, p1, p2, p3, out, wide):
    inner = wide.shape[1] // 3
    for kk, part in enumerate((p0, p1, p2, p3)):
        for j in range(n):
            first = pl.multiple_of(((sc[1] ^ kk) * n + j) * rows, 8)
            block = part[j].astype(F4)
            for c in range(3):
                wide[pl.ds(first, rows), c * inner : (c + 1) * inner] = block[
                    c * rows : (c + 1) * rows
                ]
    out[...] = wide[...].astype(BF)


def token_grads(n, sc, stacked, weights, tokens, hidden_grad, misc_t, out, buf):
    own, both = split_units(stacked)
    inner = weights.shape[1] // 3
    for pair in range(n // 2):
        at = 3 * pair * HEAD_DIM
        last = at + 2 * HEAD_DIM
        for turn in range(2):
            j = 2 * pair + turn
            for c, piece in enumerate((2, 0, 1)):
                lo = c * inner + at + turn * HEAD_DIM
                buf[lo : lo + HEAD_DIM, :] = own[j, piece * HEAD_DIM : (piece + 1) * HEAD_DIM, :]
            half = slice(turn * LANES, (turn + 1) * LANES)
            buf[last : last + HEAD_DIM, half] = unfolded(both[j, 2 * HEAD_DIM :, :])
        for c in (1, 2):
            rows = slice((c - 1) * HEAD_DIM, c * HEAD_DIM)
            total = both[2 * pair, rows, :].astype(F4) + both[2 * pair + 1, rows, :].astype(F4)
            buf[c * inner + last : c * inner + last + HEAD_DIM, :] = total.astype(BF)
    made = jnp.transpose(dot(weights[...], buf[...]))
    normed, unused = norm_back(made, tokens[...].astype(F4), misc_t[0:1, :])
    out[...] = (hidden_grad[...] + normed).reshape(out.shape)


def unit_weight_grads(n, heads, sc, normed, stacked, lines_ref, buckets, *rest):
    own, both = split_units(stacked)
    outs, (buf, table) = rest[:heads], rest[heads:]
    width = buf.shape[1]
    sums = []
    for unit in range(2):
        made = jnp.zeros((NUM_BUCKETS, 1), F4)
        for far in range(n):
            lines = lines_ref.at[unit * n : (unit + 1) * n]
            line = lines[far][:, QB:]
            if far + 1 < n:
                line = line + lines[far + 1][:, :QB]
            inside = iota((NUM_BUCKETS, QB), 0) == buckets[:, far * QB : (far + 1) * QB]
            made = made + jnp.sum(jnp.where(inside, line, 0.0), axis=1, keepdims=True)
        sums.append(made)
    lane = iota((NUM_BUCKETS, width), 1)
    high = [value.astype(BF).astype(F4) for value in sums]
    listed = jnp.zeros((NUM_BUCKETS, width), F4)
    for at, value in enumerate(high + [sums[0] - high[0], sums[1] - high[1]]):
        listed = jnp.where(lane == at, value, listed)
    table[...] = listed
    total = None
    for j in range(n):
        shared = unfolded(both[j, 2 * HEAD_DIM :, :]).astype(F4)
        blank = jnp.zeros(shared.shape, F4)
        turn = jnp.broadcast_to((sc[0] & 1) == 0, shared.shape)
        shared = jnp.concatenate(
            [jnp.where(turn, shared, blank), jnp.where(turn, blank, shared)], axis=1
        )
        pieces = [own[j, 2 * HEAD_DIM :, :], shared.astype(BF)]
        for c in range(2):
            rows = slice(c * HEAD_DIM, (c + 1) * HEAD_DIM)
            pieces += [own[j, rows, :], both[j, rows, :]]
        part = dot(jnp.concatenate(pieces, axis=0), normed[j])
        total = part if total is None else total + part
    buf[...] = jnp.transpose(total)
    rows = buf.shape[0] // heads
    for kk in range(heads):
        to = sc[1] ^ kk
        outs[kk][...] = jnp.concatenate(
            [
                buf[pl.ds(pl.multiple_of(to * rows, 8), rows), :],
                table[pl.ds(pl.multiple_of(to * n, 8), n), :],
                jnp.zeros((8, width), F4),
            ],
            axis=0,
        ).astype(BF)


def two_parts(values, gap):
    high = values.astype(BF).astype(F4)
    lane = iota(values.shape, 1)
    low = pltpu.roll(jnp.where(lane < gap, values - high, 0.0), gap, 1)
    return jnp.where(lane < gap, high, low)


def one_part(values, gap):
    return values + pltpu.roll(values, values.shape[1] - gap, 1)


def weight_sums(n, rows, heads, sc, *refs):
    units, outer = refs[:heads], refs[heads : 2 * heads]
    outs, buf = refs[2 * heads : -1], refs[-1]
    total = (units[0][...].astype(F4) + units[1][...].astype(F4)) + (
        units[2][...].astype(F4) + units[3][...].astype(F4)
    )
    base = n * rows
    entries = two_parts(one_part(total[base : base + n], 2), 2)
    wide = (outer[0][...].astype(F4) + outer[1][...].astype(F4)) + (
        outer[2][...].astype(F4) + outer[3][...].astype(F4)
    )
    width = wide.shape[1] - LANES
    extra = two_parts(one_part(wide[:, width:], 16), 16)
    for to in range(n):
        at = slice(to * rows, (to + 1) * rows)
        entry = pltpu.roll(entries[to : to + 1, 0:LANES], 64, 1)
        entry = jnp.where(iota((rows, LANES), 0) == 0, entry, 0.0)
        buf[to] = jnp.concatenate([total[at], wide[at, 0:width], extra[at] + entry], axis=1)
    for k in range(n):
        outs[k][...] = buf[sc[0] ^ k].astype(BF)


def as_row(values):
    size = values.shape[0]
    square = jnp.where(iota((size, size), 0) == iota((size, size), 1), values, 0.0)
    return jnp.sum(square, axis=0, keepdims=True)


def weight_final(n, experts, sc, *refs):
    parts, (wq, wk, wv, gain_a) = refs[:n], refs[n : n + 4]
    grads = refs[n + 4 : n + 7]
    gain, table, grad_out, gain_out, router, buf, tables = refs[n + 7 :]
    rows = wq.shape[0]
    units = 3 * LANES
    small = slice(parts[0].shape[1] - LANES, parts[0].shape[1])
    total = None
    for j in range(n):
        part = parts[j][...].astype(F4)
        buf[sc[0] ^ j] = part[:, 0:units]
        tables[sc[0] ^ j] = part[0:1, small]
        total = part[:, units:] if total is None else total + part[:, units:]
    lane = iota((rows, LANES), 1)
    inner = jnp.zeros((rows, 1), F4)
    for c, weight in enumerate((wq, wk, wv)):
        lo = LANES * c

        def piece(head, place):
            pair, turn = head // 3, head % 3
            if turn < 2:
                tile, half = buf[2 * pair + turn, 0:rows, lo : lo + LANES], 0
            else:
                tile = (
                    buf[2 * pair, 0:rows, lo : lo + LANES]
                    + buf[2 * pair + 1, 0:rows, lo : lo + LANES]
                )
                half = 1
            return tile if half == place else pltpu.roll(tile, HEAD_DIM, 1)

        for m in range(weight.shape[1] // LANES):
            tile = jnp.where(lane < HEAD_DIM, piece(2 * m, 0), piece(2 * m + 1, 1))
            cols = slice(LANES * m, LANES * m + LANES)
            grads[c][:, cols] = tile
            inner = inner + jnp.sum(weight[:, cols].astype(F4) * tile, axis=-1, keepdims=True)
    gain[...] = as_row(inner / column(gain_a[...], rows))
    lane = iota((1, HEADS), 1)
    listed = jnp.zeros((1, HEADS), F4)
    for j in range(n):
        entry = one_part(pltpu.roll(tables[j], 64, 1), 2)
        listed = listed + jnp.where(lane == 3 * (j // 2) + j % 2, entry[:, 0:1], 0.0)
        listed = listed + jnp.where(lane == 3 * (j // 2) + 2, entry[:, 1:2], 0.0)
    table[...] = listed
    width = grad_out.shape[1]
    grad_out[...] = total[:, 0:width]
    extra = total[0:rows, width:]
    extra = one_part(jnp.where(iota(extra.shape, 1) < 32, extra, 0.0), 16)
    gain_out[...] = as_row(extra[:, 1:2])
    router[...] = jnp.transpose(pltpu.roll(extra, LANES - 2, 1))[0:experts]


def out_weight_grads(heads, sc, low, attn, rows_a, rows_b, logs_a, logs_b, gain, *rest):
    outs, buf = rest[:heads], rest[heads]
    width = attn.shape[1]
    buf[:, 0:width] = dot(low[...], attn[...], 0, 0)
    router = dot(flat_rows(rows_a), logs_a[...], 0, 0) + dot(flat_rows(rows_b), logs_b[...], 0, 0)
    wide = jnp.where(iota((LANES, gain.shape[1]), 0) == 1, gain[0:1, :], 0.0)
    buf[:, width : width + LANES] = two_parts(router + jnp.transpose(wide), 16)
    rows = buf.shape[0] // heads
    for kk in range(heads):
        first = pl.multiple_of((sc[1] ^ kk) * rows, 8)
        outs[kk][...] = buf[pl.ds(first, rows), :].astype(BF)


def last_grads(n, experts, sc, *refs):
    parts, own, rest = refs[: n + 4], refs[n + 4 : n + 9], refs[n + 9 :]
    weight_final(n, experts, sc, *parts, *rest[:8], *rest[9:11])
    token_grads(n, sc, *own, rest[8], rest[11])


def swap(values, axis, flip):
    if flip == 0:
        return values
    size = lax.axis_size(axis)
    return lax.ppermute(values, axis, [(i, i ^ flip) for i in range(size)])


def exchange(messages, axis):
    return [swap(message, axis, k) for k, message in enumerate(messages)]


def hold(values, *earlier):
    return lax.optimization_barrier((values, earlier))[0]


def over_heads(stack):
    across = swap(stack, HEAD, 2)
    return (stack, swap(stack, HEAD, 1), across, swap(across, HEAD, 1))


def on_plane(
    tokens,
    attn_gain,
    w_query,
    w_key,
    w_value,
    w_out,
    bias_table,
    moe_gain,
    w_router,
    expert_in,
    expert_out,
    seq_lengths,
    rel_buckets,
    routes,
    cotangent,
):
    heads = lax.axis_size(HEAD)
    n = lax.axis_size(BLK)
    tok, width = tokens.shape[0], tokens.shape[2]
    rows = w_query.shape[0]
    total_rows = n * tok
    experts = w_router.shape[1]
    cap = 3 * tok // (2 * experts)
    slots = n * cap
    scope = jax.named_scope
    x = tokens.reshape(tok, width)
    cot = cotangent.reshape(tok, width)
    gain_a = attn_gain.reshape(1, rows)
    gain_m = moe_gain.reshape(1, rows)
    in_own, out_own = expert_in.reshape(expert_in.shape[1:]), expert_out.reshape(expert_out.shape[1:])

    def call(body, args, outs, scratch=(), ties=(), loose=(), away=()):
        return vmem_call(body, seq_lengths, args, outs, scratch, ties, loose, away)

    def all_to_all(stack, axis=BLK):
        return lax.all_to_all(stack, axis, split_axis=0, concat_axis=0, tiled=True)

    order = [ring_of(i, n) for i in range(n)]
    ahead = [(order[i], order[(i + 1) % n]) for i in range(n)]
    astern = [(b, a) for a, b in ahead]
    unit_cols = 4 * LANES

    def hop(front, back):
        with scope("rin"):
            front = lax.ppermute(front, BLK, ahead)
            back = lax.ppermute(back, BLK, astern)
            return lax.optimization_barrier((front, back))

    first = hop(x, x)
    with scope("uw"):
        packed, packed_token = call(
            functools.partial(pack_units, n),
            (w_query, w_key, w_value)
            + (gain_a, gain_m, jnp.transpose(w_router), bias_table.reshape(1, -1)),
            [shaped((n, rows, unit_cols), BF)],
        )
        unit_in = all_to_all(hold(packed, first[0]))
    with scope("cr"):
        cot_out, target, w_stack, cot_token = call(
            functools.partial(dispatch_rows, n, cap),
            (routes.reshape(1, tok), cot, jnp.transpose(w_out), w_query, w_key, w_value),
            [
                shaped((n, cap + rows, width), BF),
                shaped((8, tok), jnp.int32),
                shaped((n, 3 * rows, width), BF),
            ],
            ties=(packed_token,),
        )
    with scope("es"):
        in_other = swap(in_own, HEAD, 2)
    second = hop(*hold(first, packed_token))
    with scope("uw"):
        unit_parts = over_heads(hold(unit_in, second[0]))
    third = hop(*hold(second, unit_in, in_other, cot_token))
    half = tok // 2
    with scope("rin"):
        front_half, back_half = (third[0][:half], third[1][half:])
        front, back = lax.ppermute(front_half, BLK, ahead), lax.ppermute(back_half, BLK, astern)
    with scope("uw"):
        unit_w, misc, misc_t, table, unused = call(
            functools.partial(unpack_units, n, rows),
            unit_parts,
            [
                shaped((width, 3 * LANES), BF),
                shaped((width, LANES), BF),
                shaped((LANES, width), F4),
                shaped((NUM_BUCKETS, LANES), F4),
            ],
            [pltpu.VMEM((width, unit_cols), F4)],
        )
    with scope("es"):
        out_other = swap(hold(out_own, unit_parts[2], unit_parts[3]), HEAD, 2)

    buckets = rel_buckets.reshape(1, -1)

    with scope("cr"):
        cot_in = all_to_all(hold(cot_out, front, back, table))
        cot_rows, wo_rows = cot_in[:, :cap], cot_in[:, cap:]

    kept = [
        shaped((n, tok, width), BF),
        shaped((total_rows, LANES), BF),
        shaped((total_rows, LANES), BF),
        shaped((LANES, total_rows), BF),
        shaped((LANES, total_rows), BF),
        shaped((total_rows, LANES), BF),
        shaped((2, n + 1, QB, QB), F4),
    ]
    with scope("att"):
        (
            head_out,
            logs_own,
            logs_both,
            normed,
            key_own,
            key_both,
            query_t,
            key_t,
            value_r,
            strips,
            attend_token,
        ) = call(
            functools.partial(attend_units, n),
            (x,) + first + second + third + (front, back, misc_t, unit_w, table, buckets),
            [
                shaped((n, HEAD_DIM, QB + LANES), BF),
                shaped((n, 1, QB), F4),
                shaped((n, 1, LANES), F4),
            ]
            + kept,
            [pltpu.VMEM(k.shape, k.dtype) for k in kept]
            + [
                pltpu.VMEM((LANES, total_rows), BF),
                pltpu.VMEM((1, QB + total_rows), F4),
                pltpu.SemaphoreType.DMA((len(kept),)),
            ],
            ties=(cot_token,),
            away=range(3, 3 + len(kept)),
        )
        head_in = all_to_all(head_out)
    with scope("ow"):
        wo_parts = over_heads(hold(wo_rows, logs_both))
    with scope("cp"):
        all_cot = over_heads(hold(cot_rows, wo_parts[2]))
        cot_pair = all_cot[1]
    with scope("hid"):
        attn, hidden, moe_out, out_t, hidden_token = call(
            functools.partial(hidden_rows, n, cap),
            (head_in,) + wo_parts + (x, misc_t, target),
            [
                shaped((tok, width), BF),
                shaped((tok, width), F4),
                shaped((n, cap, width), BF),
                shaped((width, width), BF),
            ],
            [pltpu.VMEM((width, tok), F4), pltpu.VMEM((width, width), F4)],
            ties=(hold(attend_token, out_other),),

        )

    with scope("mr"):
        moe_rows = all_to_all(moe_out)
        moe_pair = swap(hold(moe_rows, all_cot[2], cot_pair), HEAD, 1)
    def backward_rows(rows_in, cots_in, kind, ties=()):
        return call(
            functools.partial(expert_back, experts),
            (rows_in, cots_in, in_own, out_own, in_other, out_other, misc),
            [
                shaped((slots, width), kind),
                shaped((slots, width), BF),
                shaped((slots, LANES), BF),
            ],
            ties=ties,
        )

    with scope("fw"):
        w_in = all_to_all(hold(w_stack, moe_pair))
    with scope("mf"):
        moe_far = swap(moe_rows, HEAD, 2)
        far_pair = swap(moe_far, HEAD, 1)

    with scope("eb"):
        back_pair, made_pair, logs_pair, token = backward_rows(moe_pair, cot_pair, BF)
        back_other = swap(back_pair, HEAD, 1)
        back_own, made_own, logs_own2, token = backward_rows(
            moe_rows, cot_rows, F4, (token,)
        )
        back_out = (back_own + back_other.astype(F4)).astype(BF).reshape(n, cap, width)
        back_out, back_token = hold((back_out, token), w_in)
        back_in = all_to_all(back_out)
    with scope("fw"):
        w_parts = over_heads(hold(w_in, back_token))
    with scope("ewg"):
        expert_ends = (in_own, out_own, misc)
        *begun, expert_token = expert_weights_call(
            experts,
            seq_lengths,
            (moe_rows, moe_pair),
            all_cot[:2],
            *expert_ends,
            (back_token,),
        )
    with scope("hg"):
        grad_hidden, grad_low, gain_moe_part, grad_heads_out, unused = call(
            functools.partial(hidden_grads, n, cap),
            (back_in, target, hidden, misc_t, cot, out_t),
            [
                shaped((tok, width), F4),
                shaped((tok, width), BF),
                shaped((8, width), F4),
                shaped((n, HEAD_DIM, QB + LANES), BF),
            ],
            [pltpu.VMEM((width, tok), BF)],
            ties=(hold(expert_token, far_pair, all_cot[3]),),
        )
        grad_heads = all_to_all(grad_heads_out)
    wide = width + LANES
    with scope("owg"):
        *out_parts, out_token = call(
            functools.partial(out_weight_grads, heads),
            (grad_low, attn, moe_rows, moe_pair, logs_own2, logs_pair, gain_moe_part),
            [shaped((width // heads, wide), BF)] * heads,
            [pltpu.VMEM((width, wide), F4)],
        )
        out_parts_in = exchange(out_parts, HEAD)
    with scope("rr"):
        res_out = made_own.astype(F4) + swap(made_pair, HEAD, 1).astype(F4)
        res_out = res_out.astype(BF).reshape(n, cap, width)
        res_in = all_to_all(hold(res_out, grad_heads, out_token))

    with scope("ag"):
        stacked, lines, unused = call(
            functools.partial(unit_grads, n),
            (
                key_own,
                key_both,
                query_t,
                key_t,
                value_r,
                strips,
                head_out,
                grad_heads,
                logs_own,
                logs_both,
            ),
            [shaped((n, 5 * HEAD_DIM + HEAD_DIM // 2, tok), BF), shaped((2 * n, 1, TILE), F4)],
            [
                pltpu.VMEM((HEAD_DIM, total_rows), BF),
                pltpu.VMEM((HEAD_DIM, total_rows // 2), BF),
                pltpu.VMEM((n, 1, QB), F4),
                pltpu.VMEM((n, 1, LANES), F4),
                pltpu.VMEM((total_rows, LANES), F4),
                pltpu.VMEM((total_rows, LANES), F4),
                pltpu.VMEM((n + 1, QB, QB), F4),
                pltpu.VMEM((2, n + 1, QB, QB), F4),
                pltpu.SemaphoreType.DMA((2,)),
            ],
            loose=(5,),
            ties=(hold(out_token, w_parts),),
        )
        unit_in = all_to_all(hold(stacked, res_in, out_parts_in))

    with scope("wg"):
        *unit_grad_parts, parts_token = call(
            functools.partial(unit_weight_grads, n, heads),
            (normed, stacked, lines, buckets),
            [shaped((width // heads + n + 8, 3 * LANES), BF)] * heads,
            [pltpu.VMEM((width, 3 * LANES), F4), pltpu.VMEM((NUM_BUCKETS, 3 * LANES), F4)],
        )
        unit_parts_in = exchange(unit_grad_parts, HEAD)
    with scope("res"):
        result, result_token = call(
            functools.partial(result_rows, n, cap),
            (res_in, target, hidden),
            [shaped((tok, width), BF)],
            ties=(parts_token,),
        )
    with scope("fw"):
        full_w, full_token = call(
            functools.partial(unpack_full, n, rows),
            w_parts,
            [shaped((width, 3 * width), BF)],
            [pltpu.VMEM((width, 3 * width), F4)],
            ties=(parts_token,),
        )
    with scope("wg"):
        *sums, sums_token = call(
            functools.partial(weight_sums, n, rows, heads),
            unit_parts_in + out_parts_in,
            [shaped((rows, 3 * LANES + wide), BF)] * n,
            [pltpu.VMEM((n, rows, 3 * LANES + wide), F4)],
            ties=(full_token, result_token),
        )
        sums_in = exchange(sums, BLK)
    with scope("ewg"):
        grad_in, grad_out, expert_token = expert_weights_call(
            experts,
            seq_lengths,
            (moe_far, far_pair),
            all_cot[2:],
            *expert_ends,
            (sums_token,),
            begun,
        )
    with scope("fin"):
        (
            grad_q,
            grad_k,
            grad_v,
            grad_gain_attn,
            grad_table,
            grad_out_w,
            grad_gain_moe,
            grad_router,
            grad_tokens,
            unused,
        ) = call(
            functools.partial(last_grads, n, experts),
            sums_in
            + [w_query, w_key, w_value, gain_a]
            + [unit_in, full_w, x, grad_hidden, misc_t],
            [shaped((rows, width), F4)] * 3
            + [
                shaped((1, rows), F4),
                shaped((1, HEADS), F4),
                shaped((rows, width), F4),
                shaped((1, rows), F4),
                shaped((experts, rows), F4),
                shaped(tokens.shape, F4),
            ],
            [
                pltpu.VMEM((n, rows, 3 * LANES), F4),
                pltpu.VMEM((n, 1, LANES), F4),
                pltpu.VMEM((3 * width, tok), BF),
            ],
            ties=(expert_token,),
        )
    return (
        result.reshape(tokens.shape),
        grad_tokens,
        grad_gain_attn.reshape(-1),
        grad_q,
        grad_k,
        grad_v,
        jnp.transpose(grad_out_w),
        grad_table.reshape(-1),
        grad_gain_moe.reshape(-1),
        jnp.transpose(grad_router),
        grad_in.reshape(expert_in.shape),
        grad_out.reshape(expert_out.shape),
    )


def ring_of(place, ring_len):
    return 2 * place if place < ring_len // 2 else 2 * ring_len - 1 - 2 * place


def solution(mesh):
    in_specs = (
        P(BLK, HEAD, None),
        P((HEAD, BLK)),
        P((HEAD, BLK), None),
        P((HEAD, BLK), None),
        P((HEAD, BLK), None),
        P(None, (HEAD, BLK)),
        P((HEAD, BLK)),
        P((HEAD, BLK)),
        P((HEAD, BLK), None),
        P(BLK, None, HEAD),
        P(BLK, HEAD, None),
        P(),
        P(),
        P(HEAD, BLK, None, None),
        P(BLK, HEAD, None),
    )
    out_specs = (
        P(BLK, HEAD, None),
        P(BLK, HEAD, None),
        P((HEAD, BLK)),
        P((HEAD, BLK), None),
        P((HEAD, BLK), None),
        P((HEAD, BLK), None),
        P(None, (HEAD, BLK)),
        P((HEAD, BLK)),
        P((HEAD, BLK)),
        P((HEAD, BLK), None),
        P(BLK, None, HEAD),
        P(BLK, HEAD, None),
    )
    one_each = mesh.shape[HEAD] == 4 and mesh.shape[BLK] == 8
    return jax.shard_map(
        on_plane if one_each else on_device, mesh=mesh, in_specs=in_specs, out_specs=out_specs, check_vma=False
    )
```

profile of v0, /device:TPU:8, one launch (start us, length us, event | category | flops | bytes accessed | tf_op | source)
XLA Modules:
  0.0 270.0 jit_solution(380014322206193037)
XLA Ops:
  6.0 7.0 %collective-permute-done.refs_1_ = bf16[256,768]{1,0:T(8,128)(2,1)S(1)} collective-permute-done((bf16[256,768]{1,0:T(8,128)(2,1)}, bf16[256,768]{1,0:T(8,128)(2,1)S(1)}, u32[]{:S(2)}, u32[]{:S(2)}) %collective-permute-start) | collective-permute-done | bytes 393248 | tf_op jit(solution)/shard_map/rin/ppermute | solution.py:1292
  16.3 5.3 %all-to-all-start = ((bf16[8,24,512]{2,1,0:T(8,128)(2,1)}), bf16[8,24,512]{2,1,0:T(8,128)(2,1)S(1)}, u32[]{:S(2)}, u32[]{:S(2)}) async-start(bf16[8,24,512]{2,1,0:T(8,128)(2,1)} %get-tuple-element.123), calls=%async_computation | async-start | bytes 393216 | tf_op jit(solution)/shard_map/uw/all_to_all | solution.py:1283
  21.6 2.7 cr.1
  32.2 4.7 %collective-permute-done.10.refs_2_ = bf16[8,24,512]{2,1,0:T(8,128)(2,1)S(1)} collective-permute-done((bf16[8,24,512]{2,1,0:T(8,128)(2,1)S(1)}, bf16[8,24,512]{2,1,0:T(8,128)(2,1)S(1)}, u32[]{:S(2)}, u32[]{:S(2)}) %collective-permute-start.10) | collective-permute-done | bytes 196640 | tf_op jit(solution)/shard_map/uw/ppermute | solution.py:1231
  43.0 2.5 uw.3
  47.6 4.8 %all-to-all-start.2 = ((bf16[8,72,768]{2,1,0:T(8,128)(2,1)}), bf16[8,72,768]{2,1,0:T(8,128)(2,1)}, u32[]{:S(2)}, u32[]{:S(2)}) async-start(bf16[8,72,768]{2,1,0:T(8,128)(2,1)} %get-tuple-element.135), calls=%async_computation.2 | async-start | bytes 1769472 | tf_op jit(solution)/shard_map/cr/all_to_all | solution.py:1283
  54.1 16.9 %att.1 = (bf16[8,64,384]{2,1,0:T(8,128)(2,1)}, f32[8,1,256]{2,1,0:T(1,128)}, f32[8,1,128]{2,1,0:T(1,128)}, bf16[8,256,768]{2,1,0:T(8,128)(2,1)}, bf16[2048,128]{...) custom-call(s32[4]{0:T(128)} %length_ref.33, ...), custom_call_target="tpu_custom_call" | custom-call | flops 1 | bytes 1 | tf_op jit(solution)/shard_map/att/pallas_call | solution.py:489
  71.0 6.1 %all-to-all-start.1 = ((bf16[8,64,384]{2,1,0:T(8,128)(2,1)}), bf16[8,64,384]{2,1,0:T(8,128)(2,1)S(1)}, u32[]{:S(2)}, u32[]{:S(2)}) async-start(bf16[8,64,384]{2,1,0:T(8,128)(2,1)} %get-tuple-element.133.refs_6_), calls=%async_computation.1 | async-start | bytes 786432 | tf_op jit(solution)/shard_map/att/all_to_all | solution.py:1283
  78.6 6.2 %collective-permute-done.13.refs_3_ = bf16[8,24,768]{2,1,0:T(8,128)(2,1)S(1)} collective-permute-done((bf16[8,24,768]{2,1,0:T(8,128)(2,1)S(1)}, bf16[8,24,768]{2,1,0:T(8,128)(2,1)S(1)}, u32[]{:S(2)}, u32[]{:S(2)}) %collective-permute-start.13) | collective-permute-done | bytes 294944 | tf_op jit(solution)/shard_map/ow/ppermute | solution.py:1231
  86.5 3.7 %hid.1 = (bf16[256,768]{1,0:T(8,128)(2,1)}, f32[256,768]{1,0:T(8,128)}, bf16[8,48,768]{2,1,0:T(8,128)(2,1)}, bf16[768,768]{1,0:T(8,128)(2,1)}, f32[8,128]{1,0:T(8,128)}) custom-call(s32[4]{0:T(128)} %length_ref.33, bf16[8,64,384]{2,1,0:T(8,128)(2,1)} %copy-done.12, bf16[8,24,768]{2,1,0:T(8,128)(2,1)} %copy-done.13, ...), custom_call_target="tpu_custom_call" | custom-call | flops 1 | bytes 1 | tf_op jit(solution)/shard_map/hid/pallas_call | solution.py:489
  90.3 6.5 %all-to-all-start.3 = ((bf16[8,48,768]{2,1,0:T(8,128)(2,1)}), bf16[8,48,768]{2,1,0:T(8,128)(2,1)S(1)}, u32[]{:S(2)}, u32[]{:S(2)}) async-start(bf16[8,48,768]{2,1,0:T(8,128)(2,1)} %get-tuple-element.142), calls=%async_computation.3 | async-start | bytes 1179648 | tf_op jit(solution)/shard_map/mr/all_to_all | solution.py:1283
  98.5 14.3 %collective-permute-done.16.refs_2_ = bf16[8,48,768]{2,1,0:T(8,128)(2,1)S(1)} collective-permute-done((bf16[8,48,768]{2,1,0:T(8,128)(2,1)S(1)}, bf16[8,48,768]{2,1,0:T(8,128)(2,1)S(1)}, u32[]{:S(2)}, u32[]{:S(2)}) %collective-permute-start.16) | collective-permute-done | bytes 589856 | tf_op jit(solution)/shard_map/cp/ppermute | solution.py:1231
  115.7 6.0 %all-to-all-start.4 = ((bf16[8,72,768]{2,1,0:T(8,128)(2,1)}), bf16[8,72,768]{2,1,0:T(8,128)(2,1)S(1)}, u32[]{:S(2)}, u32[]{:S(2)}) async-start(bf16[8,72,768]{2,1,0:T(8,128)(2,1)} %get-tuple-element.153), calls=%async_computation.4 | async-start | bytes 1769472 | tf_op jit(solution)/shard_map/fw/all_to_all | solution.py:1283
  121.7 8.5 %eb.2 = (bf16[384,768]{1,0:T(8,128)(2,1)}, bf16[384,768]{1,0:T(8,128)(2,1)}, bf16[384,128]{1,0:T(8,128)(2,1)}, f32[8,128]{1,0:T(8,128)}) custom-call(s32[4]{0:T(128)} %length_ref.33, bf16[8,48,768]{2,1,0:T(8,128)(2,1)} %copy-done.3, bf16[8,48,768]{2,1,0:T(8,128)(2,1)} %copy-done.8, bf16[768,768]{1,0:T(8,128)(2,1)} %bitcast.22, bf16[768,768]{1,0:T(8,128)(2,1)} %bitcast.26, ...), custom_call_target="tpu_custom_call" | custom-call | flops 1 | bytes 1 | tf_op jit(solution)/shard_map/eb/pallas_call | solution.py:489
  130.8 8.6 %eb.3 = (f32[384,768]{1,0:T(8,128)}, bf16[384,768]{1,0:T(8,128)(2,1)}, bf16[384,128]{1,0:T(8,128)(2,1)}, f32[8,128]{1,0:T(8,128)}) custom-call(s32[4]{0:T(128)} %length_ref.33, bf16[8,48,768]{2,1,0:T(8,128)(2,1)} %copy-done.1, bf16[8,48,768]{2,1,0:T(8,128)(2,1)} %copy-done.4, bf16[768,768]{1,0:T(8,128)(2,1)} %bitcast.23, bf16[768,768]{1,0:T(8,128)(2,1)} %bitcast.27, ...), custom_call_target="tpu_custom_call" | custom-call | flops 1 | bytes 1 | tf_op jit(solution)/shard_map/eb/pallas_call | solution.py:489
  142.3 5.7 %all-to-all-start.5 = ((bf16[8,48,768]{2,1,0:T(8,128)(2,1)}), bf16[8,48,768]{2,1,0:T(8,128)(2,1)S(1)}, u32[]{:S(2)}, u32[]{:S(2)}) async-start(bf16[8,48,768]{2,1,0:T(8,128)(2,1)} %bitcast.12), calls=%async_computation.5 | async-start | bytes 1179648 | tf_op jit(solution)/shard_map/eb/all_to_all | solution.py:1283
  150.0 9.3 %ewg.2 = (f32[768,768]{1,0:T(8,128)}, f32[768,768]{1,0:T(8,128)}, f32[8,128]{1,0:T(8,128)}) custom-call(s32[4]{0:T(128)} %length_ref.33, bf16[8,48,768]{2,1,0:T(8,128)(2,1)} %copy-done.1, bf16[8,48,768]{2,1,0:T(8,128)(2,1)} %copy-done.3, bf16[8,48,768]{2,1,0:T(8,128)(2,1)} %copy-done.4, bf16[8,48,768]{2,1,0:T(8,128)(2,1)} %copy-done.8, ...), custom_call_target="tpu_custom_call" | custom-call | flops 1 | bytes 1 | tf_op jit(solution)/shard_map/ewg/pallas_call | solution.py:970
  159.2 3.5 %all-to-all-done.5.refs_0_ = bf16[8,48,768]{2,1,0:T(8,128)(2,1)S(1)} async-done(((bf16[8,48,768]{2,1,0:T(8,128)(2,1)}), bf16[8,48,768]{2,1,0:T(8,128)(2,1)S(1)}, u32[]{:S(2)}, u32[]{:S(2)}) %all-to-all-start.5) | async-done | bytes 589856 | tf_op jit(solution)/shard_map/eb/all_to_all | solution.py:1283
  163.6 4.0 %hg.1 = (f32[256,768]{1,0:T(8,128)}, bf16[256,768]{1,0:T(8,128)(2,1)}, f32[8,768]{1,0:T(8,128)}, bf16[8,64,384]{2,1,0:T(8,128)(2,1)}, f32[8,128]{1,0:T(8,128)}) custom-call(s32[4]{0:T(128)} %length_ref.33, bf16[8,48,768]{2,1,0:T(8,128)(2,1)} %copy-done.10, s32[8,256]{1,0:T(8,128)} %get-tuple-element.138.refs_7_.refs_1_, ...), custom_call_target="tpu_custom_call" | custom-call | flops 1 | bytes 1 | tf_op jit(solution)/shard_map/hg/pallas_call | solution.py:489
  167.6 5.1 %all-to-all-start.6 = ((bf16[8,64,384]{2,1,0:T(8,128)(2,1)}), bf16[8,64,384]{2,1,0:T(8,128)(2,1)S(1)}, u32[]{:S(2)}, u32[]{:S(2)}) async-start(bf16[8,64,384]{2,1,0:T(8,128)(2,1)} %get-tuple-element.160), calls=%async_computation.6 | async-start | bytes 786432 | tf_op jit(solution)/shard_map/hg/all_to_all | solution.py:1283
  174.7 3.8 %owg.1 = (bf16[192,896]{1,0:T(8,128)(2,1)}, bf16[192,896]{1,0:T(8,128)(2,1)}, bf16[192,896]{1,0:T(8,128)(2,1)}, bf16[192,896]{1,0:T(8,128)(2,1)}, f32[8,128]{1,0:T(8,128)}) custom-call(s32[4]{0:T(128)} %length_ref.33, bf16[256,768]{1,0:T(8,128)(2,1)} %get-tuple-element.161.refs_0_, bf16[256,768]{1,0:T(8,128)(2,1)} %get-tuple-element.162.refs_1_, ...), custom_call_target="tpu_custom_call" | custom-call | flops 1 | bytes 1 | tf_op jit(solution)/shard_map/owg/pallas_call | solution.py:489
  178.5 5.0 %all-to-all-done.6.refs_7_ = bf16[8,64,384]{2,1,0:T(8,128)(2,1)S(1)} async-done(((bf16[8,64,384]{2,1,0:T(8,128)(2,1)}), bf16[8,64,384]{2,1,0:T(8,128)(2,1)S(1)}, u32[]{:S(2)}, u32[]{:S(2)}) %all-to-all-start.6) | async-done | bytes 393248 | tf_op jit(solution)/shard_map/hg/all_to_all | solution.py:1283
  183.4 4.9 %all-to-all-start.7 = ((bf16[8,48,768]{2,1,0:T(8,128)(2,1)}), bf16[8,48,768]{2,1,0:T(8,128)(2,1)S(1)}, u32[]{:S(2)}, u32[]{:S(2)}) async-start(bf16[8,48,768]{2,1,0:T(8,128)(2,1)} %bitcast.11), calls=%async_computation.7 | async-start | bytes 1179648 | tf_op jit(solution)/shard_map/rr/all_to_all | solution.py:1283
  193.6 16.5 %ag.1 = (bf16[8,352,256]{2,1,0:T(8,128)(2,1)}, f32[16,1,512]{2,1,0:T(1,128)}, f32[8,128]{1,0:T(8,128)}) custom-call(s32[4]{0:T(128)} %length_ref.33, bf16[2048,128]{1,0:T(8,128)(2,1)} %get-tuple-element.169.refs_0_, bf16[2048,128]{1,0:T(8,128)(2,1)} %get-tuple-element.170.refs_1_, bf16[128,2048]{1,0:T(8,128)(2,1)} %get-tuple-element.171.refs_2_, ...), custom_call_target="tpu_custom_call" | custom-call | flops 1 | bytes 1 | tf_op jit(solution)/shard_map/ag/pallas_call | solution.py:489
  211.2 6.2 %all-to-all-start.8 = ((bf16[8,352,256]{2,1,0:T(8,128)(2,1)}), bf16[8,352,256]{2,1,0:T(8,128)(2,1)S(1)}, u32[]{:S(2)}, u32[]{:S(2)}) async-start(bf16[8,352,256]{2,1,0:T(8,128)(2,1)} %get-tuple-element.200.refs_1_), calls=%async_computation.8 | async-start | bytes 2883584 | tf_op jit(solution)/shard_map/ag/all_to_all | solution.py:1283
  217.4 4.8 %wg.2 = (bf16[208,384]{1,0:T(8,128)(2,1)}, bf16[208,384]{1,0:T(8,128)(2,1)}, bf16[208,384]{1,0:T(8,128)(2,1)}, bf16[208,384]{1,0:T(8,128)(2,1)}, f32[8,128]{1,0:T(8,128)}) custom-call(s32[4]{0:T(128)} %length_ref.33, bf16[8,256,768]{2,1,0:T(8,128)(2,1)} %get-tuple-element.168.refs_0_, bf16[8,352,256]{2,1,0:T(8,128)(2,1)} %get-tuple-element.200.refs_1_, ...), custom_call_target="tpu_custom_call" | custom-call | flops 1 | bytes 1 | tf_op jit(solution)/shard_map/wg/pallas_call | solution.py:489
  224.1 4.7 %fw.1 = (bf16[768,2304]{1,0:T(8,128)(2,1)}, f32[8,128]{1,0:T(8,128)}) custom-call(s32[4]{0:T(128)} %length_ref.33, bf16[8,72,768]{2,1,0:T(8,128)(2,1)} %copy-done.7, bf16[8,72,768]{2,1,0:T(8,128)(2,1)} %copy-done.17, bf16[8,72,768]{2,1,0:T(8,128)(2,1)} %copy-done.16, bf16[8,72,768]{2,1,0:T(8,128)(2,1)} %copy-done.18, f32[8,128]{1,0:T(8,128)} %get-tuple-element.180.refs_3_.refs_4_), custom_call_target="tpu_custom_call" | custom-call | flops 1 | bytes 1 | tf_op jit(solution)/shard_map/fw/pallas_call | solution.py:489
  228.7 2.5 res.1
  232.6 2.8 %wg.3 = (bf16[24,1280]{1,0:T(8,128)(2,1)}, bf16[24,1280]{1,0:T(8,128)(2,1)}, bf16[24,1280]{1,0:T(8,128)(2,1)}, bf16[24,1280]{1,0:T(8,128)(2,1)}, bf16[24,1280]{1...) custom-call(s32[4]{0:T(128)} %length_ref.33, ...), custom_call_target="tpu_custom_call" | custom-call | flops 1 | bytes 1 | tf_op jit(solution)/shard_map/wg/pallas_call | solution.py:489
  244.7 2.9 %collective-permute-start.39 = (bf16[24,1280]{1,0:T(8,128)(2,1)}, bf16[24,1280]{1,0:T(8,128)(2,1)S(1)}, u32[]{:S(2)}, u32[]{:S(2)}) collective-permute-start(bf16[24,1280]{1,0:T(8,128)(2,1)} %get-tuple-element.199), channel_id=1, source_target_pairs={{0,7},{1,6},{2,5},{3,4},{4,3},{5,2},{6,1},{7,0},{8,15},{9,14},{10,... | collective-permute-start | bytes 184328 | tf_op jit(solution)/shard_map/wg/ppermute | solution.py:1231
  247.6 10.2 %ewg.3 = (f32[768,768]{1,0:T(8,128)}, f32[768,768]{1,0:T(8,128)}, f32[8,128]{1,0:T(8,128)}) custom-call(s32[4]{0:T(128)} %length_ref.33, bf16[8,48,768]{2,1,0:T(8,128)(2,1)} %collective-permute-done.21.refs_0_, bf16[8,48,768]{2,1,0:T(8,128)(2,1)} %collective-permute-done.22.refs_1_, bf16[8,48,768]{2,1,0:T(8,128)(2,1)} %copy-done.20, ...), custom_call_target="tpu_custom_call" | custom-call | flops 1 | bytes 1 | tf_op jit(solution)/shard_map/ewg/pallas_call | solution.py:970
  262.9 6.8 %fin.1 = (f32[24,768]{1,0:T(8,128)}, f32[24,768]{1,0:T(8,128)}, f32[24,768]{1,0:T(8,128)}, f32[1,24]{1,0:T(1,128)}, f32[1,12]{1,0:T(1,128)}, /*index=5*/f32[24,7...) custom-call(s32[4]{0:T(128)} %length_ref.33, ...), custom_call_target="tpu_custom_call" | custom-call | flops 1 | bytes 1 | tf_op jit(solution)/shard_map/fin/pallas_call | solution.py:489
  (175 shorter events, 66.3 us)
Async XLA Ops:
  0.6 28.4 %collective-permute-start.4 = (bf16[768,768]{1,0:T(8,128)(2,1)}, bf16[768,768]{1,0:T(8,128)(2,1)S(1)}, u32[]{:S(2)}, u32[]{:S(2)}) collective-permute-start(bf16[768,768]{1,0:T(8,128)(2,1)} %bitcast.21), channel_id=1, source_target_pairs={{0,16},{8,24},{16,0},{24,8},{1,17},{9,25},{17,1},{25,9},{2,18},{10... | collective-permute-start | bytes 3538952 | tf_op jit(solution)/shard_map/es/ppermute | solution.py:1231
  2.2 10.8 %collective-permute-start = (bf16[256,768]{1,0:T(8,128)(2,1)}, bf16[256,768]{1,0:T(8,128)(2,1)S(1)}, u32[]{:S(2)}, u32[]{:S(2)}) collective-permute-start(bf16[256,768]{1,0:T(8,128)(2,1)} %bitcast.31), channel_id=1, source_target_pairs={{0,2},{2,4},{4,6},{6,7},{7,5},{5,3},{3,1},{1,0},{8,10},{10,12},{12... | collective-permute-start | bytes 1179656 | tf_op jit(solution)/shard_map/rin/ppermute | solution.py:1292
  3.8 10.5 %collective-permute-start.1 = (bf16[256,768]{1,0:T(8,128)(2,1)}, bf16[256,768]{1,0:T(8,128)(2,1)S(1)}, u32[]{:S(2)}, u32[]{:S(2)}) collective-permute-start(bf16[256,768]{1,0:T(8,128)(2,1)} %bitcast.32), channel_id=1, source_target_pairs={{2,0},{4,2},{6,4},{7,6},{5,7},{3,5},{1,3},{0,1},{10,8},{12,10},{14... | collective-permute-start | bytes 1179656 | tf_op jit(solution)/shard_map/rin/ppermute | solution.py:1293
  14.3 11.1 %collective-permute-start.2 = (bf16[256,768]{1,0:T(8,128)(2,1)S(1)}, bf16[256,768]{1,0:T(8,128)(2,1)S(1)}, u32[]{:S(2)}, u32[]{:S(2)}) collective-permute-start(bf16[256,768]{1,0:T(8,128)(2,1)S(1)} %collective-permute-done.refs_1_), channel_id=1, source_target_pairs={{0,2},{2,4},{4,6},{6,7},{7,5},{5,3},{3,1},{1,0},{8,10},{10,12},{12... | collective-permute-start | bytes 1179656 | tf_op jit(solution)/shard_map/rin/ppermute | solution.py:1292
  15.9 11.2 %collective-permute-start.3 = (bf16[256,768]{1,0:T(8,128)(2,1)S(1)}, bf16[256,768]{1,0:T(8,128)(2,1)S(1)}, u32[]{:S(2)}, u32[]{:S(2)}) collective-permute-start(bf16[256,768]{1,0:T(8,128)(2,1)S(1)} %collective-permute-done.1.refs_2_), channel_id=1, source_target_pairs={{2,0},{4,2},{6,4},{7,6},{5,7},{3,5},{1,3},{0,1},{10,8},{12,10},{14... | collective-permute-start | bytes 1179656 | tf_op jit(solution)/shard_map/rin/ppermute | solution.py:1293
  16.3 12.8 %all-to-all-start = ((bf16[8,24,512]{2,1,0:T(8,128)(2,1)}), bf16[8,24,512]{2,1,0:T(8,128)(2,1)S(1)}, u32[]{:S(2)}, u32[]{:S(2)}) async-start(bf16[8,24,512]{2,1,0:T(8,128)(2,1)} %get-tuple-element.123), calls=%async_computation | async-start | bytes 393216 | tf_op jit(solution)/shard_map/uw/all_to_all | solution.py:1283
  30.2 9.9 %collective-permute-start.6 = (bf16[256,768]{1,0:T(8,128)(2,1)}, bf16[256,768]{1,0:T(8,128)(2,1)S(1)}, u32[]{:S(2)}, u32[]{:S(2)}) collective-permute-start(bf16[256,768]{1,0:T(8,128)(2,1)} %copy-done.26), channel_id=1, source_target_pairs={{2,0},{4,2},{6,4},{7,6},{5,7},{3,5},{1,3},{0,1},{10,8},{12,10},{14... | collective-permute-start | bytes 1179656 | tf_op jit(solution)/shard_map/rin/ppermute | solution.py:1293
  32.2 10.2 %collective-permute-start.9 = (bf16[8,24,512]{2,1,0:T(8,128)(2,1)S(1)}, bf16[8,24,512]{2,1,0:T(8,128)(2,1)S(1)}, u32[]{:S(2)}, u32[]{:S(2)}) collective-permute-start(bf16[8,24,512]{2,1,0:T(8,128)(2,1)S(1)} %all-to-all-done.refs_0_), channel_id=1, source_target_pairs={{0,8},{8,0},{16,24},{24,16},{1,9},{9,1},{17,25},{25,17},{2,10},{10... | collective-permute-start | bytes 589832 | tf_op jit(solution)/shard_map/uw/ppermute | solution.py:1231
  47.6 23.3 %all-to-all-start.2 = ((bf16[8,72,768]{2,1,0:T(8,128)(2,1)}), bf16[8,72,768]{2,1,0:T(8,128)(2,1)}, u32[]{:S(2)}, u32[]{:S(2)}) async-start(bf16[8,72,768]{2,1,0:T(8,128)(2,1)} %get-tuple-element.135), calls=%async_computation.2 | async-start | bytes 1769472 | tf_op jit(solution)/shard_map/cr/all_to_all | solution.py:1283
  52.5 32.3 %collective-permute-start.15 = (bf16[768,768]{1,0:T(8,128)(2,1)S(1)}, bf16[768,768]{1,0:T(8,128)(2,1)S(1)}, u32[]{:S(2)}, u32[]{:S(2)}) collective-permute-start(bf16[768,768]{1,0:T(8,128)(2,1)S(1)} %bitcast.30), channel_id=1, source_target_pairs={{0,16},{8,24},{16,0},{24,8},{1,17},{9,25},{17,1},{25,9},{2,18},{10... | collective-permute-start | bytes 3538952 | tf_op jit(solution)/shard_map/es/ppermute | solution.py:1231
  71.0 13.9 %all-to-all-start.1 = ((bf16[8,64,384]{2,1,0:T(8,128)(2,1)}), bf16[8,64,384]{2,1,0:T(8,128)(2,1)S(1)}, u32[]{:S(2)}, u32[]{:S(2)}) async-start(bf16[8,64,384]{2,1,0:T(8,128)(2,1)} %get-tuple-element.133.refs_6_), calls=%async_computation.1 | async-start | bytes 786432 | tf_op jit(solution)/shard_map/att/all_to_all | solution.py:1283
  90.3 23.3 %all-to-all-start.3 = ((bf16[8,48,768]{2,1,0:T(8,128)(2,1)}), bf16[8,48,768]{2,1,0:T(8,128)(2,1)S(1)}, u32[]{:S(2)}, u32[]{:S(2)}) async-start(bf16[8,48,768]{2,1,0:T(8,128)(2,1)} %get-tuple-element.142), calls=%async_computation.3 | async-start | bytes 1179648 | tf_op jit(solution)/shard_map/mr/all_to_all | solution.py:1283
  97.9 14.9 %collective-permute-start.16 = (bf16[8,48,768]{2,1,0:T(8,128)(2,1)S(1)}, bf16[8,48,768]{2,1,0:T(8,128)(2,1)S(1)}, u32[]{:S(2)}, u32[]{:S(2)}) collective-permute-start(bf16[8,48,768]{2,1,0:T(8,128)(2,1)S(1)} %slice.17.refs_1_.refs_2_), channel_id=1, source_target_pairs={{0,16},{8,24},{16,0},{24,8},{1,17},{9,25},{17,1},{25,9},{2,18},{10... | collective-permute-start | bytes 1769480 | tf_op jit(solution)/shard_map/cp/ppermute | solution.py:1231
  98.5 15.1 %collective-permute-start.17 = (bf16[8,48,768]{2,1,0:T(8,128)(2,1)S(1)}, bf16[8,48,768]{2,1,0:T(8,128)(2,1)S(1)}, u32[]{:S(2)}, u32[]{:S(2)}) collective-permute-start(bf16[8,48,768]{2,1,0:T(8,128)(2,1)S(1)} %slice.17.refs_1_.refs_2_), channel_id=1, source_target_pairs={{0,8},{8,0},{16,24},{24,16},{1,9},{9,1},{17,25},{25,17},{2,10},{10... | collective-permute-start | bytes 1769480 | tf_op jit(solution)/shard_map/cp/ppermute | solution.py:1231
  115.7 26.6 %all-to-all-start.4 = ((bf16[8,72,768]{2,1,0:T(8,128)(2,1)}), bf16[8,72,768]{2,1,0:T(8,128)(2,1)S(1)}, u32[]{:S(2)}, u32[]{:S(2)}) async-start(bf16[8,72,768]{2,1,0:T(8,128)(2,1)} %get-tuple-element.153), calls=%async_computation.4 | async-start | bytes 1769472 | tf_op jit(solution)/shard_map/fw/all_to_all | solution.py:1283
  130.2 17.8 %collective-permute-start.21 = (bf16[8,48,768]{2,1,0:T(8,128)(2,1)S(1)}, bf16[8,48,768]{2,1,0:T(8,128)(2,1)}, u32[]{:S(2)}, u32[]{:S(2)}) collective-permute-start(bf16[8,48,768]{2,1,0:T(8,128)(2,1)S(1)} %all-to-all-done.3.refs_0_.refs_2_), channel_id=1, source_target_pairs={{0,16},{8,24},{16,0},{24,8},{1,17},{9,25},{17,1},{25,9},{2,18},{10... | collective-permute-start | bytes 1769480 | tf_op jit(solution)/shard_map/mf/ppermute | solution.py:1231
  142.3 20.5 %all-to-all-start.5 = ((bf16[8,48,768]{2,1,0:T(8,128)(2,1)}), bf16[8,48,768]{2,1,0:T(8,128)(2,1)S(1)}, u32[]{:S(2)}, u32[]{:S(2)}) async-start(bf16[8,48,768]{2,1,0:T(8,128)(2,1)} %bitcast.12), calls=%async_computation.5 | async-start | bytes 1179648 | tf_op jit(solution)/shard_map/eb/all_to_all | solution.py:1283
  148.0 11.2 %collective-permute-start.23 = (bf16[8,48,768]{2,1,0:T(8,128)(2,1)S(1)}, bf16[8,48,768]{2,1,0:T(8,128)(2,1)}, u32[]{:S(2)}, u32[]{:S(2)}) collective-permute-start(bf16[8,48,768]{2,1,0:T(8,128)(2,1)S(1)} %copy-done.21), channel_id=1, source_target_pairs={{0,8},{8,0},{16,24},{24,16},{1,9},{9,1},{17,25},{25,17},{2,10},{10... | collective-permute-start | bytes 1769480 | tf_op jit(solution)/shard_map/cp/ppermute | solution.py:1231
  148.0 11.2 %collective-permute-start.22 = (bf16[8,48,768]{2,1,0:T(8,128)(2,1)}, bf16[8,48,768]{2,1,0:T(8,128)(2,1)}, u32[]{:S(2)}, u32[]{:S(2)}) collective-permute-start(bf16[8,48,768]{2,1,0:T(8,128)(2,1)} %collective-permute-done.21.refs_0_), channel_id=1, source_target_pairs={{0,8},{8,0},{16,24},{24,16},{1,9},{9,1},{17,25},{25,17},{2,10},{10... | collective-permute-start | bytes 1769480 | tf_op jit(solution)/shard_map/mf/ppermute | solution.py:1231
  148.5 24.2 %collective-permute-start.19 = (bf16[384,768]{1,0:T(8,128)(2,1)}, bf16[384,768]{1,0:T(8,128)(2,1)}, u32[]{:S(2)}, u32[]{:S(2)}) collective-permute-start(bf16[384,768]{1,0:T(8,128)(2,1)} %get-tuple-element.148), channel_id=1, source_target_pairs={{0,8},{8,0},{16,24},{24,16},{1,9},{9,1},{17,25},{25,17},{2,10},{10... | collective-permute-start | bytes 1769480 | tf_op jit(solution)/shard_map/rr/ppermute | solution.py:1231
  148.6 39.9 %collective-permute-start.25 = (bf16[8,72,768]{2,1,0:T(8,128)(2,1)S(1)}, bf16[8,72,768]{2,1,0:T(8,128)(2,1)S(1)}, u32[]{:S(2)}, u32[]{:S(2)}) collective-permute-start(bf16[8,72,768]{2,1,0:T(8,128)(2,1)S(1)} %all-to-all-done.4.refs_0_), channel_id=1, source_target_pairs={{0,16},{8,24},{16,0},{24,8},{1,17},{9,25},{17,1},{25,9},{2,18},{10... | collective-permute-start | bytes 2654216 | tf_op jit(solution)/shard_map/fw/ppermute | solution.py:1231
  167.6 15.9 %all-to-all-start.6 = ((bf16[8,64,384]{2,1,0:T(8,128)(2,1)}), bf16[8,64,384]{2,1,0:T(8,128)(2,1)S(1)}, u32[]{:S(2)}, u32[]{:S(2)}) async-start(bf16[8,64,384]{2,1,0:T(8,128)(2,1)} %get-tuple-element.160), calls=%async_computation.6 | async-start | bytes 786432 | tf_op jit(solution)/shard_map/hg/all_to_all | solution.py:1283
  183.4 26.8 %all-to-all-start.7 = ((bf16[8,48,768]{2,1,0:T(8,128)(2,1)}), bf16[8,48,768]{2,1,0:T(8,128)(2,1)S(1)}, u32[]{:S(2)}, u32[]{:S(2)}) async-start(bf16[8,48,768]{2,1,0:T(8,128)(2,1)} %bitcast.11), calls=%async_computation.7 | async-start | bytes 1179648 | tf_op jit(solution)/shard_map/rr/all_to_all | solution.py:1283
  189.0 21.2 %collective-permute-start.30 = (bf16[192,896]{1,0:T(8,128)(2,1)}, bf16[192,896]{1,0:T(8,128)(2,1)S(1)}, u32[]{:S(2)}, u32[]{:S(2)}) collective-permute-start(bf16[192,896]{1,0:T(8,128)(2,1)} %get-tuple-element.187), channel_id=1, source_target_pairs={{0,8},{8,0},{16,24},{24,16},{1,9},{9,1},{17,25},{25,17},{2,10},{10... | collective-permute-start | bytes 1032200 | tf_op jit(solution)/shard_map/owg/ppermute | solution.py:1231
  189.1 21.1 %collective-permute-start.31 = (bf16[192,896]{1,0:T(8,128)(2,1)}, bf16[192,896]{1,0:T(8,128)(2,1)S(1)}, u32[]{:S(2)}, u32[]{:S(2)}) collective-permute-start(bf16[192,896]{1,0:T(8,128)(2,1)} %get-tuple-element.188), channel_id=1, source_target_pairs={{0,16},{8,24},{16,0},{24,8},{1,17},{9,25},{17,1},{25,9},{2,18},{10... | collective-permute-start | bytes 1032200 | tf_op jit(solution)/shard_map/owg/ppermute | solution.py:1231
  190.6 19.6 %collective-permute-start.32 = (bf16[192,896]{1,0:T(8,128)(2,1)}, bf16[192,896]{1,0:T(8,128)(2,1)}, u32[]{:S(2)}, u32[]{:S(2)}) collective-permute-start(bf16[192,896]{1,0:T(8,128)(2,1)} %get-tuple-element.189), channel_id=1, source_target_pairs={{0,24},{8,16},{16,8},{24,0},{1,25},{9,17},{17,9},{25,1},{2,26},{10... | collective-permute-start | bytes 1032200 | tf_op jit(solution)/shard_map/owg/ppermute | solution.py:1231
  211.2 50.6 %all-to-all-start.8 = ((bf16[8,352,256]{2,1,0:T(8,128)(2,1)}), bf16[8,352,256]{2,1,0:T(8,128)(2,1)S(1)}, u32[]{:S(2)}, u32[]{:S(2)}) async-start(bf16[8,352,256]{2,1,0:T(8,128)(2,1)} %get-tuple-element.200.refs_1_), calls=%async_computation.8 | async-start | bytes 2883584 | tf_op jit(solution)/shard_map/ag/all_to_all | solution.py:1283
  237.5 20.3 %collective-permute-start.35 = (bf16[24,1280]{1,0:T(8,128)(2,1)}, bf16[24,1280]{1,0:T(8,128)(2,1)S(1)}, u32[]{:S(2)}, u32[]{:S(2)}) collective-permute-start(bf16[24,1280]{1,0:T(8,128)(2,1)} %get-tuple-element.195), channel_id=1, source_target_pairs={{0,3},{1,2},{2,1},{3,0},{4,7},{5,6},{6,5},{7,4},{8,11},{9,10},{10,... | collective-permute-start | bytes 184328 | tf_op jit(solution)/shard_map/wg/ppermute | solution.py:1231
  239.0 18.8 %collective-permute-start.36 = (bf16[24,1280]{1,0:T(8,128)(2,1)}, bf16[24,1280]{1,0:T(8,128)(2,1)S(1)}, u32[]{:S(2)}, u32[]{:S(2)}) collective-permute-start(bf16[24,1280]{1,0:T(8,128)(2,1)} %get-tuple-element.196), channel_id=1, source_target_pairs={{0,4},{1,5},{2,6},{3,7},{4,0},{5,1},{6,2},{7,3},{8,12},{9,13},{10,... | collective-permute-start | bytes 184328 | tf_op jit(solution)/shard_map/wg/ppermute | solution.py:1231
  241.3 16.5 %collective-permute-start.37 = (bf16[24,1280]{1,0:T(8,128)(2,1)}, bf16[24,1280]{1,0:T(8,128)(2,1)S(1)}, u32[]{:S(2)}, u32[]{:S(2)}) collective-permute-start(bf16[24,1280]{1,0:T(8,128)(2,1)} %get-tuple-element.197), channel_id=1, source_target_pairs={{0,5},{1,4},{2,7},{3,6},{4,1},{5,0},{6,3},{7,2},{8,13},{9,12},{10,... | collective-permute-start | bytes 184328 | tf_op jit(solution)/shard_map/wg/ppermute | solution.py:1231
  242.8 17.5 %collective-permute-start.38 = (bf16[24,1280]{1,0:T(8,128)(2,1)}, bf16[24,1280]{1,0:T(8,128)(2,1)S(1)}, u32[]{:S(2)}, u32[]{:S(2)}) collective-permute-start(bf16[24,1280]{1,0:T(8,128)(2,1)} %get-tuple-element.198), channel_id=1, source_target_pairs={{0,6},{1,7},{2,4},{3,5},{4,2},{5,3},{6,0},{7,1},{8,14},{9,15},{10,... | collective-permute-start | bytes 184328 | tf_op jit(solution)/shard_map/wg/ppermute | solution.py:1231
  244.7 17.1 %collective-permute-start.39 = (bf16[24,1280]{1,0:T(8,128)(2,1)}, bf16[24,1280]{1,0:T(8,128)(2,1)S(1)}, u32[]{:S(2)}, u32[]{:S(2)}) collective-permute-start(bf16[24,1280]{1,0:T(8,128)(2,1)} %get-tuple-element.199), channel_id=1, source_target_pairs={{0,7},{1,6},{2,5},{3,4},{4,3},{5,2},{6,1},{7,0},{8,15},{9,14},{10,... | collective-permute-start | bytes 184328 | tf_op jit(solution)/shard_map/wg/ppermute | solution.py:1231
  (60 other events, 478.0 us)
where the time goes:
time: 275 us; the launch traced here: 270 us
  Pallas kernels  110 us (40%)
  starting transfers between devices  82.8 us (30%)
  waiting for transfers between devices  63.3 us (23%)
  local copies, waits for them, and re-layouts  8.33 us (3%)
  other arithmetic  4.28 us (2%)
    pallas_call x15, Pallas kernels, vmem_call(): pl.pallas_call(kernel, out_shape=tuple(outs) + (shaped((8, LANES), F4),),...  90.4 us
    all_to_all x9, starting transfers between devices, all_to_all(): return lax.all_to_all(stack, axis, split_axis=0, concat_axis=0, tiled=True)  50.6 us
    ppermute x32, waiting for transfers between devices, swap(): return lax.ppermute(values, axis, [(i, i ^ flip) for i in range(size)])  35.7 us
    ppermute x32, starting transfers between devices, swap(): return lax.ppermute(values, axis, [(i, i ^ flip) for i in range(size)])  24 us
    pallas_call x2, Pallas kernels, expert_weights_call(): pl.pallas_call(kernel, grid=(steps,), out_shape=(shaped((depth, hidden),...  19.4 us
    all_to_all x9, waiting for transfers between devices, all_to_all(): return lax.all_to_all(stack, axis, split_axis=0, concat_axis=0, tiled=True)  11 us
    ppermute x3, waiting for transfers between devices, hop(): front = lax.ppermute(front, BLK, ahead)  9.96 us
    unnamed x86, local copies, waits for them, and re-layouts  6.21 us
  transfers between devices with their start and end apart: 49, of which 22 were waited for; matrix products, arithmetic and copies ran while one was open for 2% of the time, Pallas kernels for 37%

commit v1 on v0

--- a/solution.py
+++ b/solution.py
@@ -900,15 +900,14 @@
     return jnp.concatenate([ref[j][0:cap] for j in range(ref.shape[0])], axis=0)
 
 
-def expert_back(
-    experts, sc, rows_ref, cot_ref, in_a, out_a, in_b, out_b, misc, back, made, log_out
-):
+def expert_back(experts, sc, rows_ref, cot_ref, *refs):
+    ins, outs, (misc, back, made, log_out) = refs[0:4], refs[4:8], refs[8:12]
     rows, cots = flat_rows(rows_ref), flat_rows(cot_ref, rows_ref.shape[1])
     probs, chosen, gate = route_probs(experts, sc, rows, misc)
     inner = jnp.zeros(gate.shape, F4)
     total = jnp.zeros(rows.shape, F4)
     result = jnp.zeros(rows.shape, F4)
-    for w_in, w_out in ((in_a, out_a), (in_b, out_b)):
+    for w_in, w_out in zip(ins, outs):
         act, slope = gelu_pair(dot(rows, w_in[...]))
         low = act.astype(BF)
         result = result + dot(low, w_out[...])
@@ -917,8 +916,12 @@
         total = total + dot((gate * grad_act * slope).astype(BF), w_in[...], 1, 1)
     grad_logits = (inner * probs * (jnp.where(chosen, 1.0, 0.0) - gate)).astype(BF)
     log_out[...] = grad_logits
-    made[...] = (gate * result).astype(made.dtype)
-    back[...] = (total + dot(grad_logits, misc[...], 1, 1)).astype(back.dtype)
+    total = (total + dot(grad_logits, misc[...], 1, 1)).astype(BF)
+    result = (gate * result).astype(BF)
+    cap = made.shape[1]
+    for j in range(made.shape[0]):
+        back[j] = total[j * cap : (j + 1) * cap]
+        made[j] = result[j * cap : (j + 1) * cap]
 
 
 def expert_weights(experts, count, more, sc, *refs):
@@ -1205,11 +1208,11 @@
     router[...] = jnp.transpose(pltpu.roll(extra, LANES - 2, 1))[0:experts]
 
 
-def out_weight_grads(heads, sc, low, attn, rows_a, rows_b, logs_a, logs_b, gain, *rest):
+def out_weight_grads(heads, sc, low, attn, rows, logs, gain, *rest):
     outs, buf = rest[:heads], rest[heads]
     width = attn.shape[1]
     buf[:, 0:width] = dot(low[...], attn[...], 0, 0)
-    router = dot(flat_rows(rows_a), logs_a[...], 0, 0) + dot(flat_rows(rows_b), logs_b[...], 0, 0)
+    router = dot(flat_rows(rows), logs[...], 0, 0)
     wide = jnp.where(iota((LANES, gain.shape[1]), 0) == 1, gain[0:1, :], 0.0)
     buf[:, width : width + LANES] = two_parts(router + jnp.transpose(wide), 16)
     rows = buf.shape[0] // heads
@@ -1318,10 +1321,10 @@
     second = hop(*hold(first, packed_token))
     with scope("uw"):
         unit_parts = over_heads(hold(unit_in, second[0]))
-    third = hop(*hold(second, unit_in, in_other, cot_token))
+    third = hop(*hold(second, unit_in, cot_token))
     half = tok // 2
     with scope("rin"):
-        front_half, back_half = (third[0][:half], third[1][half:])
+        front_half, back_half = hold((third[0][:half], third[1][half:]), in_other)
         front, back = lax.ppermute(front_half, BLK, ahead), lax.ppermute(back_half, BLK, astern)
     with scope("uw"):
         unit_w, misc, misc_t, table, unused = call(
@@ -1408,6 +1411,9 @@
     with scope("mr"):
         moe_rows = all_to_all(moe_out)
         moe_pair = swap(hold(moe_rows, all_cot[2], cot_pair), HEAD, 1)
+    with scope("ec"):
+        ins = (in_own, in_other, swap(in_own, HEAD, 1), swap(in_other, HEAD, 1))
+        outs = (out_own, out_other, swap(out_own, HEAD, 1), swap(out_other, HEAD, 1))
     def backward_rows(rows_in, cots_in, kind, ties=()):
         return call(
             functools.partial(expert_back, experts),
@@ -1421,20 +1427,22 @@
         )
 
     with scope("fw"):
-        w_in = all_to_all(hold(w_stack, moe_pair))
+        w_in = all_to_all(hold(w_stack, moe_rows, ins[2:], outs[2:], all_cot[2]))
     with scope("mf"):
         moe_far = swap(moe_rows, HEAD, 2)
         far_pair = swap(moe_far, HEAD, 1)
 
     with scope("eb"):
-        back_pair, made_pair, logs_pair, token = backward_rows(moe_pair, cot_pair, BF)
-        back_other = swap(back_pair, HEAD, 1)
-        back_own, made_own, logs_own2, token = backward_rows(
-            moe_rows, cot_rows, F4, (token,)
-        )
-        back_out = (back_own + back_other.astype(F4)).astype(BF).reshape(n, cap, width)
-        back_out, back_token = hold((back_out, token), w_in)
-        back_in = all_to_all(back_out)
+        back_out, res_out, logs, back_token = call(
+            functools.partial(expert_back, experts),
+            (moe_rows, cot_rows) + ins + outs + (misc,),
+            [
+                shaped((n, cap, width), BF),
+                shaped((n, cap, width), BF),
+                shaped((slots, LANES), BF),
+            ],
+        )
+        back_in = all_to_all(hold(back_out, w_in))
     with scope("fw"):
         w_parts = over_heads(hold(w_in, back_token))
     with scope("ewg"):
@@ -1465,14 +1473,12 @@
     with scope("owg"):
         *out_parts, out_token = call(
             functools.partial(out_weight_grads, heads),
-            (grad_low, attn, moe_rows, moe_pair, logs_own2, logs_pair, gain_moe_part),
+            (grad_low, attn, moe_rows, logs, gain_moe_part),
             [shaped((width // heads, wide), BF)] * heads,
             [pltpu.VMEM((width, wide), F4)],
         )
         out_parts_in = exchange(out_parts, HEAD)
     with scope("rr"):
-        res_out = made_own.astype(F4) + swap(made_pair, HEAD, 1).astype(F4)
-        res_out = res_out.astype(BF).reshape(n, cap, width)
         res_in = all_to_all(hold(res_out, grad_heads, out_token))
 
     with scope("ag"):

time: 275 us -> 270 us (0.982)
  starting transfers between devices: 82.8 us -> 87.1 us
  other arithmetic: 4.28 us -> 0 us
  Pallas kernels: 110 us -> 106 us
    all_to_all x9, waiting for transfers between devices: 11 us -> 17.9 us  [all_to_all(): return lax.all_to_all(stack, axis, split_axis=0, concat_axis=0, tiled=True)]
    ppermute x32 -> x34, waiting for transfers between devices: 35.7 us -> 31.2 us  [swap(): return lax.ppermute(values, axis, [(i, i ^ flip) for i in range(size)])]
    ppermute x32 -> x34, starting transfers between devices: 24 us -> 28.3 us  [swap(): return lax.ppermute(values, axis, [(i, i ^ flip) for i in range(size)])]
    convert_element_type x2 -> x0, other arithmetic: 4.28 us -> none  [the longest x1 2.26 us: on_plane(): (back_own + back_other.astype(F4)).astype(BF).reshape(n, cap, width)]
    pallas_call x15 -> x14, Pallas kernels: 90.4 us -> 86.9 us  [vmem_call(): pl.pallas_call(kernel, out_shape=tuple(outs) + (shaped((8, LANES), F4),),...]
    unnamed x86 -> x80, local copies, waits for them, and re-layouts: 6.21 us -> 8.16 us
  transfers between devices with their start and end apart: 49 -> 51, of which waited for: 22 -> 23; matrix products, arithmetic and copies ran while one was open for 2% -> 0% of each run, Pallas kernels for 37% -> 37%
where the time goes in v1:
time: 270 us; the launch traced here: 266 us
  Pallas kernels  106 us (39%)
  starting transfers between devices  87.1 us (32%)
  waiting for transfers between devices  61.6 us (23%)
  local copies, waits for them, and re-layouts  9.31 us (3%)
    pallas_call x14, Pallas kernels, vmem_call(): pl.pallas_call(kernel, out_shape=tuple(outs) + (shaped((8, LANES), F4),),...  86.9 us
    all_to_all x9, starting transfers between devices, all_to_all(): return lax.all_to_all(stack, axis, split_axis=0, concat_axis=0, tiled=True)  50.6 us
    ppermute x34, waiting for transfers between devices, swap(): return lax.ppermute(values, axis, [(i, i ^ flip) for i in range(size)])  31.2 us
    ppermute x34, starting transfers between devices, swap(): return lax.ppermute(values, axis, [(i, i ^ flip) for i in range(size)])  28.3 us
    pallas_call x2, Pallas kernels, expert_weights_call(): pl.pallas_call(kernel, grid=(steps,), out_shape=(shaped((depth, hidden),...  19.5 us
    all_to_all x9, waiting for transfers between devices, all_to_all(): return lax.all_to_all(stack, axis, split_axis=0, concat_axis=0, tiled=True)  17.9 us
    unnamed x80, local copies, waits for them, and re-layouts  8.16 us
    ppermute x3, waiting for transfers between devices, hop(): front = lax.ppermute(front, BLK, ahead)  8.03 us
  transfers between devices with their start and end apart: 51, of which 23 were waited for; matrix products, arithmetic and copies ran while one was open for 0% of the time, Pallas kernels for 37%

profile of v1, /device:TPU:8, one launch (start us, length us, event | category | flops | bytes accessed | tf_op | source)
XLA Modules:
  0.0 265.7 jit_solution(13674200425126302875)
XLA Ops:
  5.9 5.8 %collective-permute-done.refs_1_ = bf16[256,768]{1,0:T(8,128)(2,1)S(1)} collective-permute-done((bf16[256,768]{1,0:T(8,128)(2,1)}, bf16[256,768]{1,0:T(8,128)(2,1)S(1)}, u32[]{:S(2)}, u32[]{:S(2)}) %collective-permute-start) | collective-permute-done | bytes 393248 | tf_op jit(solution)/shard_map/rin/ppermute | solution.py:1295
  15.1 5.3 %all-to-all-start = ((bf16[8,24,512]{2,1,0:T(8,128)(2,1)}), bf16[8,24,512]{2,1,0:T(8,128)(2,1)S(1)}, u32[]{:S(2)}, u32[]{:S(2)}) async-start(bf16[8,24,512]{2,1,0:T(8,128)(2,1)} %get-tuple-element.120), calls=%async_computation | async-start | bytes 393216 | tf_op jit(solution)/shard_map/uw/all_to_all | solution.py:1286
  20.4 2.7 %cr.1 = (bf16[8,72,768]{2,1,0:T(8,128)(2,1)}, s32[8,256]{1,0:T(8,128)}, bf16[8,72,768]{2,1,0:T(8,128)(2,1)}, f32[8,128]{1,0:T(8,128)}) custom-call(s32[4]{0:T(128)} %length_ref.31, s32[1,256]{1,0:T(1,128)} %bitcast.42, bf16[256,768]{1,0:T(8,128)(2,1)} %bitcast.34, bf16[24,768]{1,0:T(8,128)(2,1)} %bitcast.36, bf16[24,768]{1,0:T(8,128)(2,1)} %refs_8_.1, ...), custom_call_target="tpu_custom_call" | custom-call | flops 1 | bytes 1 | tf_op jit(solution)/shard_map/cr/pallas_call | solution.py:489
  31.7 4.2 %collective-permute-done.10.refs_2_ = bf16[8,24,512]{2,1,0:T(8,128)(2,1)S(1)} collective-permute-done((bf16[8,24,512]{2,1,0:T(8,128)(2,1)S(1)}, bf16[8,24,512]{2,1,0:T(8,128)(2,1)S(1)}, u32[]{:S(2)}, u32[]{:S(2)}) %collective-permute-start.10) | collective-permute-done | bytes 196640 | tf_op jit(solution)/shard_map/uw/ppermute | solution.py:1234
  44.8 5.3 %all-to-all-start.2 = ((bf16[8,72,768]{2,1,0:T(8,128)(2,1)}), bf16[8,72,768]{2,1,0:T(8,128)(2,1)S(1)}, u32[]{:S(2)}, u32[]{:S(2)}) async-start(bf16[8,72,768]{2,1,0:T(8,128)(2,1)} %get-tuple-element.134), calls=%async_computation.2 | async-start | bytes 1769472 | tf_op jit(solution)/shard_map/cr/all_to_all | solution.py:1286
  51.7 17.0 %att.1 = (bf16[8,64,384]{2,1,0:T(8,128)(2,1)}, f32[8,1,256]{2,1,0:T(1,128)}, f32[8,1,128]{2,1,0:T(1,128)}, bf16[8,256,768]{2,1,0:T(8,128)(2,1)}, bf16[2048,128]{...) custom-call(s32[4]{0:T(128)} %length_ref.31, ...), custom_call_target="tpu_custom_call" | custom-call | flops 1 | bytes 1 | tf_op jit(solution)/shard_map/att/pallas_call | solution.py:489
  70.0 6.6 %all-to-all-start.1 = ((bf16[8,64,384]{2,1,0:T(8,128)(2,1)}), bf16[8,64,384]{2,1,0:T(8,128)(2,1)}, u32[]{:S(2)}, u32[]{:S(2)}) async-start(bf16[8,64,384]{2,1,0:T(8,128)(2,1)} %get-tuple-element.132.refs_6_), calls=%async_computation.1 | async-start | bytes 786432 | tf_op jit(solution)/shard_map/att/all_to_all | solution.py:1286
  78.2 6.4 %collective-permute-done.13.refs_3_ = bf16[8,24,768]{2,1,0:T(8,128)(2,1)} collective-permute-done((bf16[8,24,768]{2,1,0:T(8,128)(2,1)S(1)}, bf16[8,24,768]{2,1,0:T(8,128)(2,1)}, u32[]{:S(2)}, u32[]{:S(2)}) %collective-permute-start.13) | collective-permute-done | bytes 294944 | tf_op jit(solution)/shard_map/ow/ppermute | solution.py:1234
  86.9 3.7 %hid.1 = (bf16[256,768]{1,0:T(8,128)(2,1)}, f32[256,768]{1,0:T(8,128)}, bf16[8,48,768]{2,1,0:T(8,128)(2,1)}, bf16[768,768]{1,0:T(8,128)(2,1)}, f32[8,128]{1,0:T(8,128)}) custom-call(s32[4]{0:T(128)} %length_ref.31, bf16[8,64,384]{2,1,0:T(8,128)(2,1)} %all-to-all-done.1.refs_0_, bf16[8,24,768]{2,1,0:T(8,128)(2,1)} %copy-done.10, ...), custom_call_target="tpu_custom_call" | custom-call | flops 1 | bytes 1 | tf_op jit(solution)/shard_map/hid/pallas_call | solution.py:489
  90.6 6.0 %all-to-all-start.3 = ((bf16[8,48,768]{2,1,0:T(8,128)(2,1)}), bf16[8,48,768]{2,1,0:T(8,128)(2,1)S(1)}, u32[]{:S(2)}, u32[]{:S(2)}) async-start(bf16[8,48,768]{2,1,0:T(8,128)(2,1)} %get-tuple-element.141), calls=%async_computation.3 | async-start | bytes 1179648 | tf_op jit(solution)/shard_map/mr/all_to_all | solution.py:1286
  99.3 13.4 %collective-permute-done.20.refs_2_ = bf16[8,48,768]{2,1,0:T(8,128)(2,1)} collective-permute-done((bf16[8,48,768]{2,1,0:T(8,128)(2,1)S(1)}, bf16[8,48,768]{2,1,0:T(8,128)(2,1)}, u32[]{:S(2)}, u32[]{:S(2)}) %collective-permute-start.20) | collective-permute-done | bytes 589856 | tf_op jit(solution)/shard_map/cp/ppermute | solution.py:1234
  112.7 6.0 %all-to-all-start.4 = ((bf16[8,72,768]{2,1,0:T(8,128)(2,1)}), bf16[8,72,768]{2,1,0:T(8,128)(2,1)S(1)}, u32[]{:S(2)}, u32[]{:S(2)}) async-start(bf16[8,72,768]{2,1,0:T(8,128)(2,1)} %get-tuple-element.147), calls=%async_computation.4 | async-start | bytes 1769472 | tf_op jit(solution)/shard_map/fw/all_to_all | solution.py:1286
  120.2 13.9 %eb.1 = (bf16[8,48,768]{2,1,0:T(8,128)(2,1)}, bf16[8,48,768]{2,1,0:T(8,128)(2,1)}, bf16[384,128]{1,0:T(8,128)(2,1)}, f32[8,128]{1,0:T(8,128)}) custom-call(s32[4]{0:T(128)} %length_ref.31, bf16[8,48,768]{2,1,0:T(8,128)(2,1)} %copy-done.2, bf16[8,48,768]{2,1,0:T(8,128)(2,1)} %copy-done.4, bf16[768,768]{1,0:T(8,128)(2,1)} %bitcast.20, ...), custom_call_target="tpu_custom_call" | custom-call | flops 1 | bytes 1 | tf_op jit(solution)/shard_map/eb/pallas_call | solution.py:489
  134.1 3.9 %all-to-all-done.4.refs_0_ = bf16[8,72,768]{2,1,0:T(8,128)(2,1)S(1)} async-done(((bf16[8,72,768]{2,1,0:T(8,128)(2,1)}), bf16[8,72,768]{2,1,0:T(8,128)(2,1)S(1)}, u32[]{:S(2)}, u32[]{:S(2)}) %all-to-all-start.4) | async-done | bytes 884768 | tf_op jit(solution)/shard_map/fw/all_to_all | solution.py:1286
  138.0 5.5 %all-to-all-start.5 = ((bf16[8,48,768]{2,1,0:T(8,128)(2,1)}), bf16[8,48,768]{2,1,0:T(8,128)(2,1)S(1)}, u32[]{:S(2)}, u32[]{:S(2)}) async-start(bf16[8,48,768]{2,1,0:T(8,128)(2,1)} %get-tuple-element.148), calls=%async_computation.5 | async-start | bytes 1179648 | tf_op jit(solution)/shard_map/eb/all_to_all | solution.py:1286
  145.9 9.3 %ewg.2 = (f32[768,768]{1,0:T(8,128)}, f32[768,768]{1,0:T(8,128)}, f32[8,128]{1,0:T(8,128)}) custom-call(s32[4]{0:T(128)} %length_ref.31, bf16[8,48,768]{2,1,0:T(8,128)(2,1)} %copy-done.2, bf16[8,48,768]{2,1,0:T(8,128)(2,1)} %collective-permute-done.22.refs_1_, bf16[8,48,768]{2,1,0:T(8,128)(2,1)} %copy-done.4, bf16[8,48,768]{2,1,0:T(8,128)(2,1)} %copy-done.19, ...), custom_call_target="tpu_custom_call" | custom-call | flops 1 | bytes 1 | tf_op jit(solution)/shard_map/ewg/pallas_call | solution.py:973
  155.2 2.9 %all-to-all-done.5.refs_0_ = bf16[8,48,768]{2,1,0:T(8,128)(2,1)S(1)} async-done(((bf16[8,48,768]{2,1,0:T(8,128)(2,1)}), bf16[8,48,768]{2,1,0:T(8,128)(2,1)S(1)}, u32[]{:S(2)}, u32[]{:S(2)}) %all-to-all-start.5) | async-done | bytes 589856 | tf_op jit(solution)/shard_map/eb/all_to_all | solution.py:1286
  159.0 4.0 %hg.1 = (f32[256,768]{1,0:T(8,128)}, bf16[256,768]{1,0:T(8,128)(2,1)}, f32[8,768]{1,0:T(8,128)}, bf16[8,64,384]{2,1,0:T(8,128)(2,1)}, f32[8,128]{1,0:T(8,128)}) custom-call(s32[4]{0:T(128)} %length_ref.31, bf16[8,48,768]{2,1,0:T(8,128)(2,1)} %copy-done.8, s32[8,256]{1,0:T(8,128)} %get-tuple-element.137.refs_7_.refs_1_, ...), custom_call_target="tpu_custom_call" | custom-call | flops 1 | bytes 1 | tf_op jit(solution)/shard_map/hg/pallas_call | solution.py:489
  162.9 5.0 %all-to-all-start.6 = ((bf16[8,64,384]{2,1,0:T(8,128)(2,1)}), bf16[8,64,384]{2,1,0:T(8,128)(2,1)S(1)}, u32[]{:S(2)}, u32[]{:S(2)}) async-start(bf16[8,64,384]{2,1,0:T(8,128)(2,1)} %get-tuple-element.155), calls=%async_computation.6 | async-start | bytes 786432 | tf_op jit(solution)/shard_map/hg/all_to_all | solution.py:1286
  167.9 3.6 %owg.1 = (bf16[192,896]{1,0:T(8,128)(2,1)}, bf16[192,896]{1,0:T(8,128)(2,1)}, bf16[192,896]{1,0:T(8,128)(2,1)}, bf16[192,896]{1,0:T(8,128)(2,1)}, f32[8,128]{1,0:T(8,128)}) custom-call(s32[4]{0:T(128)} %length_ref.31, bf16[256,768]{1,0:T(8,128)(2,1)} %get-tuple-element.156.refs_0_, bf16[256,768]{1,0:T(8,128)(2,1)} %get-tuple-element.157.refs_1_, ...), custom_call_target="tpu_custom_call" | custom-call | flops 1 | bytes 1 | tf_op jit(solution)/shard_map/owg/pallas_call | solution.py:489
  171.5 7.2 %all-to-all-done.6.refs_7_ = bf16[8,64,384]{2,1,0:T(8,128)(2,1)S(1)} async-done(((bf16[8,64,384]{2,1,0:T(8,128)(2,1)}), bf16[8,64,384]{2,1,0:T(8,128)(2,1)S(1)}, u32[]{:S(2)}, u32[]{:S(2)}) %all-to-all-start.6) | async-done | bytes 393248 | tf_op jit(solution)/shard_map/hg/all_to_all | solution.py:1286
  178.7 4.9 %all-to-all-start.7 = ((bf16[8,48,768]{2,1,0:T(8,128)(2,1)}), bf16[8,48,768]{2,1,0:T(8,128)(2,1)S(1)}, u32[]{:S(2)}, u32[]{:S(2)}) async-start(bf16[8,48,768]{2,1,0:T(8,128)(2,1)} %get-tuple-element.161), calls=%async_computation.7 | async-start | bytes 1179648 | tf_op jit(solution)/shard_map/rr/all_to_all | solution.py:1286
  188.8 16.5 %ag.1 = (bf16[8,352,256]{2,1,0:T(8,128)(2,1)}, f32[16,1,512]{2,1,0:T(1,128)}, f32[8,128]{1,0:T(8,128)}) custom-call(s32[4]{0:T(128)} %length_ref.31, bf16[2048,128]{1,0:T(8,128)(2,1)} %get-tuple-element.163.refs_0_, bf16[2048,128]{1,0:T(8,128)(2,1)} %get-tuple-element.164.refs_1_, bf16[128,2048]{1,0:T(8,128)(2,1)} %get-tuple-element.165.refs_2_, ...), custom_call_target="tpu_custom_call" | custom-call | flops 1 | bytes 1 | tf_op jit(solution)/shard_map/ag/pallas_call | solution.py:489
  206.9 6.2 %all-to-all-start.8 = ((bf16[8,352,256]{2,1,0:T(8,128)(2,1)}), bf16[8,352,256]{2,1,0:T(8,128)(2,1)S(1)}, u32[]{:S(2)}, u32[]{:S(2)}) async-start(bf16[8,352,256]{2,1,0:T(8,128)(2,1)} %get-tuple-element.194.refs_1_), calls=%async_computation.8 | async-start | bytes 2883584 | tf_op jit(solution)/shard_map/ag/all_to_all | solution.py:1286
  213.1 4.8 %wg.2 = (bf16[208,384]{1,0:T(8,128)(2,1)}, bf16[208,384]{1,0:T(8,128)(2,1)}, bf16[208,384]{1,0:T(8,128)(2,1)}, bf16[208,384]{1,0:T(8,128)(2,1)}, f32[8,128]{1,0:T(8,128)}) custom-call(s32[4]{0:T(128)} %length_ref.31, bf16[8,256,768]{2,1,0:T(8,128)(2,1)} %get-tuple-element.162.refs_0_, bf16[8,352,256]{2,1,0:T(8,128)(2,1)} %get-tuple-element.194.refs_1_, ...), custom_call_target="tpu_custom_call" | custom-call | flops 1 | bytes 1 | tf_op jit(solution)/shard_map/wg/pallas_call | solution.py:489
  219.7 4.6 %fw.1 = (bf16[768,2304]{1,0:T(8,128)(2,1)}, f32[8,128]{1,0:T(8,128)}) custom-call(s32[4]{0:T(128)} %length_ref.31, bf16[8,72,768]{2,1,0:T(8,128)(2,1)} %copy-done.5, bf16[8,72,768]{2,1,0:T(8,128)(2,1)} %copy-done.15, bf16[8,72,768]{2,1,0:T(8,128)(2,1)} %copy-done.14, bf16[8,72,768]{2,1,0:T(8,128)(2,1)} %copy-done.16, f32[8,128]{1,0:T(8,128)} %get-tuple-element.174.refs_3_.refs_4_), custom_call_target="tpu_custom_call" | custom-call | flops 1 | bytes 1 | tf_op jit(solution)/shard_map/fw/pallas_call | solution.py:489
  224.3 2.5 res.1
  228.2 2.8 %wg.3 = (bf16[24,1280]{1,0:T(8,128)(2,1)}, bf16[24,1280]{1,0:T(8,128)(2,1)}, bf16[24,1280]{1,0:T(8,128)(2,1)}, bf16[24,1280]{1,0:T(8,128)(2,1)}, bf16[24,1280]{1...) custom-call(s32[4]{0:T(128)} %length_ref.31, ...), custom_call_target="tpu_custom_call" | custom-call | flops 1 | bytes 1 | tf_op jit(solution)/shard_map/wg/pallas_call | solution.py:489
  240.3 2.8 %collective-permute-start.41 = (bf16[24,1280]{1,0:T(8,128)(2,1)}, bf16[24,1280]{1,0:T(8,128)(2,1)S(1)}, u32[]{:S(2)}, u32[]{:S(2)}) collective-permute-start(bf16[24,1280]{1,0:T(8,128)(2,1)} %get-tuple-element.193), channel_id=1, source_target_pairs={{0,7},{1,6},{2,5},{3,4},{4,3},{5,2},{6,1},{7,0},{8,15},{9,14},{10,... | collective-permute-start | bytes 184328 | tf_op jit(solution)/shard_map/wg/ppermute | solution.py:1234
  243.2 10.2 %ewg.3 = (f32[768,768]{1,0:T(8,128)}, f32[768,768]{1,0:T(8,128)}, f32[8,128]{1,0:T(8,128)}) custom-call(s32[4]{0:T(128)} %length_ref.31, bf16[8,48,768]{2,1,0:T(8,128)(2,1)} %collective-permute-done.23.refs_0_, bf16[8,48,768]{2,1,0:T(8,128)(2,1)} %collective-permute-done.24.refs_1_, bf16[8,48,768]{2,1,0:T(8,128)(2,1)} %collective-permute-done.20.refs_2_, ...), custom_call_target="tpu_custom_call" | custom-call | flops 1 | bytes 1 | tf_op jit(solution)/shard_map/ewg/pallas_call | solution.py:973
  253.5 2.5 collective-permute-done.40.refs_6_
  258.6 6.8 %fin.1 = (f32[24,768]{1,0:T(8,128)}, f32[24,768]{1,0:T(8,128)}, f32[24,768]{1,0:T(8,128)}, f32[1,24]{1,0:T(1,128)}, f32[1,12]{1,0:T(1,128)}, /*index=5*/f32[24,7...) custom-call(s32[4]{0:T(128)} %length_ref.31, ...), custom_call_target="tpu_custom_call" | custom-call | flops 1 | bytes 1 | tf_op jit(solution)/shard_map/fin/pallas_call | solution.py:489
  (170 shorter events, 62.4 us)
Async XLA Ops:
  0.6 11.1 %collective-permute-start = (bf16[256,768]{1,0:T(8,128)(2,1)}, bf16[256,768]{1,0:T(8,128)(2,1)S(1)}, u32[]{:S(2)}, u32[]{:S(2)}) collective-permute-start(bf16[256,768]{1,0:T(8,128)(2,1)} %bitcast.29), channel_id=1, source_target_pairs={{0,2},{2,4},{4,6},{6,7},{7,5},{5,3},{3,1},{1,0},{8,10},{10,12},{12... | collective-permute-start | bytes 1179656 | tf_op jit(solution)/shard_map/rin/ppermute | solution.py:1295
  2.7 34.0 %collective-permute-start.6 = (bf16[768,768]{1,0:T(8,128)(2,1)}, bf16[768,768]{1,0:T(8,128)(2,1)S(1)}, u32[]{:S(2)}, u32[]{:S(2)}) collective-permute-start(bf16[768,768]{1,0:T(8,128)(2,1)} %bitcast.19), channel_id=1, source_target_pairs={{0,16},{8,24},{16,0},{24,8},{1,17},{9,25},{17,1},{25,9},{2,18},{10... | collective-permute-start | bytes 3538952 | tf_op jit(solution)/shard_map/es/ppermute | solution.py:1234
  13.1 11.4 %collective-permute-start.2 = (bf16[256,768]{1,0:T(8,128)(2,1)S(1)}, bf16[256,768]{1,0:T(8,128)(2,1)S(1)}, u32[]{:S(2)}, u32[]{:S(2)}) collective-permute-start(bf16[256,768]{1,0:T(8,128)(2,1)S(1)} %collective-permute-done.refs_1_), channel_id=1, source_target_pairs={{0,2},{2,4},{4,6},{6,7},{7,5},{5,3},{3,1},{1,0},{8,10},{10,12},{12... | collective-permute-start | bytes 1179656 | tf_op jit(solution)/shard_map/rin/ppermute | solution.py:1295
  14.6 11.5 %collective-permute-start.3 = (bf16[256,768]{1,0:T(8,128)(2,1)S(1)}, bf16[256,768]{1,0:T(8,128)(2,1)S(1)}, u32[]{:S(2)}, u32[]{:S(2)}) collective-permute-start(bf16[256,768]{1,0:T(8,128)(2,1)S(1)} %collective-permute-done.1.refs_2_), channel_id=1, source_target_pairs={{2,0},{4,2},{6,4},{7,6},{5,7},{3,5},{1,3},{0,1},{10,8},{12,10},{14... | collective-permute-start | bytes 1179656 | tf_op jit(solution)/shard_map/rin/ppermute | solution.py:1296
  15.1 13.1 %all-to-all-start = ((bf16[8,24,512]{2,1,0:T(8,128)(2,1)}), bf16[8,24,512]{2,1,0:T(8,128)(2,1)S(1)}, u32[]{:S(2)}, u32[]{:S(2)}) async-start(bf16[8,24,512]{2,1,0:T(8,128)(2,1)} %get-tuple-element.120), calls=%async_computation | async-start | bytes 393216 | tf_op jit(solution)/shard_map/uw/all_to_all | solution.py:1286
  44.8 25.3 %all-to-all-start.2 = ((bf16[8,72,768]{2,1,0:T(8,128)(2,1)}), bf16[8,72,768]{2,1,0:T(8,128)(2,1)S(1)}, u32[]{:S(2)}, u32[]{:S(2)}) async-start(bf16[8,72,768]{2,1,0:T(8,128)(2,1)} %get-tuple-element.134), calls=%async_computation.2 | async-start | bytes 1769472 | tf_op jit(solution)/shard_map/cr/all_to_all | solution.py:1286
  50.1 35.0 %collective-permute-start.15 = (bf16[768,768]{1,0:T(8,128)(2,1)S(1)}, bf16[768,768]{1,0:T(8,128)(2,1)}, u32[]{:S(2)}, u32[]{:S(2)}) collective-permute-start(bf16[768,768]{1,0:T(8,128)(2,1)S(1)} %bitcast.27), channel_id=1, source_target_pairs={{0,16},{8,24},{16,0},{24,8},{1,17},{9,25},{17,1},{25,9},{2,18},{10... | collective-permute-start | bytes 3538952 | tf_op jit(solution)/shard_map/es/ppermute | solution.py:1234
  70.0 16.8 %all-to-all-start.1 = ((bf16[8,64,384]{2,1,0:T(8,128)(2,1)}), bf16[8,64,384]{2,1,0:T(8,128)(2,1)}, u32[]{:S(2)}, u32[]{:S(2)}) async-start(bf16[8,64,384]{2,1,0:T(8,128)(2,1)} %get-tuple-element.132.refs_6_), calls=%async_computation.1 | async-start | bytes 786432 | tf_op jit(solution)/shard_map/att/all_to_all | solution.py:1286
  84.6 14.7 %collective-permute-start.16 = (bf16[768,768]{1,0:T(8,128)(2,1)S(1)}, bf16[768,768]{1,0:T(8,128)(2,1)}, u32[]{:S(2)}, u32[]{:S(2)}) collective-permute-start(bf16[768,768]{1,0:T(8,128)(2,1)S(1)} %bitcast.23), channel_id=1, source_target_pairs={{0,8},{8,0},{16,24},{24,16},{1,9},{9,1},{17,25},{25,17},{2,10},{10... | collective-permute-start | bytes 3538952 | tf_op jit(solution)/shard_map/ec/ppermute | solution.py:1234
  85.1 14.2 %collective-permute-start.18 = (bf16[768,768]{1,0:T(8,128)(2,1)S(1)}, bf16[768,768]{1,0:T(8,128)(2,1)}, u32[]{:S(2)}, u32[]{:S(2)}) collective-permute-start(bf16[768,768]{1,0:T(8,128)(2,1)S(1)} %bitcast.28), channel_id=1, source_target_pairs={{0,8},{8,0},{16,24},{24,16},{1,9},{9,1},{17,25},{25,17},{2,10},{10... | collective-permute-start | bytes 3538952 | tf_op jit(solution)/shard_map/ec/ppermute | solution.py:1234
  85.1 14.2 %collective-permute-start.17 = (bf16[768,768]{1,0:T(8,128)(2,1)}, bf16[768,768]{1,0:T(8,128)(2,1)}, u32[]{:S(2)}, u32[]{:S(2)}) collective-permute-start(bf16[768,768]{1,0:T(8,128)(2,1)} %copy-done.11), channel_id=1, source_target_pairs={{0,8},{8,0},{16,24},{24,16},{1,9},{9,1},{17,25},{25,17},{2,10},{10... | collective-permute-start | bytes 3538952 | tf_op jit(solution)/shard_map/ec/ppermute | solution.py:1234
  86.4 12.9 %collective-permute-start.19 = (bf16[768,768]{1,0:T(8,128)(2,1)}, bf16[768,768]{1,0:T(8,128)(2,1)}, u32[]{:S(2)}, u32[]{:S(2)}) collective-permute-start(bf16[768,768]{1,0:T(8,128)(2,1)} %collective-permute-done.15.refs_7_), channel_id=1, source_target_pairs={{0,8},{8,0},{16,24},{24,16},{1,9},{9,1},{17,25},{25,17},{2,10},{10... | collective-permute-start | bytes 3538952 | tf_op jit(solution)/shard_map/ec/ppermute | solution.py:1234
  90.6 22.1 %all-to-all-start.3 = ((bf16[8,48,768]{2,1,0:T(8,128)(2,1)}), bf16[8,48,768]{2,1,0:T(8,128)(2,1)S(1)}, u32[]{:S(2)}, u32[]{:S(2)}) async-start(bf16[8,48,768]{2,1,0:T(8,128)(2,1)} %get-tuple-element.141), calls=%async_computation.3 | async-start | bytes 1179648 | tf_op jit(solution)/shard_map/mr/all_to_all | solution.py:1286
  97.7 15.0 %collective-permute-start.20 = (bf16[8,48,768]{2,1,0:T(8,128)(2,1)S(1)}, bf16[8,48,768]{2,1,0:T(8,128)(2,1)}, u32[]{:S(2)}, u32[]{:S(2)}) collective-permute-start(bf16[8,48,768]{2,1,0:T(8,128)(2,1)S(1)} %slice.17.refs_1_.refs_2_), channel_id=1, source_target_pairs={{0,16},{8,24},{16,0},{24,8},{1,17},{9,25},{17,1},{25,9},{2,18},{10... | collective-permute-start | bytes 1769480 | tf_op jit(solution)/shard_map/cp/ppermute | solution.py:1234
  112.7 25.3 %all-to-all-start.4 = ((bf16[8,72,768]{2,1,0:T(8,128)(2,1)}), bf16[8,72,768]{2,1,0:T(8,128)(2,1)S(1)}, u32[]{:S(2)}, u32[]{:S(2)}) async-start(bf16[8,72,768]{2,1,0:T(8,128)(2,1)} %get-tuple-element.147), calls=%async_computation.4 | async-start | bytes 1769472 | tf_op jit(solution)/shard_map/fw/all_to_all | solution.py:1286
  118.7 24.8 %collective-permute-start.21 = (bf16[8,48,768]{2,1,0:T(8,128)(2,1)S(1)}, bf16[8,48,768]{2,1,0:T(8,128)(2,1)S(1)}, u32[]{:S(2)}, u32[]{:S(2)}) collective-permute-start(bf16[8,48,768]{2,1,0:T(8,128)(2,1)S(1)} %slice.17.refs_1_.refs_2_), channel_id=1, source_target_pairs={{0,8},{8,0},{16,24},{24,16},{1,9},{9,1},{17,25},{25,17},{2,10},{10... | collective-permute-start | bytes 1769480 | tf_op jit(solution)/shard_map/cp/ppermute | solution.py:1234
  118.7 25.4 %collective-permute-start.23 = (bf16[8,48,768]{2,1,0:T(8,128)(2,1)S(1)}, bf16[8,48,768]{2,1,0:T(8,128)(2,1)}, u32[]{:S(2)}, u32[]{:S(2)}) collective-permute-start(bf16[8,48,768]{2,1,0:T(8,128)(2,1)S(1)} %all-to-all-done.3.refs_0_.refs_2_), channel_id=1, source_target_pairs={{0,16},{8,24},{16,0},{24,8},{1,17},{9,25},{17,1},{25,9},{2,18},{10... | collective-permute-start | bytes 1769480 | tf_op jit(solution)/shard_map/mf/ppermute | solution.py:1234
  138.0 20.1 %all-to-all-start.5 = ((bf16[8,48,768]{2,1,0:T(8,128)(2,1)}), bf16[8,48,768]{2,1,0:T(8,128)(2,1)S(1)}, u32[]{:S(2)}, u32[]{:S(2)}) async-start(bf16[8,48,768]{2,1,0:T(8,128)(2,1)} %get-tuple-element.148), calls=%async_computation.5 | async-start | bytes 1179648 | tf_op jit(solution)/shard_map/eb/all_to_all | solution.py:1286
  143.6 11.6 %collective-permute-start.25 = (bf16[8,48,768]{2,1,0:T(8,128)(2,1)}, bf16[8,48,768]{2,1,0:T(8,128)(2,1)S(1)}, u32[]{:S(2)}, u32[]{:S(2)}) collective-permute-start(bf16[8,48,768]{2,1,0:T(8,128)(2,1)} %collective-permute-done.20.refs_2_), channel_id=1, source_target_pairs={{0,8},{8,0},{16,24},{24,16},{1,9},{9,1},{17,25},{25,17},{2,10},{10... | collective-permute-start | bytes 1769480 | tf_op jit(solution)/shard_map/cp/ppermute | solution.py:1234
  144.1 11.2 %collective-permute-start.24 = (bf16[8,48,768]{2,1,0:T(8,128)(2,1)}, bf16[8,48,768]{2,1,0:T(8,128)(2,1)}, u32[]{:S(2)}, u32[]{:S(2)}) collective-permute-start(bf16[8,48,768]{2,1,0:T(8,128)(2,1)} %collective-permute-done.23.refs_0_), channel_id=1, source_target_pairs={{0,8},{8,0},{16,24},{24,16},{1,9},{9,1},{17,25},{25,17},{2,10},{10... | collective-permute-start | bytes 1769480 | tf_op jit(solution)/shard_map/mf/ppermute | solution.py:1234
  144.3 39.4 %collective-permute-start.27 = (bf16[8,72,768]{2,1,0:T(8,128)(2,1)S(1)}, bf16[8,72,768]{2,1,0:T(8,128)(2,1)S(1)}, u32[]{:S(2)}, u32[]{:S(2)}) collective-permute-start(bf16[8,72,768]{2,1,0:T(8,128)(2,1)S(1)} %all-to-all-done.4.refs_0_), channel_id=1, source_target_pairs={{0,16},{8,24},{16,0},{24,8},{1,17},{9,25},{17,1},{25,9},{2,18},{10... | collective-permute-start | bytes 2654216 | tf_op jit(solution)/shard_map/fw/ppermute | solution.py:1234
  162.9 15.8 %all-to-all-start.6 = ((bf16[8,64,384]{2,1,0:T(8,128)(2,1)}), bf16[8,64,384]{2,1,0:T(8,128)(2,1)S(1)}, u32[]{:S(2)}, u32[]{:S(2)}) async-start(bf16[8,64,384]{2,1,0:T(8,128)(2,1)} %get-tuple-element.155), calls=%async_computation.6 | async-start | bytes 786432 | tf_op jit(solution)/shard_map/hg/all_to_all | solution.py:1286
  178.7 27.4 %all-to-all-start.7 = ((bf16[8,48,768]{2,1,0:T(8,128)(2,1)}), bf16[8,48,768]{2,1,0:T(8,128)(2,1)S(1)}, u32[]{:S(2)}, u32[]{:S(2)}) async-start(bf16[8,48,768]{2,1,0:T(8,128)(2,1)} %get-tuple-element.161), calls=%async_computation.7 | async-start | bytes 1179648 | tf_op jit(solution)/shard_map/rr/all_to_all | solution.py:1286
  184.2 21.1 %collective-permute-start.32 = (bf16[192,896]{1,0:T(8,128)(2,1)}, bf16[192,896]{1,0:T(8,128)(2,1)S(1)}, u32[]{:S(2)}, u32[]{:S(2)}) collective-permute-start(bf16[192,896]{1,0:T(8,128)(2,1)} %get-tuple-element.181), channel_id=1, source_target_pairs={{0,8},{8,0},{16,24},{24,16},{1,9},{9,1},{17,25},{25,17},{2,10},{10... | collective-permute-start | bytes 1032200 | tf_op jit(solution)/shard_map/owg/ppermute | solution.py:1234
  184.3 21.0 %collective-permute-start.33 = (bf16[192,896]{1,0:T(8,128)(2,1)}, bf16[192,896]{1,0:T(8,128)(2,1)}, u32[]{:S(2)}, u32[]{:S(2)}) collective-permute-start(bf16[192,896]{1,0:T(8,128)(2,1)} %get-tuple-element.182), channel_id=1, source_target_pairs={{0,16},{8,24},{16,0},{24,8},{1,17},{9,25},{17,1},{25,9},{2,18},{10... | collective-permute-start | bytes 1032200 | tf_op jit(solution)/shard_map/owg/ppermute | solution.py:1234
  185.7 20.3 %collective-permute-start.34 = (bf16[192,896]{1,0:T(8,128)(2,1)}, bf16[192,896]{1,0:T(8,128)(2,1)}, u32[]{:S(2)}, u32[]{:S(2)}) collective-permute-start(bf16[192,896]{1,0:T(8,128)(2,1)} %get-tuple-element.183), channel_id=1, source_target_pairs={{0,24},{8,16},{16,8},{24,0},{1,25},{9,17},{17,9},{25,1},{2,26},{10... | collective-permute-start | bytes 1032200 | tf_op jit(solution)/shard_map/owg/ppermute | solution.py:1234
  206.9 50.6 %all-to-all-start.8 = ((bf16[8,352,256]{2,1,0:T(8,128)(2,1)}), bf16[8,352,256]{2,1,0:T(8,128)(2,1)S(1)}, u32[]{:S(2)}, u32[]{:S(2)}) async-start(bf16[8,352,256]{2,1,0:T(8,128)(2,1)} %get-tuple-element.194.refs_1_), calls=%async_computation.8 | async-start | bytes 2883584 | tf_op jit(solution)/shard_map/ag/all_to_all | solution.py:1286
  233.1 20.3 %collective-permute-start.37 = (bf16[24,1280]{1,0:T(8,128)(2,1)}, bf16[24,1280]{1,0:T(8,128)(2,1)S(1)}, u32[]{:S(2)}, u32[]{:S(2)}) collective-permute-start(bf16[24,1280]{1,0:T(8,128)(2,1)} %get-tuple-element.189), channel_id=1, source_target_pairs={{0,3},{1,2},{2,1},{3,0},{4,7},{5,6},{6,5},{7,4},{8,11},{9,10},{10,... | collective-permute-start | bytes 184328 | tf_op jit(solution)/shard_map/wg/ppermute | solution.py:1234
  234.6 18.8 %collective-permute-start.38 = (bf16[24,1280]{1,0:T(8,128)(2,1)}, bf16[24,1280]{1,0:T(8,128)(2,1)S(1)}, u32[]{:S(2)}, u32[]{:S(2)}) collective-permute-start(bf16[24,1280]{1,0:T(8,128)(2,1)} %get-tuple-element.190), channel_id=1, source_target_pairs={{0,4},{1,5},{2,6},{3,7},{4,0},{5,1},{6,2},{7,3},{8,12},{9,13},{10,... | collective-permute-start | bytes 184328 | tf_op jit(solution)/shard_map/wg/ppermute | solution.py:1234
  237.0 16.5 %collective-permute-start.39 = (bf16[24,1280]{1,0:T(8,128)(2,1)}, bf16[24,1280]{1,0:T(8,128)(2,1)S(1)}, u32[]{:S(2)}, u32[]{:S(2)}) collective-permute-start(bf16[24,1280]{1,0:T(8,128)(2,1)} %get-tuple-element.191), channel_id=1, source_target_pairs={{0,5},{1,4},{2,7},{3,6},{4,1},{5,0},{6,3},{7,2},{8,13},{9,12},{10,... | collective-permute-start | bytes 184328 | tf_op jit(solution)/shard_map/wg/ppermute | solution.py:1234
  238.4 17.5 %collective-permute-start.40 = (bf16[24,1280]{1,0:T(8,128)(2,1)}, bf16[24,1280]{1,0:T(8,128)(2,1)S(1)}, u32[]{:S(2)}, u32[]{:S(2)}) collective-permute-start(bf16[24,1280]{1,0:T(8,128)(2,1)} %get-tuple-element.192), channel_id=1, source_target_pairs={{0,6},{1,7},{2,4},{3,5},{4,2},{5,3},{6,0},{7,1},{8,14},{9,15},{10,... | collective-permute-start | bytes 184328 | tf_op jit(solution)/shard_map/wg/ppermute | solution.py:1234
  240.3 17.1 %collective-permute-start.41 = (bf16[24,1280]{1,0:T(8,128)(2,1)}, bf16[24,1280]{1,0:T(8,128)(2,1)S(1)}, u32[]{:S(2)}, u32[]{:S(2)}) collective-permute-start(bf16[24,1280]{1,0:T(8,128)(2,1)} %get-tuple-element.193), channel_id=1, source_target_pairs={{0,7},{1,6},{2,5},{3,4},{4,3},{5,2},{6,1},{7,0},{8,15},{9,14},{10,... | collective-permute-start | bytes 184328 | tf_op jit(solution)/shard_map/wg/ppermute | solution.py:1234
  (59 other events, 532.3 us)

commit v2 on v1

--- a/solution.py
+++ b/solution.py
@@ -720,16 +720,19 @@
     key_own, key_both, query_t, key_t, value_r, strips_in, heads, grads_in = refs[:8]
     logs_own, logs_both, stacked, table = refs[8:12]
     grads_own, grads_both, delta_own, delta_both, grad_k, grad_v, strips, bias, sems = refs[12:]
+    leave = copies_of([(strips.at[i], table.at[i]) for i in (1, 0)], sems.at[2:4])
     copies = copies_of([(strips_in.at[i], bias.at[i]) for i in (1, 0)], sems)
     for copy in copies:
         copy.start()
     own, both = split_units(stacked)
     common = (query_t, key_t, value_r, heads, grads_in)
-    shared_only = (logs_both, both, table.at[n : 2 * n], grads_both, delta_both)
-    own_only = (logs_own, own, table.at[0:n], grads_own, delta_own)
-    sums = (grad_k, grad_v, strips)
-    grads_of_unit(n, True, sc, copies[0], bias.at[1], key_both, *common, *shared_only, *sums)
-    grads_of_unit(n, False, sc, copies[1], bias.at[0], key_own, *common, *own_only, *sums)
+    shared_only = (logs_both, both, leave[0], grads_both, delta_both)
+    own_only = (logs_own, own, leave[1], grads_own, delta_own)
+    sums = (grad_k, grad_v)
+    grads_of_unit(n, True, sc, copies[0], bias.at[1], key_both, *common, *shared_only, *sums, strips.at[1])
+    grads_of_unit(n, False, sc, copies[1], bias.at[0], key_own, *common, *own_only, *sums, strips.at[0])
+    for copy in leave:
+        copy.wait()
 
 
 def grads_of_unit(
@@ -746,7 +749,7 @@
     grads_in,
     logs,
     stacked,
-    table,
+    leave,
     grad_t,
     delta,
     grad_k,
@@ -809,10 +812,14 @@
 
     for pair in range(n // 2):
         one_tile(pair, 0)
+    leave.start()
     for j in range(n):
         block = slice(QB * j, QB * (j + 1))
         stacked[j, 0:HEAD_DIM, :] = jnp.transpose(grad_k[block, :])[rows].astype(BF)
         stacked[j, HEAD_DIM : 2 * HEAD_DIM, :] = jnp.transpose(grad_v[block, :])[rows].astype(BF)
+
+
+def distance_sums(n, strips, table):
     row = iota((8, TILE), 0)
     empty = jnp.zeros((8, QB), F4)
     for far in range(n):
@@ -1069,9 +1076,11 @@
     out[...] = (hidden_grad[...] + normed).reshape(out.shape)
 
 
-def unit_weight_grads(n, heads, sc, normed, stacked, lines_ref, buckets, *rest):
+def unit_weight_grads(n, heads, sc, normed, stacked, strips, buckets, *rest):
     own, both = split_units(stacked)
-    outs, (buf, table) = rest[:heads], rest[heads:]
+    outs, (buf, table, lines_ref) = rest[:heads], rest[heads:]
+    for unit in range(2):
+        distance_sums(n, strips.at[unit], lines_ref.at[unit * n : (unit + 1) * n])
     width = buf.shape[1]
     sums = []
     for unit in range(2):
@@ -1410,7 +1419,7 @@
 
     with scope("mr"):
         moe_rows = all_to_all(moe_out)
-        moe_pair = swap(hold(moe_rows, all_cot[2], cot_pair), HEAD, 1)
+        moe_pair = swap(moe_rows, HEAD, 1)
     with scope("ec"):
         ins = (in_own, in_other, swap(in_own, HEAD, 1), swap(in_other, HEAD, 1))
         outs = (out_own, out_other, swap(out_own, HEAD, 1), swap(out_other, HEAD, 1))
@@ -1427,7 +1436,7 @@
         )
 
     with scope("fw"):
-        w_in = all_to_all(hold(w_stack, moe_rows, ins[2:], outs[2:], all_cot[2]))
+        w_in = all_to_all(hold(w_stack, moe_rows, ins[2:], outs[2:]))
     with scope("mf"):
         moe_far = swap(moe_rows, HEAD, 2)
         far_pair = swap(moe_far, HEAD, 1)
@@ -1496,7 +1505,7 @@
                 logs_own,
                 logs_both,
             ),
-            [shaped((n, 5 * HEAD_DIM + HEAD_DIM // 2, tok), BF), shaped((2 * n, 1, TILE), F4)],
+            [shaped((n, 5 * HEAD_DIM + HEAD_DIM // 2, tok), BF), shaped((2, n + 1, QB, QB), F4)],
             [
                 pltpu.VMEM((HEAD_DIM, total_rows), BF),
                 pltpu.VMEM((HEAD_DIM, total_rows // 2), BF),
@@ -1504,11 +1513,12 @@
                 pltpu.VMEM((n, 1, LANES), F4),
                 pltpu.VMEM((total_rows, LANES), F4),
                 pltpu.VMEM((total_rows, LANES), F4),
-                pltpu.VMEM((n + 1, QB, QB), F4),
                 pltpu.VMEM((2, n + 1, QB, QB), F4),
-                pltpu.SemaphoreType.DMA((2,)),
+                pltpu.VMEM((2, n + 1, QB, QB), F4),
+                pltpu.SemaphoreType.DMA((4,)),
             ],
             loose=(5,),
+            away=(1,),
             ties=(hold(out_token, w_parts),),
         )
         unit_in = all_to_all(hold(stacked, res_in, out_parts_in))
@@ -1518,7 +1528,11 @@
             functools.partial(unit_weight_grads, n, heads),
             (normed, stacked, lines, buckets),
             [shaped((width // heads + n + 8, 3 * LANES), BF)] * heads,
-            [pltpu.VMEM((width, 3 * LANES), F4), pltpu.VMEM((NUM_BUCKETS, 3 * LANES), F4)],
+            [
+                pltpu.VMEM((width, 3 * LANES), F4),
+                pltpu.VMEM((NUM_BUCKETS, 3 * LANES), F4),
+                pltpu.VMEM((2 * n, 1, TILE), F4),
+            ],
         )
         unit_parts_in = exchange(unit_grad_parts, HEAD)
     with scope("res"):

time: 270 us -> 268 us (level)
  Pallas kernels: 106 us -> 109 us
    ppermute x34, waiting for transfers between devices: 31.2 us -> 17.2 us  [swap(): return lax.ppermute(values, axis, [(i, i ^ flip) for i in range(size)])]
    all_to_all x9, waiting for transfers between devices: 17.9 us -> 30.8 us  [all_to_all(): return lax.all_to_all(stack, axis, split_axis=0, concat_axis=0, tiled=True)]
    ppermute x3, waiting for transfers between devices: 8.03 us -> 1.17 us  [hop(): front = lax.ppermute(front, BLK, ahead)]
    ppermute x3, waiting for transfers between devices: 2.99 us -> 8.97 us  [hop(): back = lax.ppermute(back, BLK, astern)]
    pallas_call x14, Pallas kernels: 86.9 us -> 89.7 us  [vmem_call(): pl.pallas_call(kernel, out_shape=tuple(outs) + (shaped((8, LANES), F4),),...]
    unnamed x80 -> x78, local copies, waits for them, and re-layouts: 8.16 us -> 5.7 us
  transfers between devices with their start and end apart: 51 -> 51, of which waited for: 23 -> 23; matrix products, arithmetic and copies ran while one was open for 0% -> 0% of each run, Pallas kernels for 37% -> 39%
where the time goes in v2:
time: 268 us; the launch traced here: 264 us
  Pallas kernels  109 us (41%)
  starting transfers between devices  85.7 us (32%)
  waiting for transfers between devices  60.5 us (23%)
  local copies, waits for them, and re-layouts  6.86 us (3%)
    pallas_call x14, Pallas kernels, vmem_call(): pl.pallas_call(kernel, out_shape=tuple(outs) + (shaped((8, LANES), F4),),...  89.7 us
    all_to_all x9, starting transfers between devices, all_to_all(): return lax.all_to_all(stack, axis, split_axis=0, concat_axis=0, tiled=True)  50.5 us
    all_to_all x9, waiting for transfers between devices, all_to_all(): return lax.all_to_all(stack, axis, split_axis=0, concat_axis=0, tiled=True)  30.8 us
    ppermute x34, starting transfers between devices, swap(): return lax.ppermute(values, axis, [(i, i ^ flip) for i in range(size)])  27 us
    pallas_call x2, Pallas kernels, expert_weights_call(): pl.pallas_call(kernel, grid=(steps,), out_shape=(shaped((depth, hidden),...  19.4 us
    ppermute x34, waiting for transfers between devices, swap(): return lax.ppermute(values, axis, [(i, i ^ flip) for i in range(size)])  17.2 us
    ppermute x3, waiting for transfers between devices, hop(): back = lax.ppermute(back, BLK, astern)  8.97 us
    ppermute x3, starting transfers between devices, hop(): front = lax.ppermute(front, BLK, ahead)  5.8 us
  transfers between devices with their start and end apart: 51, of which 23 were waited for; matrix products, arithmetic and copies ran while one was open for 0% of the time, Pallas kernels for 39%

profile of v2, /device:TPU:8, one launch (start us, length us, event | category | flops | bytes accessed | tf_op | source)
XLA Modules:
  0.0 263.6 jit_solution(278065138414812510)
XLA Ops:
  5.9 5.8 %collective-permute-done.1.refs_2_ = bf16[256,768]{1,0:T(8,128)(2,1)S(1)} collective-permute-done((bf16[256,768]{1,0:T(8,128)(2,1)}, bf16[256,768]{1,0:T(8,128)(2,1)S(1)}, u32[]{:S(2)}, u32[]{:S(2)}) %collective-permute-start.1) | collective-permute-done | bytes 393248 | tf_op jit(solution)/shard_map/rin/ppermute | solution.py:1305
  13.9 6.5 %all-to-all-start = ((bf16[8,24,512]{2,1,0:T(8,128)(2,1)}), bf16[8,24,512]{2,1,0:T(8,128)(2,1)S(1)}, u32[]{:S(2)}, u32[]{:S(2)}) async-start(bf16[8,24,512]{2,1,0:T(8,128)(2,1)} %get-tuple-element.119), calls=%async_computation | async-start | bytes 393216 | tf_op jit(solution)/shard_map/uw/all_to_all | solution.py:1295
  20.4 2.7 %cr.1 = (bf16[8,72,768]{2,1,0:T(8,128)(2,1)}, s32[8,256]{1,0:T(8,128)}, bf16[8,72,768]{2,1,0:T(8,128)(2,1)}, f32[8,128]{1,0:T(8,128)}) custom-call(s32[4]{0:T(128)} %length_ref.31, s32[1,256]{1,0:T(1,128)} %bitcast.42, bf16[256,768]{1,0:T(8,128)(2,1)} %bitcast.34, bf16[24,768]{1,0:T(8,128)(2,1)} %bitcast.36, bf16[24,768]{1,0:T(8,128)(2,1)} %refs_8_.1, ...), custom_call_target="tpu_custom_call" | custom-call | flops 1 | bytes 1 | tf_op jit(solution)/shard_map/cr/pallas_call | solution.py:489
  30.9 4.2 %collective-permute-done.10.refs_2_ = bf16[8,24,512]{2,1,0:T(8,128)(2,1)S(1)} collective-permute-done((bf16[8,24,512]{2,1,0:T(8,128)(2,1)S(1)}, bf16[8,24,512]{2,1,0:T(8,128)(2,1)S(1)}, u32[]{:S(2)}, u32[]{:S(2)}) %collective-permute-start.10) | collective-permute-done | bytes 196640 | tf_op jit(solution)/shard_map/uw/ppermute | solution.py:1243
  40.0 2.4 uw.3
  44.9 4.8 %all-to-all-start.2 = ((bf16[8,72,768]{2,1,0:T(8,128)(2,1)}), bf16[8,72,768]{2,1,0:T(8,128)(2,1)S(1)}, u32[]{:S(2)}, u32[]{:S(2)}) async-start(bf16[8,72,768]{2,1,0:T(8,128)(2,1)} %get-tuple-element.133), calls=%async_computation.2 | async-start | bytes 1769472 | tf_op jit(solution)/shard_map/cr/all_to_all | solution.py:1295
  51.3 17.0 %att.1 = (bf16[8,64,384]{2,1,0:T(8,128)(2,1)}, f32[8,1,256]{2,1,0:T(1,128)}, f32[8,1,128]{2,1,0:T(1,128)}, bf16[8,256,768]{2,1,0:T(8,128)(2,1)}, bf16[2048,128]{...) custom-call(s32[4]{0:T(128)} %length_ref.31, ...), custom_call_target="tpu_custom_call" | custom-call | flops 1 | bytes 1 | tf_op jit(solution)/shard_map/att/pallas_call | solution.py:489
  69.5 6.6 %all-to-all-start.1 = ((bf16[8,64,384]{2,1,0:T(8,128)(2,1)}), bf16[8,64,384]{2,1,0:T(8,128)(2,1)}, u32[]{:S(2)}, u32[]{:S(2)}) async-start(bf16[8,64,384]{2,1,0:T(8,128)(2,1)} %get-tuple-element.131.refs_6_), calls=%async_computation.1 | async-start | bytes 786432 | tf_op jit(solution)/shard_map/att/all_to_all | solution.py:1295
  77.7 6.4 %collective-permute-done.13.refs_3_ = bf16[8,24,768]{2,1,0:T(8,128)(2,1)} collective-permute-done((bf16[8,24,768]{2,1,0:T(8,128)(2,1)S(1)}, bf16[8,24,768]{2,1,0:T(8,128)(2,1)}, u32[]{:S(2)}, u32[]{:S(2)}) %collective-permute-start.13) | collective-permute-done | bytes 294944 | tf_op jit(solution)/shard_map/ow/ppermute | solution.py:1243
  86.3 3.7 %hid.1 = (bf16[256,768]{1,0:T(8,128)(2,1)}, f32[256,768]{1,0:T(8,128)}, bf16[8,48,768]{2,1,0:T(8,128)(2,1)}, bf16[768,768]{1,0:T(8,128)(2,1)}, f32[8,128]{1,0:T(8,128)}) custom-call(s32[4]{0:T(128)} %length_ref.31, bf16[8,64,384]{2,1,0:T(8,128)(2,1)} %all-to-all-done.1.refs_0_, bf16[8,24,768]{2,1,0:T(8,128)(2,1)} %copy-done.11, ...), custom_call_target="tpu_custom_call" | custom-call | flops 1 | bytes 1 | tf_op jit(solution)/shard_map/hid/pallas_call | solution.py:489
  90.1 6.0 %all-to-all-start.3 = ((bf16[8,48,768]{2,1,0:T(8,128)(2,1)}), bf16[8,48,768]{2,1,0:T(8,128)(2,1)S(1)}, u32[]{:S(2)}, u32[]{:S(2)}) async-start(bf16[8,48,768]{2,1,0:T(8,128)(2,1)} %get-tuple-element.140), calls=%async_computation.3 | async-start | bytes 1179648 | tf_op jit(solution)/shard_map/mr/all_to_all | solution.py:1295
  96.1 14.8 %all-to-all-done.3.refs_0_.refs_2_ = bf16[8,48,768]{2,1,0:T(8,128)(2,1)S(1)} async-done(((bf16[8,48,768]{2,1,0:T(8,128)(2,1)}), bf16[8,48,768]{2,1,0:T(8,128)(2,1)S(1)}, u32[]{:S(2)}, u32[]{:S(2)}) %all-to-all-start.3) | async-done | bytes 589856 | tf_op jit(solution)/shard_map/mr/all_to_all | solution.py:1295
  110.9 5.0 %all-to-all-start.4 = ((bf16[8,72,768]{2,1,0:T(8,128)(2,1)}), bf16[8,72,768]{2,1,0:T(8,128)(2,1)S(1)}, u32[]{:S(2)}, u32[]{:S(2)}) async-start(bf16[8,72,768]{2,1,0:T(8,128)(2,1)} %get-tuple-element.145), calls=%async_computation.4 | async-start | bytes 1769472 | tf_op jit(solution)/shard_map/fw/all_to_all | solution.py:1295
  119.1 13.9 %eb.1 = (bf16[8,48,768]{2,1,0:T(8,128)(2,1)}, bf16[8,48,768]{2,1,0:T(8,128)(2,1)}, bf16[384,128]{1,0:T(8,128)(2,1)}, f32[8,128]{1,0:T(8,128)}) custom-call(s32[4]{0:T(128)} %length_ref.31, bf16[8,48,768]{2,1,0:T(8,128)(2,1)} %copy-done.2, bf16[8,48,768]{2,1,0:T(8,128)(2,1)} %copy-done.5, bf16[768,768]{1,0:T(8,128)(2,1)} %bitcast.20, ...), custom_call_target="tpu_custom_call" | custom-call | flops 1 | bytes 1 | tf_op jit(solution)/shard_map/eb/pallas_call | solution.py:489
  133.1 3.3 %all-to-all-done.4.refs_0_ = bf16[8,72,768]{2,1,0:T(8,128)(2,1)S(1)} async-done(((bf16[8,72,768]{2,1,0:T(8,128)(2,1)}), bf16[8,72,768]{2,1,0:T(8,128)(2,1)S(1)}, u32[]{:S(2)}, u32[]{:S(2)}) %all-to-all-start.4) | async-done | bytes 884768 | tf_op jit(solution)/shard_map/fw/all_to_all | solution.py:1295
  136.4 5.7 %all-to-all-start.5 = ((bf16[8,48,768]{2,1,0:T(8,128)(2,1)}), bf16[8,48,768]{2,1,0:T(8,128)(2,1)S(1)}, u32[]{:S(2)}, u32[]{:S(2)}) async-start(bf16[8,48,768]{2,1,0:T(8,128)(2,1)} %get-tuple-element.146), calls=%async_computation.5 | async-start | bytes 1179648 | tf_op jit(solution)/shard_map/eb/all_to_all | solution.py:1295
  146.0 9.2 %ewg.2 = (f32[768,768]{1,0:T(8,128)}, f32[768,768]{1,0:T(8,128)}, f32[8,128]{1,0:T(8,128)}) custom-call(s32[4]{0:T(128)} %length_ref.31, bf16[8,48,768]{2,1,0:T(8,128)(2,1)} %copy-done.2, bf16[8,48,768]{2,1,0:T(8,128)(2,1)} %collective-permute-done.20.refs_1_, bf16[8,48,768]{2,1,0:T(8,128)(2,1)} %copy-done.5, ...), custom_call_target="tpu_custom_call" | custom-call | flops 1 | bytes 1 | tf_op jit(solution)/shard_map/ewg/pallas_call | solution.py:980
  157.6 3.9 %hg.1 = (f32[256,768]{1,0:T(8,128)}, bf16[256,768]{1,0:T(8,128)(2,1)}, f32[8,768]{1,0:T(8,128)}, bf16[8,64,384]{2,1,0:T(8,128)(2,1)}, f32[8,128]{1,0:T(8,128)}) custom-call(s32[4]{0:T(128)} %length_ref.31, bf16[8,48,768]{2,1,0:T(8,128)(2,1)} %copy-done.9, s32[8,256]{1,0:T(8,128)} %get-tuple-element.136.refs_7_.refs_1_, ...), custom_call_target="tpu_custom_call" | custom-call | flops 1 | bytes 1 | tf_op jit(solution)/shard_map/hg/pallas_call | solution.py:489
  161.6 5.0 %all-to-all-start.6 = ((bf16[8,64,384]{2,1,0:T(8,128)(2,1)}), bf16[8,64,384]{2,1,0:T(8,128)(2,1)S(1)}, u32[]{:S(2)}, u32[]{:S(2)}) async-start(bf16[8,64,384]{2,1,0:T(8,128)(2,1)} %get-tuple-element.153), calls=%async_computation.6 | async-start | bytes 786432 | tf_op jit(solution)/shard_map/hg/all_to_all | solution.py:1295
  166.6 3.5 %owg.1 = (bf16[192,896]{1,0:T(8,128)(2,1)}, bf16[192,896]{1,0:T(8,128)(2,1)}, bf16[192,896]{1,0:T(8,128)(2,1)}, bf16[192,896]{1,0:T(8,128)(2,1)}, f32[8,128]{1,0:T(8,128)}) custom-call(s32[4]{0:T(128)} %length_ref.31, bf16[256,768]{1,0:T(8,128)(2,1)} %get-tuple-element.154.refs_0_, bf16[256,768]{1,0:T(8,128)(2,1)} %get-tuple-element.155.refs_1_, ...), custom_call_target="tpu_custom_call" | custom-call | flops 1 | bytes 1 | tf_op jit(solution)/shard_map/owg/pallas_call | solution.py:489
  170.1 7.4 %all-to-all-done.6.refs_7_ = bf16[8,64,384]{2,1,0:T(8,128)(2,1)S(1)} async-done(((bf16[8,64,384]{2,1,0:T(8,128)(2,1)}), bf16[8,64,384]{2,1,0:T(8,128)(2,1)S(1)}, u32[]{:S(2)}, u32[]{:S(2)}) %all-to-all-start.6) | async-done | bytes 393248 | tf_op jit(solution)/shard_map/hg/all_to_all | solution.py:1295
  177.4 4.7 %all-to-all-start.7 = ((bf16[8,48,768]{2,1,0:T(8,128)(2,1)}), bf16[8,48,768]{2,1,0:T(8,128)(2,1)S(1)}, u32[]{:S(2)}, u32[]{:S(2)}) async-start(bf16[8,48,768]{2,1,0:T(8,128)(2,1)} %get-tuple-element.159), calls=%async_computation.7 | async-start | bytes 1179648 | tf_op jit(solution)/shard_map/rr/all_to_all | solution.py:1295
  186.7 16.3 %ag.1 = (bf16[8,352,256]{2,1,0:T(8,128)(2,1)}, f32[2,9,256,256]{3,2,1,0:T(8,128)}, f32[8,128]{1,0:T(8,128)}) custom-call(s32[4]{0:T(128)} %length_ref.31, bf16[2048,128]{1,0:T(8,128)(2,1)} %get-tuple-element.161.refs_0_, bf16[2048,128]{1,0:T(8,128)(2,1)} %get-tuple-element.162.refs_1_, bf16[128,2048]{1,0:T(8,128)(2,1)} %get-tuple-element.163.refs_2_, ...), custom_call_target="tpu_custom_call" | custom-call | flops 1 | bytes 1 | tf_op jit(solution)/shard_map/ag/pallas_call | solution.py:489
  204.7 6.2 %all-to-all-start.8 = ((bf16[8,352,256]{2,1,0:T(8,128)(2,1)}), bf16[8,352,256]{2,1,0:T(8,128)(2,1)S(1)}, u32[]{:S(2)}, u32[]{:S(2)}) async-start(bf16[8,352,256]{2,1,0:T(8,128)(2,1)} %get-tuple-element.192.refs_1_), calls=%async_computation.8 | async-start | bytes 2883584 | tf_op jit(solution)/shard_map/ag/all_to_all | solution.py:1295
  210.8 7.7 %wg.2 = (bf16[208,384]{1,0:T(8,128)(2,1)}, bf16[208,384]{1,0:T(8,128)(2,1)}, bf16[208,384]{1,0:T(8,128)(2,1)}, bf16[208,384]{1,0:T(8,128)(2,1)}, f32[8,128]{1,0:T(8,128)}) custom-call(s32[4]{0:T(128)} %length_ref.31, bf16[8,256,768]{2,1,0:T(8,128)(2,1)} %get-tuple-element.160.refs_0_, bf16[8,352,256]{2,1,0:T(8,128)(2,1)} %get-tuple-element.192.refs_1_, ...), custom_call_target="tpu_custom_call" | custom-call | flops 1 | bytes 1 | tf_op jit(solution)/shard_map/wg/pallas_call | solution.py:489
  220.4 4.6 %fw.1 = (bf16[768,2304]{1,0:T(8,128)(2,1)}, f32[8,128]{1,0:T(8,128)}) custom-call(s32[4]{0:T(128)} %length_ref.31, bf16[8,72,768]{2,1,0:T(8,128)(2,1)} %copy-done.6, bf16[8,72,768]{2,1,0:T(8,128)(2,1)} %copy-done.15, bf16[8,72,768]{2,1,0:T(8,128)(2,1)} %collective-permute-done.27.refs_2_, bf16[8,72,768]{2,1,0:T(8,128)(2,1)} %collective-permute-done.28.refs_3_, ...), custom_call_target="tpu_custom_call" | custom-call | flops 1 | bytes 1 | tf_op jit(solution)/shard_map/fw/pallas_call | solution.py:489
  225.0 2.5 res.1
  229.0 2.8 %wg.3 = (bf16[24,1280]{1,0:T(8,128)(2,1)}, bf16[24,1280]{1,0:T(8,128)(2,1)}, bf16[24,1280]{1,0:T(8,128)(2,1)}, bf16[24,1280]{1,0:T(8,128)(2,1)}, bf16[24,1280]{1...) custom-call(s32[4]{0:T(128)} %length_ref.31, ...), custom_call_target="tpu_custom_call" | custom-call | flops 1 | bytes 1 | tf_op jit(solution)/shard_map/wg/pallas_call | solution.py:489
  235.3 2.4 collective-permute-start.38
  239.2 4.0 %collective-permute-start.40 = (bf16[24,1280]{1,0:T(8,128)(2,1)}, bf16[24,1280]{1,0:T(8,128)(2,1)S(1)}, u32[]{:S(2)}, u32[]{:S(2)}) collective-permute-start(bf16[24,1280]{1,0:T(8,128)(2,1)} %get-tuple-element.190), channel_id=1, source_target_pairs={{0,6},{1,7},{2,4},{3,5},{4,2},{5,3},{6,0},{7,1},{8,14},{9,15},{10,... | collective-permute-start | bytes 184328 | tf_op jit(solution)/shard_map/wg/ppermute | solution.py:1243
  243.2 10.2 %ewg.3 = (f32[768,768]{1,0:T(8,128)}, f32[768,768]{1,0:T(8,128)}, f32[8,128]{1,0:T(8,128)}) custom-call(s32[4]{0:T(128)} %length_ref.31, bf16[8,48,768]{2,1,0:T(8,128)(2,1)} %collective-permute-done.22.refs_0_, bf16[8,48,768]{2,1,0:T(8,128)(2,1)} %copy-done.18, bf16[8,48,768]{2,1,0:T(8,128)(2,1)} %collective-permute-done.24.refs_2_, ...), custom_call_target="tpu_custom_call" | custom-call | flops 1 | bytes 1 | tf_op jit(solution)/shard_map/ewg/pallas_call | solution.py:980
  256.6 6.8 %fin.1 = (f32[24,768]{1,0:T(8,128)}, f32[24,768]{1,0:T(8,128)}, f32[24,768]{1,0:T(8,128)}, f32[1,24]{1,0:T(1,128)}, f32[1,12]{1,0:T(1,128)}, /*index=5*/f32[24,7...) custom-call(s32[4]{0:T(128)} %length_ref.31, ...), custom_call_target="tpu_custom_call" | custom-call | flops 1 | bytes 1 | tf_op jit(solution)/shard_map/fin/pallas_call | solution.py:489
  (168 shorter events, 56.1 us)
Async XLA Ops:
  0.6 11.1 %collective-permute-start.1 = (bf16[256,768]{1,0:T(8,128)(2,1)}, bf16[256,768]{1,0:T(8,128)(2,1)S(1)}, u32[]{:S(2)}, u32[]{:S(2)}) collective-permute-start(bf16[256,768]{1,0:T(8,128)(2,1)} %bitcast.29), channel_id=1, source_target_pairs={{2,0},{4,2},{6,4},{7,6},{5,7},{3,5},{1,3},{0,1},{10,8},{12,10},{14... | collective-permute-start | bytes 1179656 | tf_op jit(solution)/shard_map/rin/ppermute | solution.py:1305
  0.7 11.1 %collective-permute-start = (bf16[256,768]{1,0:T(8,128)(2,1)}, bf16[256,768]{1,0:T(8,128)(2,1)S(1)}, u32[]{:S(2)}, u32[]{:S(2)}) collective-permute-start(bf16[256,768]{1,0:T(8,128)(2,1)} %bitcast.30), channel_id=1, source_target_pairs={{0,2},{2,4},{4,6},{6,7},{7,5},{5,3},{3,1},{1,0},{8,10},{10,12},{12... | collective-permute-start | bytes 1179656 | tf_op jit(solution)/shard_map/rin/ppermute | solution.py:1304
  2.7 34.5 %collective-permute-start.6 = (bf16[768,768]{1,0:T(8,128)(2,1)}, bf16[768,768]{1,0:T(8,128)(2,1)S(1)}, u32[]{:S(2)}, u32[]{:S(2)}) collective-permute-start(bf16[768,768]{1,0:T(8,128)(2,1)} %bitcast.19), channel_id=1, source_target_pairs={{0,16},{8,24},{16,0},{24,8},{1,17},{9,25},{17,1},{25,9},{2,18},{10... | collective-permute-start | bytes 3538952 | tf_op jit(solution)/shard_map/es/ppermute | solution.py:1243
  11.8 11.7 %collective-permute-start.2 = (bf16[256,768]{1,0:T(8,128)(2,1)S(1)}, bf16[256,768]{1,0:T(8,128)(2,1)S(1)}, u32[]{:S(2)}, u32[]{:S(2)}) collective-permute-start(bf16[256,768]{1,0:T(8,128)(2,1)S(1)} %collective-permute-done.refs_1_), channel_id=1, source_target_pairs={{0,2},{2,4},{4,6},{6,7},{7,5},{5,3},{3,1},{1,0},{8,10},{10,12},{12... | collective-permute-start | bytes 1179656 | tf_op jit(solution)/shard_map/rin/ppermute | solution.py:1304
  13.5 11.7 %collective-permute-start.3 = (bf16[256,768]{1,0:T(8,128)(2,1)S(1)}, bf16[256,768]{1,0:T(8,128)(2,1)S(1)}, u32[]{:S(2)}, u32[]{:S(2)}) collective-permute-start(bf16[256,768]{1,0:T(8,128)(2,1)S(1)} %collective-permute-done.1.refs_2_), channel_id=1, source_target_pairs={{2,0},{4,2},{6,4},{7,6},{5,7},{3,5},{1,3},{0,1},{10,8},{12,10},{14... | collective-permute-start | bytes 1179656 | tf_op jit(solution)/shard_map/rin/ppermute | solution.py:1305
  13.9 13.4 %all-to-all-start = ((bf16[8,24,512]{2,1,0:T(8,128)(2,1)}), bf16[8,24,512]{2,1,0:T(8,128)(2,1)S(1)}, u32[]{:S(2)}, u32[]{:S(2)}) async-start(bf16[8,24,512]{2,1,0:T(8,128)(2,1)} %get-tuple-element.119), calls=%async_computation | async-start | bytes 393216 | tf_op jit(solution)/shard_map/uw/all_to_all | solution.py:1295
  44.9 24.6 %all-to-all-start.2 = ((bf16[8,72,768]{2,1,0:T(8,128)(2,1)}), bf16[8,72,768]{2,1,0:T(8,128)(2,1)S(1)}, u32[]{:S(2)}, u32[]{:S(2)}) async-start(bf16[8,72,768]{2,1,0:T(8,128)(2,1)} %get-tuple-element.133), calls=%async_computation.2 | async-start | bytes 1769472 | tf_op jit(solution)/shard_map/cr/all_to_all | solution.py:1295
  49.7 34.9 %collective-permute-start.15 = (bf16[768,768]{1,0:T(8,128)(2,1)S(1)}, bf16[768,768]{1,0:T(8,128)(2,1)}, u32[]{:S(2)}, u32[]{:S(2)}) collective-permute-start(bf16[768,768]{1,0:T(8,128)(2,1)S(1)} %bitcast.27), channel_id=1, source_target_pairs={{0,16},{8,24},{16,0},{24,8},{1,17},{9,25},{17,1},{25,9},{2,18},{10... | collective-permute-start | bytes 3538952 | tf_op jit(solution)/shard_map/es/ppermute | solution.py:1243
  69.5 16.8 %all-to-all-start.1 = ((bf16[8,64,384]{2,1,0:T(8,128)(2,1)}), bf16[8,64,384]{2,1,0:T(8,128)(2,1)}, u32[]{:S(2)}, u32[]{:S(2)}) async-start(bf16[8,64,384]{2,1,0:T(8,128)(2,1)} %get-tuple-element.131.refs_6_), calls=%async_computation.1 | async-start | bytes 786432 | tf_op jit(solution)/shard_map/att/all_to_all | solution.py:1295
  84.1 12.0 %collective-permute-start.16 = (bf16[768,768]{1,0:T(8,128)(2,1)S(1)}, bf16[768,768]{1,0:T(8,128)(2,1)}, u32[]{:S(2)}, u32[]{:S(2)}) collective-permute-start(bf16[768,768]{1,0:T(8,128)(2,1)S(1)} %bitcast.23), channel_id=1, source_target_pairs={{0,8},{8,0},{16,24},{24,16},{1,9},{9,1},{17,25},{25,17},{2,10},{10... | collective-permute-start | bytes 3538952 | tf_op jit(solution)/shard_map/ec/ppermute | solution.py:1243
  84.6 11.5 %collective-permute-start.18 = (bf16[768,768]{1,0:T(8,128)(2,1)S(1)}, bf16[768,768]{1,0:T(8,128)(2,1)}, u32[]{:S(2)}, u32[]{:S(2)}) collective-permute-start(bf16[768,768]{1,0:T(8,128)(2,1)S(1)} %bitcast.28), channel_id=1, source_target_pairs={{0,8},{8,0},{16,24},{24,16},{1,9},{9,1},{17,25},{25,17},{2,10},{10... | collective-permute-start | bytes 3538952 | tf_op jit(solution)/shard_map/ec/ppermute | solution.py:1243
  84.6 11.5 %collective-permute-start.17 = (bf16[768,768]{1,0:T(8,128)(2,1)}, bf16[768,768]{1,0:T(8,128)(2,1)}, u32[]{:S(2)}, u32[]{:S(2)}) collective-permute-start(bf16[768,768]{1,0:T(8,128)(2,1)} %copy-done.12), channel_id=1, source_target_pairs={{0,8},{8,0},{16,24},{24,16},{1,9},{9,1},{17,25},{25,17},{2,10},{10... | collective-permute-start | bytes 3538952 | tf_op jit(solution)/shard_map/ec/ppermute | solution.py:1243
  85.8 10.3 %collective-permute-start.19 = (bf16[768,768]{1,0:T(8,128)(2,1)}, bf16[768,768]{1,0:T(8,128)(2,1)}, u32[]{:S(2)}, u32[]{:S(2)}) collective-permute-start(bf16[768,768]{1,0:T(8,128)(2,1)} %collective-permute-done.15.refs_7_), channel_id=1, source_target_pairs={{0,8},{8,0},{16,24},{24,16},{1,9},{9,1},{17,25},{25,17},{2,10},{10... | collective-permute-start | bytes 3538952 | tf_op jit(solution)/shard_map/ec/ppermute | solution.py:1243
  90.1 20.8 %all-to-all-start.3 = ((bf16[8,48,768]{2,1,0:T(8,128)(2,1)}), bf16[8,48,768]{2,1,0:T(8,128)(2,1)S(1)}, u32[]{:S(2)}, u32[]{:S(2)}) async-start(bf16[8,48,768]{2,1,0:T(8,128)(2,1)} %get-tuple-element.140), calls=%async_computation.3 | async-start | bytes 1179648 | tf_op jit(solution)/shard_map/mr/all_to_all | solution.py:1295
  110.9 25.5 %all-to-all-start.4 = ((bf16[8,72,768]{2,1,0:T(8,128)(2,1)}), bf16[8,72,768]{2,1,0:T(8,128)(2,1)S(1)}, u32[]{:S(2)}, u32[]{:S(2)}) async-start(bf16[8,72,768]{2,1,0:T(8,128)(2,1)} %get-tuple-element.145), calls=%async_computation.4 | async-start | bytes 1769472 | tf_op jit(solution)/shard_map/fw/all_to_all | solution.py:1295
  117.0 25.7 %collective-permute-start.24 = (bf16[8,48,768]{2,1,0:T(8,128)(2,1)S(1)}, bf16[8,48,768]{2,1,0:T(8,128)(2,1)}, u32[]{:S(2)}, u32[]{:S(2)}) collective-permute-start(bf16[8,48,768]{2,1,0:T(8,128)(2,1)S(1)} %slice.17.refs_1_.refs_2_), channel_id=1, source_target_pairs={{0,16},{8,24},{16,0},{24,8},{1,17},{9,25},{17,1},{25,9},{2,18},{10... | collective-permute-start | bytes 1769480 | tf_op jit(solution)/shard_map/cp/ppermute | solution.py:1243
  118.6 25.9 %collective-permute-start.22 = (bf16[8,48,768]{2,1,0:T(8,128)(2,1)S(1)}, bf16[8,48,768]{2,1,0:T(8,128)(2,1)}, u32[]{:S(2)}, u32[]{:S(2)}) collective-permute-start(bf16[8,48,768]{2,1,0:T(8,128)(2,1)S(1)} %all-to-all-done.3.refs_0_.refs_2_), channel_id=1, source_target_pairs={{0,16},{8,24},{16,0},{24,8},{1,17},{9,25},{17,1},{25,9},{2,18},{10... | collective-permute-start | bytes 1769480 | tf_op jit(solution)/shard_map/mf/ppermute | solution.py:1243
  136.4 20.4 %all-to-all-start.5 = ((bf16[8,48,768]{2,1,0:T(8,128)(2,1)}), bf16[8,48,768]{2,1,0:T(8,128)(2,1)S(1)}, u32[]{:S(2)}, u32[]{:S(2)}) async-start(bf16[8,48,768]{2,1,0:T(8,128)(2,1)} %get-tuple-element.146), calls=%async_computation.5 | async-start | bytes 1179648 | tf_op jit(solution)/shard_map/eb/all_to_all | solution.py:1295
  142.7 12.5 %collective-permute-start.25 = (bf16[8,48,768]{2,1,0:T(8,128)(2,1)}, bf16[8,48,768]{2,1,0:T(8,128)(2,1)S(1)}, u32[]{:S(2)}, u32[]{:S(2)}) collective-permute-start(bf16[8,48,768]{2,1,0:T(8,128)(2,1)} %collective-permute-done.24.refs_2_), channel_id=1, source_target_pairs={{0,8},{8,0},{16,24},{24,16},{1,9},{9,1},{17,25},{25,17},{2,10},{10... | collective-permute-start | bytes 1769480 | tf_op jit(solution)/shard_map/cp/ppermute | solution.py:1243
  144.5 10.8 %collective-permute-start.23 = (bf16[8,48,768]{2,1,0:T(8,128)(2,1)}, bf16[8,48,768]{2,1,0:T(8,128)(2,1)S(1)}, u32[]{:S(2)}, u32[]{:S(2)}) collective-permute-start(bf16[8,48,768]{2,1,0:T(8,128)(2,1)} %collective-permute-done.22.refs_0_), channel_id=1, source_target_pairs={{0,8},{8,0},{16,24},{24,16},{1,9},{9,1},{17,25},{25,17},{2,10},{10... | collective-permute-start | bytes 1769480 | tf_op jit(solution)/shard_map/mf/ppermute | solution.py:1243
  144.5 37.7 %collective-permute-start.27 = (bf16[8,72,768]{2,1,0:T(8,128)(2,1)S(1)}, bf16[8,72,768]{2,1,0:T(8,128)(2,1)}, u32[]{:S(2)}, u32[]{:S(2)}) collective-permute-start(bf16[8,72,768]{2,1,0:T(8,128)(2,1)S(1)} %all-to-all-done.4.refs_0_), channel_id=1, source_target_pairs={{0,16},{8,24},{16,0},{24,8},{1,17},{9,25},{17,1},{25,9},{2,18},{10... | collective-permute-start | bytes 2654216 | tf_op jit(solution)/shard_map/fw/ppermute | solution.py:1243
  161.6 15.9 %all-to-all-start.6 = ((bf16[8,64,384]{2,1,0:T(8,128)(2,1)}), bf16[8,64,384]{2,1,0:T(8,128)(2,1)S(1)}, u32[]{:S(2)}, u32[]{:S(2)}) async-start(bf16[8,64,384]{2,1,0:T(8,128)(2,1)} %get-tuple-element.153), calls=%async_computation.6 | async-start | bytes 786432 | tf_op jit(solution)/shard_map/hg/all_to_all | solution.py:1295
  177.4 26.4 %all-to-all-start.7 = ((bf16[8,48,768]{2,1,0:T(8,128)(2,1)}), bf16[8,48,768]{2,1,0:T(8,128)(2,1)S(1)}, u32[]{:S(2)}, u32[]{:S(2)}) async-start(bf16[8,48,768]{2,1,0:T(8,128)(2,1)} %get-tuple-element.159), calls=%async_computation.7 | async-start | bytes 1179648 | tf_op jit(solution)/shard_map/rr/all_to_all | solution.py:1295
  182.7 20.4 %collective-permute-start.32 = (bf16[192,896]{1,0:T(8,128)(2,1)}, bf16[192,896]{1,0:T(8,128)(2,1)S(1)}, u32[]{:S(2)}, u32[]{:S(2)}) collective-permute-start(bf16[192,896]{1,0:T(8,128)(2,1)} %get-tuple-element.179), channel_id=1, source_target_pairs={{0,8},{8,0},{16,24},{24,16},{1,9},{9,1},{17,25},{25,17},{2,10},{10... | collective-permute-start | bytes 1032200 | tf_op jit(solution)/shard_map/owg/ppermute | solution.py:1243
  182.8 20.3 %collective-permute-start.33 = (bf16[192,896]{1,0:T(8,128)(2,1)}, bf16[192,896]{1,0:T(8,128)(2,1)}, u32[]{:S(2)}, u32[]{:S(2)}) collective-permute-start(bf16[192,896]{1,0:T(8,128)(2,1)} %get-tuple-element.180), channel_id=1, source_target_pairs={{0,16},{8,24},{16,0},{24,8},{1,17},{9,25},{17,1},{25,9},{2,18},{10... | collective-permute-start | bytes 1032200 | tf_op jit(solution)/shard_map/owg/ppermute | solution.py:1243
  184.1 19.7 %collective-permute-start.34 = (bf16[192,896]{1,0:T(8,128)(2,1)}, bf16[192,896]{1,0:T(8,128)(2,1)}, u32[]{:S(2)}, u32[]{:S(2)}) collective-permute-start(bf16[192,896]{1,0:T(8,128)(2,1)} %get-tuple-element.181), channel_id=1, source_target_pairs={{0,24},{8,16},{16,8},{24,0},{1,25},{9,17},{17,9},{25,1},{2,26},{10... | collective-permute-start | bytes 1032200 | tf_op jit(solution)/shard_map/owg/ppermute | solution.py:1243
  204.7 50.8 %all-to-all-start.8 = ((bf16[8,352,256]{2,1,0:T(8,128)(2,1)}), bf16[8,352,256]{2,1,0:T(8,128)(2,1)S(1)}, u32[]{:S(2)}, u32[]{:S(2)}) async-start(bf16[8,352,256]{2,1,0:T(8,128)(2,1)} %get-tuple-element.192.refs_1_), calls=%async_computation.8 | async-start | bytes 2883584 | tf_op jit(solution)/shard_map/ag/all_to_all | solution.py:1295
  233.9 19.5 %collective-permute-start.37 = (bf16[24,1280]{1,0:T(8,128)(2,1)}, bf16[24,1280]{1,0:T(8,128)(2,1)S(1)}, u32[]{:S(2)}, u32[]{:S(2)}) collective-permute-start(bf16[24,1280]{1,0:T(8,128)(2,1)} %get-tuple-element.187), channel_id=1, source_target_pairs={{0,3},{1,2},{2,1},{3,0},{4,7},{5,6},{6,5},{7,4},{8,11},{9,10},{10,... | collective-permute-start | bytes 184328 | tf_op jit(solution)/shard_map/wg/ppermute | solution.py:1243
  235.3 18.1 %collective-permute-start.38 = (bf16[24,1280]{1,0:T(8,128)(2,1)}, bf16[24,1280]{1,0:T(8,128)(2,1)S(1)}, u32[]{:S(2)}, u32[]{:S(2)}) collective-permute-start(bf16[24,1280]{1,0:T(8,128)(2,1)} %get-tuple-element.188), channel_id=1, source_target_pairs={{0,4},{1,5},{2,6},{3,7},{4,0},{5,1},{6,2},{7,3},{8,12},{9,13},{10,... | collective-permute-start | bytes 184328 | tf_op jit(solution)/shard_map/wg/ppermute | solution.py:1243
  237.7 15.8 %collective-permute-start.39 = (bf16[24,1280]{1,0:T(8,128)(2,1)}, bf16[24,1280]{1,0:T(8,128)(2,1)S(1)}, u32[]{:S(2)}, u32[]{:S(2)}) collective-permute-start(bf16[24,1280]{1,0:T(8,128)(2,1)} %get-tuple-element.189), channel_id=1, source_target_pairs={{0,5},{1,4},{2,7},{3,6},{4,1},{5,0},{6,3},{7,2},{8,13},{9,12},{10,... | collective-permute-start | bytes 184328 | tf_op jit(solution)/shard_map/wg/ppermute | solution.py:1243
  239.2 14.6 %collective-permute-start.40 = (bf16[24,1280]{1,0:T(8,128)(2,1)}, bf16[24,1280]{1,0:T(8,128)(2,1)S(1)}, u32[]{:S(2)}, u32[]{:S(2)}) collective-permute-start(bf16[24,1280]{1,0:T(8,128)(2,1)} %get-tuple-element.190), channel_id=1, source_target_pairs={{0,6},{1,7},{2,4},{3,5},{4,2},{5,3},{6,0},{7,1},{8,14},{9,15},{10,... | collective-permute-start | bytes 184328 | tf_op jit(solution)/shard_map/wg/ppermute | solution.py:1243
  243.2 12.3 %collective-permute-start.41 = (bf16[24,1280]{1,0:T(8,128)(2,1)}, bf16[24,1280]{1,0:T(8,128)(2,1)S(1)}, u32[]{:S(2)}, u32[]{:S(2)}) collective-permute-start(bf16[24,1280]{1,0:T(8,128)(2,1)} %get-tuple-element.191), channel_id=1, source_target_pairs={{0,7},{1,6},{2,5},{3,4},{4,3},{5,2},{6,1},{7,0},{8,15},{9,14},{10,... | collective-permute-start | bytes 184328 | tf_op jit(solution)/shard_map/wg/ppermute | solution.py:1243
  (58 other events, 532.1 us)
